TPU v7x, 32 devices: a whole 2x2x4 slice. The times are simulated.
32 devices in a mesh: dp: 8 (over y, x, core), expert: 4 (over z).
Axes of the slice: x: 2, y: 2, z: 4, core: 2. Of those that a mesh axis runs over, the one named last changes fastest.
Arguments:
- tokens: bfloat16 [24576, 1152], P(('dp', 'expert')), may hold values from -6 to 6
- cotangent: bfloat16 [24576, 1152], P(('dp', 'expert')), may hold values from -6 to 6
- routes: int32 [24576, 1], P(('dp', 'expert')), may hold values from 0 to 3; in each aligned block of 768 rows (0 to 767, 768 to 1535, ...) at most 480 rows name the same one
- starts: int32 [24576], P(('dp', 'expert')), may hold values from 0 to 1, as said below
- input_proj: bfloat16 [1152, 4608], P(None, 'dp'), may hold values from -0.1875 to 0.1875
- conv_kernel: bfloat16 [4, 2304], P(None, 'dp'), may hold values from -3 to 3
- conv_bias: bfloat16 [2304], P('dp'), may hold values from -3 to 3
- select_proj: bfloat16 [2304, 104], P('dp'), may hold values from -0.125 to 0.125
- step_proj: bfloat16 [72, 2304], P(None, 'dp'), may hold values from -0.75 to 0.75
- step_bias: bfloat16 [2304], P('dp'), may hold values from -9 to -2.5
- decay_log: bfloat16 [2304, 16], P('dp'), may hold values from -1.1953125 to 2.796875
- skip_gain: bfloat16 [2304], P('dp'), may hold values from 0.5 to 1.5
- output_proj: bfloat16 [2304, 1152], P('dp'), may hold values from -0.375 to 0.375
- norm_gain: bfloat16 [1152], P('dp'), may hold values from 0.5 to 1.5
- ffn_gain: bfloat16 [1152], P('dp'), may hold values from 0.5 to 1.5
- router: bfloat16 [1152, 4], P('dp'), may hold values from -0.19921875 to 0.19921875
- expert_up: bfloat16 [4, 1152, 3072], P('expert', None, 'dp'), may hold values from -0.1875 to 0.1875
- expert_down: bfloat16 [4, 3072, 1152], P('expert', 'dp'), may hold values from -0.875 to 0.875
Outputs:
- output: bfloat16 [24576, 1152], P(('dp', 'expert'))
- grad_tokens: bfloat16 [24576, 1152], P(('dp', 'expert'))
- grad_input_proj: float32 [1152, 4608], P(None, 'dp')
- grad_conv_kernel: float32 [4, 2304], P(None, 'dp')
- grad_conv_bias: float32 [2304], P('dp')
- grad_select_proj: float32 [2304, 104], P('dp')
- grad_step_proj: float32 [72, 2304], P(None, 'dp')
- grad_step_bias: float32 [2304], P('dp')
- grad_decay_log: float32 [2304, 16], P('dp')
- grad_skip_gain: float32 [2304], P('dp')
- grad_output_proj: float32 [2304, 1152], P('dp')
- grad_norm_gain: float32 [1152], P('dp')
- grad_ffn_gain: float32 [1152], P('dp')
- grad_router: float32 [1152, 4], P('dp')
- grad_expert_up: float32 [4, 1152, 3072], P('expert', None, 'dp')
- grad_expert_down: float32 [4, 3072, 1152], P('expert', 'dp')
Inputs may be any that keep to these rules, and one draw needn't show every extreme that they name: `routes`: in the 768 rows of one device no expert is named more than 480 times, and in every draw some device names some expert exactly 480 times, more than its 384 slots. The first token of every aligned run of 3072 tokens has starts = 1. In each such run one sequence begins within its first 384 tokens and ends within its last 384 tokens; the others are short.
All inputs are finite; a program needn't handle non-finite values.
Results may differ from a plain program's by a relative error of at most 0.02.
Values may be sent and summed in bfloat16 or wider, within the bound.
A program may use at most 320 MiB of HBM per device.

v0:
```python
from functools import partial

import jax
import jax.numpy as jnp
from jax import lax
from jax.sharding import PartitionSpec as P

BLK = 32


epsilon = 1e-05


def shifted(array, axis, by):
    length = lax.axis_size(axis)
    pairs = [(i, i + by) for i in range(length) if 0 <= i + by < length]
    return lax.ppermute(array, axis, pairs)


def entering(array, axis, combine, identity, reverse):
    length, here = (lax.axis_size(axis), lax.axis_index(axis))
    everything = jax.tree.map(
        lambda part, kind: lax.all_gather(part.astype(kind), axis),
        array,
        (jnp.bfloat16, jnp.bfloat16),
    )
    start = jax.tree.map(
        lambda part, zero: jnp.broadcast_to(jnp.asarray(zero, part.dtype), part.shape),
        array,
        identity,
    )

    def step(k, before):
        at = length - 1 - k if reverse else k
        reached = at > here if reverse else at < here
        new = combine(
            before, jax.tree.map(lambda part, own: part[at].astype(own.dtype), everything, array)
        )
        return jax.tree.map(lambda a, b: jnp.where(reached, a, b), new, before)

    return lax.fori_loop(0, length, step, start)


def rms_norm(values, gain):
    return values * lax.rsqrt(jnp.mean(values * values, axis=-1, keepdims=True) + epsilon) * gain


def gate_probs(normed, weights, chosen):
    logits = jnp.dot(
        normed, weights, precision=lax.Precision.HIGHEST, preferred_element_type=jnp.float32
    )
    probs = jax.nn.softmax(logits, axis=-1)
    return jnp.sum(probs * chosen, axis=-1)


def scan_block(rate, state, block):
    delta, values, b_coeff, c_coeff, keep = block
    outputs = []
    for step in range(delta.shape[0]):
        decay = jnp.exp(rate * delta[step][None, :]) * keep[step]
        state = decay * state + b_coeff[step][:, None] * (delta[step] * values[step])[None, :]
        outputs.append(jnp.sum(state * c_coeff[step][:, None], axis=0))
    return (state, jnp.stack(outputs))


def run_scan(rate, state, delta, values, b_coeff, c_coeff, keep, width):
    count = delta.shape[0] // width
    blocks = (
        delta.reshape(count, width, -1),
        values.reshape(count, width, -1),
        b_coeff.reshape(count, width, -1),
        c_coeff.reshape(count, width, -1),
        keep.reshape(count, width),
    )
    state, outputs = lax.scan(jax.checkpoint(partial(scan_block, rate)), state, blocks)
    return (state, outputs.reshape(delta.shape))


def end_terms(rate, total, carried, block):
    running, gathered_sum = carried
    delta_part, drive_part, b_part, after_part = block
    summed = running[None, :] + jnp.cumsum(delta_part, axis=0)
    weight = (
        jnp.exp(rate[None, :, :] * (total[None, :] - summed)[:, None, :])
        * after_part[:, None, None]
    )
    gathered_sum = gathered_sum + jnp.sum(
        weight * drive_part[:, None, :] * b_part[:, :, None], axis=0
    )
    return ((summed[-1], gathered_sum), None)


def start_terms(rate, carried, block):
    running, gathered_sum = carried
    delta_part, grad_part, c_part, before_part = block
    summed = running[None, :] + jnp.cumsum(delta_part, axis=0)
    weight = jnp.exp(rate[None, :, :] * summed[:, None, :]) * before_part[:, None, None]
    gathered_sum = gathered_sum + jnp.sum(
        weight * c_part[:, :, None] * grad_part[:, None, :], axis=0
    )
    return ((summed[-1], gathered_sum), None)


def combine(earlier, later):
    return (earlier[0] * later[0], later[0] * earlier[1] + later[1])


def product(left, right):
    return jnp.dot(left, right, preferred_element_type=jnp.float32)


def product_back(left, right):
    return lax.dot_general(
        left, right, (((1,), (1,)), ((), ())), preferred_element_type=jnp.float32
    )


def contract(left, right):
    return lax.dot_general(
        left, right, (((0,), (0,)), ((), ())), preferred_element_type=jnp.float32
    )


def silu_slope(values):
    sigma = jax.nn.sigmoid(values)
    return sigma * (1.0 + values * (1.0 - sigma))


def body(
    tokens,
    cotangent,
    routes,
    starts,
    input_proj,
    conv_kernel,
    conv_bias,
    select_proj,
    step_proj,
    step_bias,
    decay_log,
    skip_gain,
    output_proj,
    norm_gain,
    ffn_gain,
    router,
    expert_up,
    expert_down,
):
    gathered = (
        lax.all_gather(input_proj, "dp", axis=1, tiled=True),
        lax.all_gather(conv_kernel, "dp", axis=1, tiled=True),
        lax.all_gather(conv_bias, "dp", axis=0, tiled=True),
        lax.all_gather(select_proj, "dp", axis=0, tiled=True),
        lax.all_gather(step_proj, "dp", axis=1, tiled=True),
        lax.all_gather(step_bias, "dp", axis=0, tiled=True),
        lax.all_gather(decay_log, "dp", axis=0, tiled=True),
        lax.all_gather(skip_gain, "dp", axis=0, tiled=True),
        lax.all_gather(output_proj, "dp", axis=0, tiled=True),
        lax.all_gather(norm_gain, "dp", axis=0, tiled=True),
        lax.all_gather(ffn_gain, "dp", axis=0, tiled=True),
        lax.all_gather(router, "dp", axis=0, tiled=True),
        lax.all_gather(expert_up, "dp", axis=2, tiled=True),
        lax.all_gather(expert_down, "dp", axis=1, tiled=True),
    )
    (
        w_input,
        w_conv,
        b_conv,
        w_select,
        w_step,
        b_step,
        w_decay,
        w_skip,
        w_output,
        g_norm,
        g_ffn,
        w_router,
        w_up,
        w_down,
    ) = gathered
    rows = tokens.shape[0]
    groups = lax.axis_size("expert")
    width = w_input.shape[1] // 2
    rank = w_step.shape[0]
    states = w_decay.shape[1]
    taps = w_conv.shape[0]
    model = tokens.shape[1]
    capacity = 2 * rows // groups
    conv_f = w_conv.astype(jnp.float32)
    skip_f = w_skip.astype(jnp.float32)
    norm_f = g_norm.astype(jnp.float32)
    ffn_f = g_ffn.astype(jnp.float32)
    router_f = w_router.astype(jnp.float32)
    hidden_in = tokens.astype(jnp.float32)
    norm_low = rms_norm(hidden_in, norm_f).astype(jnp.bfloat16)
    mixed_in = product(norm_low, w_input).astype(jnp.bfloat16)
    conv_in = mixed_in[:, :width]
    gate_in = mixed_in[:, width:].astype(jnp.float32)
    flags = starts.astype(jnp.float32)
    counts = jnp.cumsum(starts)
    edge_keep = (counts[rows - taps + 1 :] == counts[rows - 1]).astype(jnp.float32)
    tail = (conv_in[rows - taps + 1 :].astype(jnp.float32) * edge_keep[:, None]).astype(
        jnp.bfloat16
    )
    before_rows = shifted(tail, "expert", 1)
    extended = jnp.concatenate([before_rows, conv_in], 0).astype(jnp.float32)
    conv_sum = jnp.broadcast_to(b_conv.astype(jnp.float32), (rows, width))
    valid_list = []
    for lag in range(taps):
        if lag == 0:
            valid = jnp.ones((rows,), jnp.float32)
        else:
            earlier = jnp.concatenate([jnp.zeros((lag,), jnp.int32), counts[: rows - lag]], 0)
            valid = (counts == earlier).astype(jnp.float32)
        valid_list.append(valid)
        conv_sum = (
            conv_sum
            + valid[:, None]
            * conv_f[taps - 1 - lag]
            * extended[taps - 1 - lag : taps - 1 - lag + rows]
        )
    inner_low = jax.nn.silu(conv_sum).astype(jnp.bfloat16)
    inner_val = inner_low.astype(jnp.float32)
    selected = product(inner_low, w_select)
    step_low = selected[:, :rank].astype(jnp.bfloat16)
    b_coeff = selected[:, rank : rank + states]
    c_coeff = selected[:, rank + states :]
    step_pre = product(step_low, w_step) + b_step.astype(jnp.float32)
    delta = jax.nn.softplus(step_pre)
    rate = -jnp.exp(w_decay.astype(jnp.float32)).T
    keep = 1.0 - flags
    total = jnp.sum(delta, axis=0)
    last_count = counts[rows - 1]
    after_mask = (counts == last_count).astype(jnp.float32)
    before_mask = (counts == 0).astype(jnp.float32)
    drive = delta * inner_val
    block_count = rows // BLK
    delta_blocks = delta.reshape(block_count, BLK, width)
    zero_run = jnp.zeros((width,), jnp.float32)
    zero_state = jnp.zeros((states, width), jnp.float32)
    (_, local_end), _ = lax.scan(
        partial(end_terms, rate, total),
        (zero_run, zero_state),
        (
            delta_blocks,
            drive.reshape(block_count, BLK, width),
            b_coeff.reshape(block_count, BLK, states),
            after_mask.reshape(block_count, BLK),
        ),
    )
    through = jnp.exp(rate * total[None, :]) * (last_count == 0).astype(jnp.float32)
    identity = (jnp.ones_like(through), jnp.zeros_like(local_end))
    _, start_state = entering((through, local_end), "expert", combine, identity, False)

    def scan_part(delta_in, values_in, b_in, c_in, rate_in, state_in):
        return run_scan(rate_in, state_in, delta_in, values_in, b_in, c_in, keep, BLK)

    (_, scan_out), scan_back = jax.vjp(
        scan_part, delta, inner_val, b_coeff, c_coeff, rate, start_state
    )
    gate_act = jax.nn.silu(gate_in)
    scanned = scan_out + skip_f * inner_val
    gated_low = (scanned * gate_act).astype(jnp.bfloat16)
    hidden_one = hidden_in + product(gated_low, w_output)
    norm_two = rms_norm(hidden_one, ffn_f)
    route = routes[:, 0]
    chosen_int = (route[:, None] == jnp.arange(groups, dtype=jnp.int32)[None, :]).astype(jnp.int32)
    ranks = jnp.cumsum(chosen_int, axis=0) - chosen_int
    slot = jnp.sum(ranks * chosen_int, axis=1)
    target = jnp.where(slot < capacity, route * capacity + slot, groups * capacity)
    chosen = chosen_int.astype(jnp.float32)
    sending = (
        jnp.zeros((groups * capacity + 1, model), jnp.bfloat16)
        .at[target]
        .set(norm_two.astype(jnp.bfloat16))
    )
    arrived = lax.all_to_all(
        sending[:-1].reshape(groups, capacity, model),
        "expert",
        split_axis=0,
        concat_axis=0,
        tiled=True,
    )
    arrived_rows = arrived.reshape(groups * capacity, model)
    up_pre = product(arrived_rows, w_up[0])
    up_low = jax.nn.gelu(up_pre).astype(jnp.bfloat16)
    expert_out = product(up_low, w_down[0]).astype(jnp.bfloat16).reshape(groups, capacity, model)
    returned = lax.all_to_all(expert_out, "expert", split_axis=0, concat_axis=0, tiled=True)
    padded = jnp.concatenate(
        [returned.reshape(groups * capacity, model), jnp.zeros((1, model), jnp.bfloat16)], 0
    )
    picked = padded[target].astype(jnp.float32)

    def routing(normed, weights):
        return gate_probs(normed, weights, chosen)

    gate_value, gate_back = jax.vjp(routing, norm_two, router_f)
    output = (hidden_one + gate_value[:, None] * picked).astype(jnp.bfloat16)
    grad_out = cotangent.astype(jnp.float32)
    grad_gate = jnp.sum(grad_out * picked, axis=1)
    grad_picked = (gate_value[:, None] * grad_out).astype(jnp.bfloat16)
    send_back = jnp.zeros((groups * capacity + 1, model), jnp.bfloat16).at[target].set(grad_picked)
    grad_arrived = lax.all_to_all(
        send_back[:-1].reshape(groups, capacity, model),
        "expert",
        split_axis=0,
        concat_axis=0,
        tiled=True,
    ).reshape(groups * capacity, model)
    grad_down = contract(up_low, grad_arrived)
    grad_act = product_back(grad_arrived, w_down[0])
    _, gelu_back = jax.vjp(jax.nn.gelu, up_pre)
    grad_pre = gelu_back(grad_act)[0].astype(jnp.bfloat16)
    grad_up = contract(arrived_rows, grad_pre)
    grad_rows = (
        product_back(grad_pre, w_up[0]).astype(jnp.bfloat16).reshape(groups, capacity, model)
    )
    grad_sent = lax.all_to_all(grad_rows, "expert", split_axis=0, concat_axis=0, tiled=True)
    expert_grads = (
        lax.psum_scatter(
            grad_up[None].astype(jnp.bfloat16), "dp", scatter_dimension=2, tiled=True
        ).astype(jnp.float32),
        lax.psum_scatter(
            grad_down[None].astype(jnp.bfloat16), "dp", scatter_dimension=1, tiled=True
        ).astype(jnp.float32),
    )
    grad_padded = jnp.concatenate(
        [grad_sent.reshape(groups * capacity, model), jnp.zeros((1, model), jnp.bfloat16)], 0
    )
    grad_norm_r, grad_router = gate_back(grad_gate)
    grad_norm_two = grad_padded[target].astype(jnp.float32) + grad_norm_r
    _, norm_two_back = jax.vjp(rms_norm, hidden_one, ffn_f)
    grad_hidden_n, grad_ffn_gain = norm_two_back(grad_norm_two)
    grad_hidden = grad_out + grad_hidden_n
    grad_mixer = grad_hidden.astype(jnp.bfloat16)
    grad_output_w = contract(gated_low, grad_mixer)
    grad_gated = product_back(grad_mixer, w_output)
    grad_scanned = grad_gated * gate_act
    grad_gate_in = grad_gated * scanned * silu_slope(gate_in)
    grad_skip = jnp.sum(grad_scanned * inner_val, axis=0)
    (_, start_grad), _ = lax.scan(
        partial(start_terms, rate),
        (zero_run, zero_state),
        (
            delta_blocks,
            grad_scanned.reshape(block_count, BLK, width),
            c_coeff.reshape(block_count, BLK, states),
            before_mask.reshape(block_count, BLK),
        ),
    )
    _, later_grad = entering((through, start_grad), "expert", combine, identity, True)
    scan_grads = scan_back((later_grad, grad_scanned))
    grad_delta = scan_grads[0]
    grad_b = scan_grads[2]
    grad_c = scan_grads[3]
    grad_decay = (scan_grads[4] * rate).T
    grad_pre_step = (grad_delta * jax.nn.sigmoid(step_pre)).astype(jnp.bfloat16)
    grad_step_bias = jnp.sum(grad_pre_step.astype(jnp.float32), axis=0)
    grad_step_w = contract(step_low, grad_pre_step)
    grad_step_low = product_back(grad_pre_step, w_step)
    grad_selected = jnp.concatenate([grad_step_low, grad_b, grad_c], 1).astype(jnp.bfloat16)
    grad_select_w = contract(inner_low, grad_selected)
    grad_inner = grad_scanned * skip_f + scan_grads[1] + product_back(grad_selected, w_select)
    grad_conv = grad_inner * silu_slope(conv_sum)
    grad_conv_b = jnp.sum(grad_conv, axis=0)
    grad_extended = jnp.zeros((rows + taps - 1, width), jnp.float32)
    kernel_rows = []
    for lag in range(taps):
        weighted = valid_list[lag][:, None] * grad_conv
        kernel_rows.append(
            jnp.sum(weighted * extended[taps - 1 - lag : taps - 1 - lag + rows], axis=0)
        )
        grad_extended = grad_extended + jnp.pad(
            weighted * conv_f[taps - 1 - lag], ((taps - 1 - lag, lag), (0, 0))
        )
    grad_kernel = jnp.stack(kernel_rows[::-1])
    returned_edge = shifted(grad_extended[: taps - 1], "expert", -1)
    grad_conv_in = (
        grad_extended[taps - 1 :].at[rows - taps + 1 :].add(returned_edge * edge_keep[:, None])
    )
    grad_mixed = jnp.concatenate([grad_conv_in, grad_gate_in], 1).astype(jnp.bfloat16)
    grad_input_w = contract(norm_low, grad_mixed)
    grad_norm_one = product_back(grad_mixed, w_input)
    _, norm_one_back = jax.vjp(rms_norm, hidden_in, norm_f)
    grad_tokens_n, grad_norm_gain = norm_one_back(grad_norm_one)
    grad_tokens = (grad_hidden + grad_tokens_n).astype(jnp.bfloat16)
    parts = (
        lax.psum_scatter(
            grad_input_w.astype(jnp.bfloat16), "dp", scatter_dimension=1, tiled=True
        ).astype(jnp.float32),
        lax.psum_scatter(
            grad_kernel.astype(jnp.bfloat16), "dp", scatter_dimension=1, tiled=True
        ).astype(jnp.float32),
        lax.psum_scatter(
            grad_conv_b.astype(jnp.bfloat16), "dp", scatter_dimension=0, tiled=True
        ).astype(jnp.float32),
        lax.psum_scatter(
            grad_select_w.astype(jnp.bfloat16), "dp", scatter_dimension=0, tiled=True
        ).astype(jnp.float32),
        lax.psum_scatter(
            grad_step_w.astype(jnp.bfloat16), "dp", scatter_dimension=1, tiled=True
        ).astype(jnp.float32),
        lax.psum_scatter(
            grad_step_bias.astype(jnp.bfloat16), "dp", scatter_dimension=0, tiled=True
        ).astype(jnp.float32),
        lax.psum_scatter(
            grad_decay.astype(jnp.bfloat16), "dp", scatter_dimension=0, tiled=True
        ).astype(jnp.float32),
        lax.psum_scatter(
            grad_skip.astype(jnp.bfloat16), "dp", scatter_dimension=0, tiled=True
        ).astype(jnp.float32),
        lax.psum_scatter(
            grad_output_w.astype(jnp.bfloat16), "dp", scatter_dimension=0, tiled=True
        ).astype(jnp.float32),
        lax.psum_scatter(
            grad_norm_gain.astype(jnp.bfloat16), "dp", scatter_dimension=0, tiled=True
        ).astype(jnp.float32),
        lax.psum_scatter(
            grad_ffn_gain.astype(jnp.bfloat16), "dp", scatter_dimension=0, tiled=True
        ).astype(jnp.float32),
        lax.psum_scatter(
            grad_router.astype(jnp.bfloat16), "dp", scatter_dimension=0, tiled=True
        ).astype(jnp.float32),
    )
    (
        part_input,
        part_kernel,
        part_conv_b,
        part_select,
        part_step,
        part_step_b,
        part_decay,
        part_skip,
        part_output,
        part_norm,
        part_ffn,
        part_router,
    ) = parts
    summed = (
        lax.psum(part_input.astype(jnp.bfloat16), "expert").astype(jnp.float32),
        lax.psum(part_kernel.astype(jnp.bfloat16), "expert").astype(jnp.float32),
        lax.psum(part_conv_b.astype(jnp.bfloat16), "expert").astype(jnp.float32),
        lax.psum(part_select.astype(jnp.bfloat16), "expert").astype(jnp.float32),
        lax.psum(part_step.astype(jnp.bfloat16), "expert").astype(jnp.float32),
        lax.psum(part_step_b.astype(jnp.bfloat16), "expert").astype(jnp.float32),
        lax.psum(part_decay.astype(jnp.bfloat16), "expert").astype(jnp.float32),
        lax.psum(part_skip.astype(jnp.bfloat16), "expert").astype(jnp.float32),
        lax.psum(part_output.astype(jnp.bfloat16), "expert").astype(jnp.float32),
        lax.psum(part_norm.astype(jnp.bfloat16), "expert").astype(jnp.float32),
        lax.psum(part_ffn.astype(jnp.bfloat16), "expert").astype(jnp.float32),
        lax.psum(part_router.astype(jnp.bfloat16), "expert").astype(jnp.float32),
    )
    (
        sum_input,
        sum_kernel,
        sum_conv_b,
        sum_select,
        sum_step,
        sum_step_b,
        sum_decay,
        sum_skip,
        sum_output,
        sum_norm,
        sum_ffn,
        sum_router,
    ) = summed
    return (
        output,
        grad_tokens,
        sum_input,
        sum_kernel,
        sum_conv_b,
        sum_select,
        sum_step,
        sum_step_b,
        sum_decay,
        sum_skip,
        sum_output,
        sum_norm,
        sum_ffn,
        sum_router,
        expert_grads[0],
        expert_grads[1],
    )


def solution(mesh):
    placed = (
        P(("dp", "expert"), None),
        P(("dp", "expert"), None),
        P(("dp", "expert"), None),
        P(("dp", "expert")),
        P(None, "dp"),
        P(None, "dp"),
        P("dp"),
        P("dp", None),
        P(None, "dp"),
        P("dp"),
        P("dp", None),
        P("dp"),
        P("dp", None),
        P("dp"),
        P("dp"),
        P("dp", None),
        P("expert", None, "dp"),
        P("expert", "dp", None),
    )
    return jax.shard_map(
        body,
        mesh=mesh,
        in_specs=placed,
        out_specs=(
            P(("dp", "expert"), None),
            P(("dp", "expert"), None),
            P(None, "dp"),
            P(None, "dp"),
            P("dp"),
            P("dp", None),
            P(None, "dp"),
            P("dp"),
            P("dp", None),
            P("dp"),
            P("dp", None),
            P("dp"),
            P("dp"),
            P("dp", None),
            P("expert", None, "dp"),
            P("expert", "dp", None),
        ),
        check_vma=False,
    )
```

profile of v0, /device:TPU:4, one launch (start us, length us, event | category | flops | bytes accessed | tf_op | source)
XLA Modules:
  0.0 5733.7 jit_solution(14226618242834667257)
XLA Ops:
  18.8 23.6 all-reduce.179
  151.7 68.5 %while.97 = (s32[]{:T(128)}, f32[2304]{0:T(1024)S(1)}, f32[16,2304]{1,0:T(8,128)S(1)}, f32[24,32,2304]{2,1,0:T(8,128)}, f32[16,2304]{1,0:T(8,128)S(1)}, /*index=...) while((s32[]{:T(128)}, f32[2304]{0:T(1024)S(1)}, ...), condition=%wide.region_7.8_spmd.clone, body=%wide.region_4.7_spmd.clone.sunk | while | flops 8368131 | bytes 4028951 | solution.py:241
  245.4 1111.4 %while.96 = (s32[]{:T(128)}, f32[16,2304]{1,0:T(8,128)S(1)}, f32[24,32,2304]{2,1,0:T(8,128)}, f32[24,16,2304]{2,1,0:T(8,128)}, f32[24,32,2304]{2,1,0:T(8,128)}, ...) while((s32[]{:T(128)}, f32[16,2304]{1,0:T(8,128)S(1)}, ...), condition=%wide.region_43.44_spmd, body=%wide.region_10.43_spmd.sunk | while | flops 11206689 | bytes 12106633 | solution.py:75
  1393.6 74.6 %all-to-all-done = bf16[4,384,1152]{2,1,0:T(8,128)(2,1)} async-done(((bf16[4,384,1152]{2,1,0:T(8,128)(2,1)}), bf16[4,384,1152]{2,1,0:T(8,128)(2,1)}, u32[]{:S(2)}, u32[]{:S(2)}) %all-to-all-start) | async-done | bytes 3538976 | tf_op jit(solution)/shard_map/all_to_all | solution.py:277
  1486.3 22.9 convolution_convert_fusion.6
  1528.9 63.9 %all-to-all-done.1 = bf16[4,384,1152]{2,1,0:T(8,128)(2,1)} async-done(((bf16[4,384,1152]{2,1,0:T(8,128)(2,1)}), bf16[4,384,1152]{2,1,0:T(8,128)(2,1)}, u32[]{:S(2)}, u32[]{:S(2)}) %all-to-all-start.1) | async-done | bytes 3538976 | tf_op jit(solution)/shard_map/all_to_all | solution.py:288
  1619.8 81.6 %all_to_all.20 = bf16[4,384,1152]{2,1,0:T(8,128)(2,1)S(1)} all-to-all(bf16[4,384,1152]{2,1,0:T(8,128)(2,1)S(1)} %bitcast.897), channel_id=1, replica_groups=mesh['dp'=8,'expert'=4] {'expert'}, dimensions={0} | all-to-all | bytes 7077888 | tf_op jit(solution)/shard_map/all_to_all | solution.py:303
  1701.5 28.6 fusion.139
  1756.6 72.5 %all-to-all-done.3 = bf16[4,384,1152]{2,1,0:T(8,128)(2,1)} async-done(((bf16[4,384,1152]{2,1,0:T(8,128)(2,1)}), bf16[4,384,1152]{2,1,0:T(8,128)(2,1)}, u32[]{:S(2)}, u32[]{:S(2)}) %all-to-all-start.3) | async-done | bytes 3538976 | tf_op jit(solution)/shard_map/all_to_all | solution.py:318
  1864.8 104.8 %while.99 = (s32[]{:T(128)}, f32[2304]{0:T(1024)S(1)}, f32[16,2304]{1,0:T(8,128)S(1)}, f32[24,32,2304]{2,1,0:T(8,128)}, f32[16,2304]{1,0:T(8,128)S(1)}, /*index=...) while((s32[]{:T(128)}, f32[2304]{0:T(1024)S(1)}, ...), condition=%wide.region_59.60_spmd.clone, body=%wide.region_56.59_spmd.clone.sunk | while | flops 8294403 | bytes 3724815 | solution.py:341
  1995.2 3127.8 %while.101 = (s32[]{:T(128)}, f32[16,2304]{1,0:T(8,128)S(1)}, f32[16,2304]{1,0:T(8,128)S(1)}, f32[24,32,2304]{2,1,0:T(8,128)}, f32[24,32,2304]{2,1,0:T(8,128)}, ...) while((s32[]{:T(128)}, f32[16,2304]{1,0:T(8,128)S(1)}, ...), condition=%wide.region_191.192_spmd.clone, body=%wide.region_62.191_spmd.clone.sunk | while | flops 56985604 | bytes 32162180 | solution.py:75
  2070.0 22.8 select_add_fusion.8
  2200.3 22.8 select_add_fusion.8
  2330.6 22.8 select_add_fusion.8
  2460.9 22.8 select_add_fusion.8
  2591.2 22.8 select_add_fusion.8
  2721.5 22.8 select_add_fusion.8
  2851.8 22.8 select_add_fusion.8
  2982.1 22.8 select_add_fusion.8
  3112.4 22.8 select_add_fusion.8
  3242.6 22.8 select_add_fusion.8
  3503.2 22.8 select_add_fusion.8
  4154.8 22.8 select_add_fusion.8
  4676.0 22.8 select_add_fusion.8
  5133.3 28.4 multiply_reduce_fusion.198
  5274.2 36.5 reduce-scatter.22.cloned.1.call-done
  5327.6 30.2 copy.122
  5390.7 66.3 %reduce-scatter.20.cloned.1.call-done = bf16[1152,576]{0,1:T(8,128)(2,1)} async-done(((bf16[1152,4608]{0,1:T(8,128)(2,1)}), bf16[1152,576]{0,1:T(8,128)(2,1)}) %reduce-scatter.20.cloned.1.call-update) | async-done | bytes 1327120 | tf_op jit(solution)/shard_map/reduce_scatter | solution.py:388
  5462.4 34.9 all-reduce.185.cloned.1.call-done
  5510.3 56.1 reduce-scatter.36.cloned.1.call-done
  5571.8 63.9 %reduce-scatter.26.cloned.1.call-done = bf16[1,384,1152]{2,1,0:T(8,128)(2,1)} async-done(((bf16[1,3072,1152]{2,1,0:T(8,128)(2,1)}), bf16[1,384,1152]{2,1,0:T(8,128)(2,1)}) %reduce-scatter.26.cloned.1.call-update) | async-done | bytes 884752 | tf_op jit(solution)/shard_map/reduce_scatter | solution.py:323
  5638.3 83.2 %all-reduce.187.cloned.1.call-done = (bf16[1152,576]{0,1:T(8,128)(2,1)}, bf16[288,1152]{1,0:T(8,128)(2,1)}) async-done(((bf16[1152,576]{0,1:T(8,128)(2,1)}, bf16[288,1152]{1,0:T(8,128)(2,1)}), (bf16[1152,576]{0,1:T(8,128)(2,1)}, bf16[288,1152]{1,0:T(8,128)(2,1)})) %all-reduce.187.cloned.1.call-update) | async-done | bytes 1990672 | tf_op jit(solution)/shard_map/psum | solution.py:440
  (5129 shorter events, 4628.1 us)
Async XLA Ops:
  7.2 73.4 %copy-start.11 = (bf16[768,1152]{1,0:T(8,128)(2,1)S(1)}, bf16[768,1152]{1,0:T(8,128)(2,1)}, u32[]{:S(2)}) copy-start(bf16[768,1152]{1,0:T(8,128)(2,1)} %param.32) | copy-start | bytes 5308420
  7.2 69.7 %copy-start.66 = (s32[768,1]{0,1:T(1,128)S(1)}, s32[768,1]{0,1:T(1,128)}, u32[]{:S(2)}) copy-start(s32[768,1]{0,1:T(1,128)} %param.34) | copy-start | bytes 9220
  7.2 73.4 %all-gather.12.cloned.1.call-start = ((), (), s32[]{:S(2)}) async-start(), calls=%async_computation.13 | async-start | bytes 11943936 | tf_op jit(solution)/shard_map/all_gather | solution.py:150
  7.9 1357.1 %all-gather.14.cloned.1.call-start = ((), (), s32[]{:S(2)}) async-start(), calls=%async_computation.14 | async-start | bytes 5971968 | tf_op jit(solution)/shard_map/all_gather | solution.py:158
  8.7 1384.9 %all-gather.16.cloned.1.call-start = ((), (), s32[]{:S(2)}) async-start(), calls=%async_computation.15 | async-start | bytes 7962624 | tf_op jit(solution)/shard_map/all_gather | solution.py:162
  9.4 1476.9 %all-gather.18.cloned.1.call-start = ((), (), s32[]{:S(2)}) async-start(), calls=%async_computation.16 | async-start | bytes 7962624 | tf_op jit(solution)/shard_map/all_gather | solution.py:163
  55.3 59.7 %copy-start.37 = (f32[2304]{0:T(1024)}, f32[2304]{0:T(1024)S(1)}, u32[]{:S(2)}) copy-start(f32[2304]{0:T(1024)S(1)} %get-tuple-element.1437) | copy-start | bytes 27652
  55.3 59.7 %copy-start.39 = (f32[2304]{0:T(1024)}, f32[2304]{0:T(1024)S(1)}, u32[]{:S(2)}) copy-start(f32[2304]{0:T(1024)S(1)} %get-tuple-element.1438) | copy-start | bytes 27652
  96.0 16.2 collective-permute-start
  112.2 1244.6 %copy-start.35 = (f32[2304]{0:T(1024)}, f32[2304]{0:T(1024)S(1)}, u32[]{:S(2)}) copy-start(f32[2304]{0:T(1024)S(1)} %convert_element_type.334) | copy-start | bytes 27652
  112.2 1261.7 %copy-start.24 = (f32[1152]{0:T(1024)}, f32[1152]{0:T(1024)S(1)}, u32[]{:S(2)}) copy-start(f32[1152]{0:T(1024)S(1)} %convert_element_type.337) | copy-start | bytes 13828
  1373.9 151.6 %copy-start.3 = (f32[768,1152]{1,0:T(8,128)}, f32[768,1152]{1,0:T(8,128)S(1)}, u32[]{:S(2)}) copy-start(f32[768,1152]{1,0:T(8,128)S(1)} %get-tuple-element.1929) | copy-start | bytes 10616836
  1388.6 79.6 %all-to-all-start = ((bf16[4,384,1152]{2,1,0:T(8,128)(2,1)}), bf16[4,384,1152]{2,1,0:T(8,128)(2,1)}, u32[]{:S(2)}, u32[]{:S(2)}) async-start(bf16[4,384,1152]{2,1,0:T(8,128)(2,1)} %bitcast.898), calls=%async_computation | async-start | bytes 7077888 | tf_op jit(solution)/shard_map/all_to_all | solution.py:277
  1509.2 83.5 %all-to-all-start.1 = ((bf16[4,384,1152]{2,1,0:T(8,128)(2,1)}), bf16[4,384,1152]{2,1,0:T(8,128)(2,1)}, u32[]{:S(2)}, u32[]{:S(2)}) async-start(bf16[4,384,1152]{2,1,0:T(8,128)(2,1)} %bitcast.904), calls=%async_computation.1 | async-start | bytes 7077888 | tf_op jit(solution)/shard_map/all_to_all | solution.py:288
  1528.2 68.6 %copy-start.45 = (s32[1024]{0:T(1024)S(1)}, s32[1024]{0:T(1024)}, u32[]{:S(2)}) copy-start(s32[1024]{0:T(1024)} %pad_clamp_fusion) | copy-start | bytes 12292
  1619.8 110.2 %slice-start.8 = ((s8[7077888]{0:T(1024)(128)(4,1)}), s8[4194304]{0:T(1024)(128)(4,1)S(1)}, s32[]{:S(2)}) async-start(s8[7077888]{0:T(1024)(128)(4,1)} %bitcast.992), calls=%async_computation.36 | async-start | bytes 8388608
  1746.0 83.1 %all-to-all-start.3 = ((bf16[4,384,1152]{2,1,0:T(8,128)(2,1)}), bf16[4,384,1152]{2,1,0:T(8,128)(2,1)}, u32[]{:S(2)}, u32[]{:S(2)}) async-start(bf16[4,384,1152]{2,1,0:T(8,128)(2,1)} %bitcast.903), calls=%async_computation.3 | async-start | bytes 7077888 | tf_op jit(solution)/shard_map/all_to_all | solution.py:318
  1750.9 3468.5 %reduce-scatter.34.cloned.1.call-start = ((), (), s32[]{:S(2)}) async-start(), calls=%async_computation.24 | async-start | bytes 331776
  1756.1 3464.7 %reduce-scatter.28.cloned.1.call-start = ((), (), s32[]{:S(2)}) async-start(), calls=%async_computation.21 | async-start | bytes 663552
  1995.2 3128.1 %copy-start.30 = (f32[2304]{0:T(1024)S(1)}, f32[2304]{0:T(1024)}, u32[]{:S(2)}) copy-start(f32[2304]{0:T(1024)} %copy-done.29) | copy-start | bytes 27652
  5163.0 101.9 %reduce-scatter.32.cloned.1.call-start = ((), (), s32[]{:S(2)}) async-start(), calls=%async_computation.23 | async-start | bytes 663552
  5165.8 106.8 %reduce-scatter.30.cloned.1.call-start = ((), (), s32[]{:S(2)}) async-start(), calls=%async_computation.22 | async-start | bytes 663552
  5171.6 139.2 %reduce-scatter.22.cloned.1.call-start = ((), (), s32[]{:S(2)}) async-start(), calls=%async_computation.18 | async-start | bytes 663552 | tf_op jit(solution)/shard_map/reduce_scatter | solution.py:397
  5175.7 215.0 %reduce-scatter.24.cloned.1.call-start = ((), (), s32[]{:S(2)}) async-start(), calls=%async_computation.19 | async-start | bytes 5971968 | tf_op jit(solution)/shard_map/reduce_scatter | solution.py:412
  5185.2 271.8 %reduce-scatter.20.cloned.1.call-start = ((), (), s32[]{:S(2)}) async-start(), calls=%async_computation.17 | async-start | bytes 11943936 | tf_op jit(solution)/shard_map/reduce_scatter | solution.py:388
  5186.4 13.9 collective-permute-start.1
  5217.9 279.4 %all-reduce.185.cloned.1.call-start = ((), (), s32[]{:S(2)}) async-start(), calls=%async_computation.26 | async-start | bytes 301056 | tf_op jit(solution)/shard_map/psum | solution.py:441
  5310.8 255.7 %reduce-scatter.36.cloned.1.call-start = ((), (), s32[]{:S(2)}) async-start(), calls=%async_computation.25 | async-start | bytes 7962624
  5367.3 268.5 %reduce-scatter.26.cloned.1.call-start = ((), (), s32[]{:S(2)}) async-start(), calls=%async_computation.20 | async-start | bytes 7962624 | tf_op jit(solution)/shard_map/reduce_scatter | solution.py:323
  5390.6 66.4 %copy-start.47 = (f32[768]{0:T(1024)S(1)}, f32[768]{0:T(1024)}, u32[]{:S(2)}) copy-start(f32[768]{0:T(1024)} %copy-done.46) | copy-start | bytes 9220
  5390.6 67.1 %copy-start.10 = (f32[768,1152]{1,0:T(8,128)S(1)}, f32[768,1152]{1,0:T(8,128)}, u32[]{:S(2)}) copy-start(f32[768,1152]{1,0:T(8,128)} %get-tuple-element.1916) | copy-start | bytes 10616836
  5390.6 330.9 %all-reduce.187.cloned.1.call-start = ((), (), s32[]{:S(2)}) async-start(), calls=%async_computation.27 | async-start | bytes 3981312 | tf_op jit(solution)/shard_map/psum | solution.py:440
  (70 other events, 1005.4 us)
Sparse Core Ops, SparseCore 0:
  9.9 67.7 all-gather.11
  79.6 42.6 all-gather.13
  124.2 48.5 all-gather.15
  174.5 49.7 all-gather.17
  1756.2 33.4 reduce-scatter.33
  5163.1 33.2 reduce-scatter.27
  5200.1 34.3 reduce-scatter.31
  5238.2 34.3 reduce-scatter.29
  5276.3 34.3 reduce-scatter.21
  5314.0 56.8 reduce-scatter.23
  5374.9 82.0 reduce-scatter.19
  5461.5 35.8 all-reduce.184
  5500.8 65.5 reduce-scatter.35
  5570.2 65.5 reduce-scatter.25
  5638.1 83.3 all-reduce.186
where the time goes:
time: 5800 us; the launch traced here: 5730 us
  other arithmetic  3930 us (68%)
  local copies, waits for them, and re-layouts  692 us (12%)
  waiting for transfers between devices  561 us (10%)
  matrix products  261 us (4%)
  blocking collectives  221 us (4%)
    reduce_sum x384, other arithmetic, scan_block(): decay = jnp.exp(rate * delta[step][None, :]) * keep[step]  1340 us
    reduce_sum x288, other arithmetic, scan_block(): outputs.append(jnp.sum(state * c_coeff[step][:, None], axis=0))  1320 us
    add_any x24, other arithmetic, run_scan(): lax.scan(jax.checkpoint(partial(scan_block, rate)), state, blocks)  548 us
    reduce_sum x264, other arithmetic, scan_block(): b_coeff[step][:, None] * (delta[step] * values[step])[None, :]  391 us
    slice x168, local copies, waits for them, and re-layouts, scan_block(): decay = jnp.exp(rate * delta[step][None, :]) * keep[step]  180 us

commit v1 on v0

v1 whole, which is shorter than its diff:
```python
from functools import partial

import jax
import jax.numpy as jnp
from jax import lax
from jax.experimental import pallas as pl
from jax.experimental.pallas import tpu as pltpu
from jax.sharding import PartitionSpec as P

TC = 16
ROWS = 64
FAR = 1e4
LOG2E = 1.4426950408889634
LN2 = 0.6931471805599453
F32 = jnp.float32
BF16 = jnp.bfloat16


def tiled(x, n):
    return jnp.concatenate([x] * n, axis=1) if n > 1 else x


def folded(x):
    n = x.shape[1] // 128
    out = x[:, :128]
    for i in range(1, n):
        out = out + x[:, i * 128 : (i + 1) * 128]
    return out


def dot(a, b):
    return jnp.dot(a, b, preferred_element_type=F32)


def prepare(s_ref, w_ref, b_ref, st_ref, u_ref, dk_ref, dv_ref, pre_ref=None):
    def block(i, carry):
        r = pl.ds(pl.multiple_of(i * ROWS, ROWS), ROWS)
        pre = dot(s_ref[r, :], w_ref[...]) + b_ref[...].astype(F32)
        delta = jnp.maximum(pre, 0.0) + jnp.log1p(jnp.exp(-jnp.abs(pre)))
        dk = jnp.where(st_ref[r, :] > 0.0, FAR, delta)
        dk_ref[r, :] = dk
        if u_ref is not None:
            dv_ref[r, :] = delta * u_ref[r, :].astype(F32)
        if pre_ref is not None:
            pre_ref[r, :] = pre
        return carry + jnp.sum(dk, axis=0, keepdims=True)

    return lax.fori_loop(
        0, s_ref.shape[0] // ROWS, block, jnp.zeros((1, w_ref.shape[1]), F32)
    )


def end_kernel(s_ref, w_ref, b_ref, st_ref, u_ref, a_ref, bb_ref, end_ref, sum_ref, dk_ref, dv_ref):
    reps = w_ref.shape[1] // 128
    sum_ref[...] = prepare(s_ref, w_ref, b_ref, st_ref, u_ref, dk_ref, dv_ref)
    a = a_ref[...]

    def chunk(c, h):
        t0 = pl.multiple_of(c * TC, TC)
        for i in range(TC):
            f = jnp.exp2(a * dk_ref[pl.ds(t0 + i, 1), :])
            h = f * h + dv_ref[pl.ds(t0 + i, 1), :] * tiled(bb_ref[t0 + i], reps)
        return h

    end_ref[...] = lax.fori_loop(0, s_ref.shape[0] // TC, chunk, jnp.zeros_like(a))


def forward_kernel(
    s_ref, w_ref, b_ref, st_ref, u_ref, z_ref, a_ref, skip_ref, bb_ref, cm_ref, h0_ref,
    g_ref, y_ref, ck_ref, dk_ref, dv_ref, ys_ref, hb0, hb1,
):
    reps = w_ref.shape[1] // 128
    states = a_ref.shape[0]
    chunks = s_ref.shape[0] // TC
    prepare(s_ref, w_ref, b_ref, st_ref, u_ref, dk_ref, dv_ref)
    a = a_ref[...]
    hb1[...] = jnp.zeros_like(hb1)

    def scan(c, h, hb):
        t0 = pl.multiple_of(c * TC, TC)
        ck_ref[c] = h
        for i in range(TC):
            f = jnp.exp2(a * dk_ref[pl.ds(t0 + i, 1), :])
            h = f * h + dv_ref[pl.ds(t0 + i, 1), :] * tiled(bb_ref[t0 + i], reps)
            hb[pl.ds(i * states, states), :] = h.astype(BF16)
        return h

    def emit(c, hb):
        t0 = pl.multiple_of(c * TC, TC)
        ys_ref[pl.ds(t0, TC), :] = dot(cm_ref[c], hb[...])

    def pair(c, h):
        emit(jnp.maximum(2 * c - 1, 0), hb1)
        h = scan(2 * c, h, hb0)
        emit(2 * c, hb0)
        return scan(2 * c + 1, h, hb1)

    lax.fori_loop(0, chunks // 2, pair, h0_ref[...])
    emit(chunks - 1, hb1)

    def finish(i, carry):
        r = pl.ds(pl.multiple_of(i * ROWS, ROWS), ROWS)
        y = ys_ref[r, :] + skip_ref[...].astype(F32) * u_ref[r, :].astype(F32)
        z = z_ref[r, :].astype(F32)
        y_ref[r, :] = y.astype(BF16)
        g_ref[r, :] = (y * (z / (1.0 + jnp.exp(-z)))).astype(BF16)
        return carry

    lax.fori_loop(0, s_ref.shape[0] // ROWS, finish, 0)


def start_kernel(s_ref, w_ref, b_ref, st_ref, dg_ref, z_ref, a_ref, cb_ref, out_ref, dk_ref, dy_ref):
    reps = w_ref.shape[1] // 128
    chunks = s_ref.shape[0] // TC
    prepare(s_ref, w_ref, b_ref, st_ref, None, dk_ref, None)

    def gate(i, carry):
        r = pl.ds(pl.multiple_of(i * ROWS, ROWS), ROWS)
        z = z_ref[r, :].astype(F32)
        dy_ref[r, :] = dg_ref[r, :].astype(F32) * (z / (1.0 + jnp.exp(-z)))
        return carry

    lax.fori_loop(0, s_ref.shape[0] // ROWS, gate, 0)
    a = a_ref[...]

    def chunk(j, grad):
        t0 = pl.multiple_of((chunks - 1 - j) * TC, TC)
        for i in range(TC - 1, -1, -1):
            f = jnp.exp2(a * dk_ref[pl.ds(t0 + i, 1), :])
            lam = grad + dy_ref[pl.ds(t0 + i, 1), :] * tiled(cb_ref[t0 + i], reps)
            grad = f * lam
        return grad

    out_ref[...] = lax.fori_loop(0, chunks, chunk, jnp.zeros_like(a))


def backward_kernel(
    s_ref, w_ref, b_ref, st_ref, u_ref, z_ref, y_ref, dg_ref, a_ref, skip_ref,
    bb_ref, cb_ref, bm_ref, om_ref, ck_ref, g0_ref,
    dz_ref, ds_ref, du_ref, da_ref, dskip_ref, dbc_ref,
    pre_ref, dk_ref, dv_ref, dy_ref, q_ref, p_ref, f_ref, fh_ref, lb_ref, wb_ref, accb_ref, accc_ref,
):
    step = pl.program_id(0)
    reps = w_ref.shape[1] // 128
    states = a_ref.shape[0]
    rows = s_ref.shape[0]
    chunks = rows // TC
    prepare(s_ref, w_ref, b_ref, st_ref, u_ref, dk_ref, dv_ref, pre_ref)

    @pl.when(step == 0)
    def _():
        accb_ref[...] = jnp.zeros_like(accb_ref)
        accc_ref[...] = jnp.zeros_like(accc_ref)

    def gate(i, carry):
        r = pl.ds(pl.multiple_of(i * ROWS, ROWS), ROWS)
        z = z_ref[r, :].astype(F32)
        dg = dg_ref[r, :].astype(F32)
        sig = 1.0 / (1.0 + jnp.exp(-z))
        dy = dg * (z * sig)
        dy_ref[r, :] = dy
        dz_ref[r, :] = (dg * y_ref[r, :].astype(F32) * (sig * (1.0 + z * (1.0 - sig)))).astype(BF16)
        return carry + jnp.sum(dy * u_ref[r, :].astype(F32), axis=0, keepdims=True)

    dskip_ref[...] = lax.fori_loop(0, rows // ROWS, gate, jnp.zeros(dskip_ref.shape, F32))
    a = a_ref[...]

    def chunk(j, carry):
        grad, da = carry
        c = chunks - 1 - j
        t0 = pl.multiple_of(c * TC, TC)
        h = ck_ref[c]
        for i in range(TC):
            f = jnp.exp2(a * dk_ref[pl.ds(t0 + i, 1), :])
            fh = f * h
            h = fh + dv_ref[pl.ds(t0 + i, 1), :] * tiled(bb_ref[t0 + i], reps)
            f_ref[i] = f
            fh_ref[i] = fh
            accc_ref[t0 + i] += folded(dy_ref[pl.ds(t0 + i, 1), :] * h)
        for i in range(TC - 1, -1, -1):
            lam = grad + dy_ref[pl.ds(t0 + i, 1), :] * tiled(cb_ref[t0 + i], reps)
            grad = f_ref[i] * lam
            lb_ref[pl.ds(i * states, states), :] = lam.astype(BF16)
            w = lam * fh_ref[i]
            wb_ref[pl.ds(i * states, states), :] = (w * a).astype(BF16)
            da = da + w * dk_ref[pl.ds(t0 + i, 1), :]
            accb_ref[t0 + i] += folded(lam * dv_ref[pl.ds(t0 + i, 1), :])
        q_ref[pl.ds(t0, TC), :] = dot(bm_ref[c], lb_ref[...])
        p_ref[pl.ds(t0, TC), :] = dot(om_ref[...], wb_ref[...])
        return grad, da

    _, da = lax.fori_loop(0, chunks, chunk, (g0_ref[...], jnp.zeros_like(a)))
    da_ref[...] = da * a * LN2

    def finish(i, carry):
        r = pl.ds(pl.multiple_of(i * ROWS, ROWS), ROWS)
        u = u_ref[r, :].astype(F32)
        q = q_ref[r, :]
        pre = pre_ref[r, :]
        delta = jnp.maximum(pre, 0.0) + jnp.log1p(jnp.exp(-jnp.abs(pre)))
        dd = p_ref[r, :] * LN2 + u * q
        ds_ref[r, :] = (dd / (1.0 + jnp.exp(-pre))).astype(BF16)
        du_ref[r, :] = delta * q + dy_ref[r, :] * skip_ref[...].astype(F32)
        return carry

    lax.fori_loop(0, rows // ROWS, finish, 0)

    @pl.when(step == pl.num_programs(0) - 1)
    def _():
        ones = jnp.ones((128, 128), BF16)
        row = lax.broadcasted_iota(jnp.int32, (TC * states, 128), 0) % states
        lane = lax.broadcasted_iota(jnp.int32, (TC * states, 128), 1)

        def gather(c, carry):
            t0 = pl.multiple_of(c * TC, TC)
            b = dot(accb_ref[pl.ds(t0, TC)].reshape(TC * states, 128).astype(BF16), ones)
            d = dot(accc_ref[pl.ds(t0, TC)].reshape(TC * states, 128).astype(BF16), ones)
            both = jnp.where(lane == row, b, jnp.where(lane == row + states, d, 0.0))
            dbc_ref[pl.ds(t0, TC), :] = dot(om_ref[...], both.astype(BF16)).astype(BF16)
            return carry

        lax.fori_loop(0, chunks, gather, 0)


def scan_width(width, limit):
    n = width // 128
    best = max(d for d in range(1, n + 1) if n % d == 0 and d * 128 <= limit)
    return best * 128


def specs(rows, cb, states, chunks):
    tok = lambda n: pl.BlockSpec((rows, n), lambda k: (0, 0))
    chan = lambda n: pl.BlockSpec((n, cb), lambda k: (0, k))
    full3 = lambda a, b, c: pl.BlockSpec((a, b, c), lambda k: (0, 0, 0), pipeline_mode=pl.Buffered(1))
    ck = pl.BlockSpec((chunks, states, cb), lambda k: (0, 0, k))
    return tok, chan, full3, ck


def params():
    return pltpu.CompilerParams(vmem_limit_bytes=58 * 2**20)


def sds(*a):
    return jax.ShapeDtypeStruct(*a)


def end_states(s, w, b, st, u, a, bb):
    rows, width, states = s.shape[0], w.shape[1], a.shape[0]
    cb = scan_width(width, 768)
    tok, chan, full3, ck = specs(rows, cb, states, rows // TC)
    return pl.pallas_call(
        end_kernel,
        grid=(width // cb,),
        in_specs=[tok(s.shape[1]), chan(w.shape[0]), chan(1), tok(1), chan(rows), chan(states), full3(rows, states, 128)],
        out_specs=[chan(states), chan(1)],
        out_shape=[sds((states, width), F32), sds((1, width), F32)],
        scratch_shapes=[pltpu.VMEM((rows, cb), F32)] * 2,
        compiler_params=params(),
        cost_estimate=pl.CostEstimate(flops=6 * rows * width * states, bytes_accessed=rows * width * 2, transcendentals=rows * width * states),
        name="end_states",
    )(s, w, b, st, u, a, bb)


def forward_scan(s, w, b, st, u, z, a, skip, bb, cm, h0):
    rows, width, states = s.shape[0], w.shape[1], a.shape[0]
    cb = scan_width(width, 768)
    tok, chan, full3, ck = specs(rows, cb, states, rows // TC)
    off = z.shape[1] // cb - width // cb
    return pl.pallas_call(
        forward_kernel,
        grid=(width // cb,),
        in_specs=[tok(s.shape[1]), chan(w.shape[0]), chan(1), tok(1), chan(rows), pl.BlockSpec((rows, cb), lambda k: (0, k + off)), chan(states), chan(1), full3(rows, states, 128), full3(*cm.shape), chan(states)],
        out_specs=[chan(rows), chan(rows), ck],
        out_shape=[sds((rows, width), BF16), sds((rows, width), BF16), sds((rows // TC, states, width), F32)],
        scratch_shapes=[pltpu.VMEM((rows, cb), F32)] * 3 + [pltpu.VMEM((TC * states, cb), BF16)] * 2,
        compiler_params=params(),
        cost_estimate=pl.CostEstimate(flops=9 * rows * width * states, bytes_accessed=rows * width * 12, transcendentals=rows * width * states),
        name="forward_scan",
    )(s, w, b, st, u, z, a, skip, bb, cm, h0)


def start_grads(s, w, b, st, dg, z, a, cb_):
    rows, width, states = s.shape[0], w.shape[1], a.shape[0]
    cb = scan_width(width, 768)
    tok, chan, full3, ck = specs(rows, cb, states, rows // TC)
    off = z.shape[1] // cb - width // cb
    return pl.pallas_call(
        start_kernel,
        grid=(width // cb,),
        in_specs=[tok(s.shape[1]), chan(w.shape[0]), chan(1), tok(1), chan(rows), pl.BlockSpec((rows, cb), lambda k: (0, k + off)), chan(states), full3(rows, states, 128)],
        out_specs=chan(states),
        out_shape=sds((states, width), F32),
        scratch_shapes=[pltpu.VMEM((rows, cb), F32)] * 2,
        compiler_params=params(),
        cost_estimate=pl.CostEstimate(flops=6 * rows * width * states, bytes_accessed=rows * width * 6, transcendentals=rows * width * states),
        name="start_grads",
    )(s, w, b, st, dg, z, a, cb_)


def backward_scan(s, w, b, st, u, z, y, dg, a, skip, bb, cb_, bm, om, ck, g0):
    rows, width, states = s.shape[0], w.shape[1], a.shape[0]
    cb = scan_width(width, 384)
    tok, chan, full3, cks = specs(rows, cb, states, rows // TC)
    off = z.shape[1] // cb - width // cb
    return pl.pallas_call(
        backward_kernel,
        grid=(width // cb,),
        in_specs=[tok(s.shape[1]), chan(w.shape[0]), chan(1), tok(1), chan(rows), pl.BlockSpec((rows, cb), lambda k: (0, k + off)), chan(rows), chan(rows), chan(states), chan(1),
                  full3(rows, states, 128), full3(rows, states, 128), full3(*bm.shape), tok_full(om), cks, chan(states)],
        out_specs=[chan(rows), chan(rows), chan(rows), chan(states), chan(1), pl.BlockSpec((rows, 128), lambda k: (0, 0))],
        out_shape=[sds((rows, width), BF16), sds((rows, width), BF16), sds((rows, width), F32), sds((states, width), F32), sds((1, width), F32), sds((rows, 128), BF16)],
        scratch_shapes=[pltpu.VMEM((rows, cb), F32)] * 6
        + [pltpu.VMEM((TC, states, cb), F32)] * 2
        + [pltpu.VMEM((TC * states, cb), BF16)] * 2
        + [pltpu.VMEM((rows, states, 128), F32)] * 2,
        compiler_params=params(),
        cost_estimate=pl.CostEstimate(flops=25 * rows * width * states, bytes_accessed=rows * width * 24, transcendentals=rows * width * states),
        name="backward_scan",
    )(s, w, b, st, u, z, y, dg, a, skip, bb, cb_, bm, om, ck, g0)


def tok_full(x):
    return pl.BlockSpec(x.shape, lambda k: (0,) * x.ndim)


def spread(coeff):
    return jnp.broadcast_to(coeff[:, :, None], (*coeff.shape, 128))


def block_rows(coeff):
    rows, states = coeff.shape
    mask = jnp.arange(TC * states)[None, None] // states == jnp.arange(TC)[None, :, None]
    return jnp.where(mask, coeff.reshape(rows // TC, 1, TC * states), 0.0).astype(BF16)


epsilon = 1e-05


def shifted(array, axis, by):
    length = lax.axis_size(axis)
    pairs = [(i, i + by) for i in range(length) if 0 <= i + by < length]
    return lax.ppermute(array, axis, pairs)


def entering(through, ends, axis, reverse):
    length, here = (lax.axis_size(axis), lax.axis_index(axis))
    every = lax.all_gather(jnp.stack([through, ends]).astype(BF16), axis)
    state = jnp.zeros_like(ends)
    for k in range(length):
        at = length - 1 - k if reverse else k
        reached = at > here if reverse else at < here
        new = every[at, 0].astype(F32) * state + every[at, 1].astype(F32)
        state = jnp.where(reached, new, state)
    return state


def product_back(left, right):
    return lax.dot_general(left, right, (((1,), (1,)), ((), ())), preferred_element_type=F32)


def contract(left, right):
    return lax.dot_general(left, right, (((0,), (0,)), ((), ())), preferred_element_type=F32)


def silu_slope(values):
    sigma = jax.nn.sigmoid(values)
    return sigma * (1.0 + values * (1.0 - sigma))


def inverse_rms(values):
    return lax.rsqrt(jnp.mean(values * values, axis=-1, keepdims=True) + epsilon)


def gather_small(parts):
    n = lax.axis_size("dp")
    flat = jnp.concatenate([p.reshape(-1) for p, _ in parts])
    size = flat.shape[0]
    padded = -(-size // 1024) * 1024
    flat = jnp.pad(flat, (0, padded - size)).reshape(padded // 128, 128)
    every = lax.all_gather(flat, "dp").reshape(n, padded)
    out, at = [], 0
    for p, dim in parts:
        piece = every[:, at : at + p.size].reshape(n, *p.shape)
        at += p.size
        piece = jnp.moveaxis(piece, 0, dim)
        out.append(piece.reshape(*p.shape[:dim], n * p.shape[dim], *p.shape[dim + 1 :]))
    return out


def scatter_small(parts):
    n = lax.axis_size("dp")
    pieces, shapes = [], []
    for p, dim in parts:
        shape = (*p.shape[:dim], p.shape[dim] // n, *p.shape[dim + 1 :])
        split = p.astype(BF16).reshape(*p.shape[:dim], n, p.shape[dim] // n, *p.shape[dim + 1 :])
        pieces.append(jnp.moveaxis(split, dim, 0).reshape(n, -1))
        shapes.append(shape)
    flat = jnp.concatenate(pieces, axis=1)
    size = flat.shape[1]
    padded = -(-size // 1024) * 1024
    flat = jnp.pad(flat, ((0, 0), (0, padded - size))).reshape(n, padded // 128, 128)
    mine = lax.psum_scatter(flat, "dp", scatter_dimension=0, tiled=True)
    mine = lax.psum(mine, "expert").astype(F32).reshape(-1)
    out, at = [], 0
    for shape in shapes:
        count = 1
        for d in shape:
            count *= d
        out.append(mine[at : at + count].reshape(shape))
        at += count
    return out


def body(
    tokens, cotangent, routes, starts, input_proj, conv_kernel, conv_bias, select_proj, step_proj,
    step_bias, decay_log, skip_gain, output_proj, norm_gain, ffn_gain, router, expert_up, expert_down,
):
    w_input = lax.all_gather(input_proj, "dp", axis=1, tiled=True)
    (
        w_conv, b_conv, w_select, w_step, b_step, w_decay, w_skip, g_norm, g_ffn, w_router,
    ) = gather_small(
        [
            (conv_kernel, 1), (conv_bias, 0), (select_proj, 0), (step_proj, 1), (step_bias, 0),
            (decay_log, 0), (skip_gain, 0), (norm_gain, 0), (ffn_gain, 0), (router, 0),
        ]
    )
    w_output = lax.all_gather(output_proj, "dp", axis=0, tiled=True)
    w_up = lax.all_gather(expert_up[0], "dp", axis=1, tiled=True)
    w_down = lax.all_gather(expert_down[0], "dp", axis=0, tiled=True)
    rows, model = tokens.shape
    groups = lax.axis_size("expert")
    width = w_input.shape[1] // 2
    rank = w_step.shape[0]
    states = w_decay.shape[1]
    taps = w_conv.shape[0]
    capacity = 2 * rows // groups
    conv_f = w_conv.astype(F32)
    norm_f = g_norm.astype(F32)
    ffn_f = g_ffn.astype(F32)
    router_f = w_router.astype(F32)

    route = routes[:, 0]
    chosen = (route[:, None] == jnp.arange(groups, dtype=jnp.int32)[None, :]).astype(F32)
    before = (jnp.arange(rows)[:, None] > jnp.arange(rows)[None, :]).astype(BF16)
    ranks = dot(before, chosen.astype(BF16))
    slot = jnp.sum(ranks * chosen, axis=1).astype(jnp.int32)
    target = jnp.where(slot < capacity, route * capacity + slot, groups * capacity)
    place = (jnp.arange(groups * capacity)[:, None] == target[None, :]).astype(BF16)

    hidden_in = tokens.astype(F32)
    norm_r = inverse_rms(hidden_in)
    norm_low = (hidden_in * norm_r * norm_f).astype(BF16)
    mixed = dot(norm_low, w_input).astype(BF16)
    conv_in = mixed[:, :width]
    flag = starts.astype(F32)
    same = 1.0 - flag
    valid = [jnp.ones((rows,), F32)]
    for lag in range(1, taps):
        moved = jnp.concatenate([jnp.ones((lag - 1,), F32), same[: rows - lag + 1]])
        valid.append(valid[-1] * moved)
    edge = [jnp.ones((), F32)]
    for lag in range(1, taps - 1):
        edge.append(edge[-1] * same[rows - lag])
    edge_keep = jnp.stack(edge[::-1])[:, None]
    tail = (conv_in[rows - taps + 1 :].astype(F32) * edge_keep).astype(BF16)
    before_rows = shifted(tail, "expert", 1)
    extended = jnp.concatenate([before_rows, conv_in], 0).astype(F32)
    conv_sum = jnp.broadcast_to(b_conv.astype(F32), (rows, width))
    for lag in range(taps):
        at = taps - 1 - lag
        conv_sum = conv_sum + valid[lag][:, None] * conv_f[at] * extended[at : at + rows]
    inner_low = jax.nn.silu(conv_sum).astype(BF16)
    selected = dot(inner_low, w_select)
    step_low = selected[:, :rank].astype(BF16)
    b_coeff = selected[:, rank : rank + states]
    c_coeff = selected[:, rank + states :]
    rate2 = -jnp.exp(w_decay.astype(F32)).T * LOG2E
    st = flag[:, None]
    bias2 = b_step[None, :]
    skip2 = w_skip[None, :]
    b_wide, c_wide = spread(b_coeff), spread(c_coeff)
    b_block, c_block = block_rows(b_coeff), block_rows(c_coeff)
    one_block = (jnp.arange(TC * states)[None] // states == jnp.arange(TC)[:, None]).astype(BF16)
    local_end, total = end_states(step_low, w_step, bias2, st, inner_low, rate2, b_wide)
    through = jnp.exp2(rate2 * total)
    start_state = entering(through, local_end, "expert", False)
    gated_low, scanned, marks = forward_scan(
        step_low, w_step, bias2, st, inner_low, mixed, rate2, skip2, b_wide, c_block, start_state
    )
    hidden_one = hidden_in + dot(gated_low, w_output)

    r2 = inverse_rms(hidden_one)
    norm_two = hidden_one * r2 * ffn_f
    logits = jnp.dot(norm_two, router_f, precision=lax.Precision.HIGHEST, preferred_element_type=F32)
    probs = jax.nn.softmax(logits, axis=-1)
    gate_value = jnp.sum(probs * chosen, axis=-1)
    grad_out = cotangent.astype(F32)
    grad_picked = (gate_value[:, None] * grad_out).astype(BF16)

    def exchange(x):
        return lax.all_to_all(
            x.reshape(groups, capacity, model), "expert", split_axis=0, concat_axis=0, tiled=True
        ).reshape(groups * capacity, model)

    arrived = exchange(dot(place, norm_two.astype(BF16)).astype(BF16))
    grad_arrived = exchange(dot(place, grad_picked).astype(BF16))
    up_pre = dot(arrived, w_up)
    up_low = jax.nn.gelu(up_pre).astype(BF16)
    returned = exchange(dot(up_low, w_down).astype(BF16))
    _, gelu_back = jax.vjp(jax.nn.gelu, up_pre)
    grad_pre = gelu_back(product_back(grad_arrived, w_down))[0].astype(BF16)
    grad_sent = exchange(product_back(grad_pre, w_up).astype(BF16))
    grad_down = contract(up_low, grad_arrived)
    grad_up = contract(arrived, grad_pre)
    sum_up = lax.psum_scatter(grad_up.astype(BF16), "dp", scatter_dimension=1, tiled=True)
    sum_down = lax.psum_scatter(grad_down.astype(BF16), "dp", scatter_dimension=0, tiled=True)

    picked = contract(place, returned)
    output = (hidden_one + gate_value[:, None] * picked).astype(BF16)
    grad_gate = jnp.sum(grad_out * picked, axis=1)
    grad_logits = probs * (grad_gate[:, None] * chosen - (grad_gate * gate_value)[:, None])
    grad_router = lax.dot_general(
        norm_two, grad_logits, (((0,), (0,)), ((), ())),
        precision=lax.Precision.HIGHEST, preferred_element_type=F32,
    )
    grad_norm_two = contract(place, grad_sent) + lax.dot_general(
        grad_logits, router_f, (((1,), (1,)), ((), ())),
        precision=lax.Precision.HIGHEST, preferred_element_type=F32,
    )
    grad_ffn_gain = jnp.sum(grad_norm_two * hidden_one * r2, axis=0)
    scaled = ffn_f * grad_norm_two
    grad_hidden = (
        grad_out
        + r2 * scaled
        - hidden_one * (r2 * r2 * r2) * jnp.mean(hidden_one * scaled, axis=-1, keepdims=True)
    )

    grad_mixer = grad_hidden.astype(BF16)
    grad_output_w = contract(gated_low, grad_mixer)
    sum_output = lax.psum_scatter(grad_output_w.astype(BF16), "dp", scatter_dimension=0, tiled=True)
    grad_gated = product_back(grad_mixer, w_output)
    start_grad = start_grads(step_low, w_step, bias2, st, grad_gated, mixed, rate2, c_wide)
    later_grad = entering(through, start_grad, "expert", True)
    grad_gate_in, grad_pre_step, grad_inner, grad_decay_t, grad_skip, grad_bc = backward_scan(
        step_low, w_step, bias2, st, inner_low, mixed, scanned, grad_gated, rate2, skip2,
        b_wide, c_wide, b_block, one_block, marks, later_grad,
    )
    grad_step_bias = jnp.sum(grad_pre_step.astype(F32), axis=0)
    grad_step_w = contract(step_low, grad_pre_step)
    grad_step_low = product_back(grad_pre_step, w_step).astype(BF16)
    grad_selected = jnp.concatenate([grad_step_low, grad_bc[:, : 2 * states]], 1)
    grad_select_w = contract(inner_low, grad_selected)
    grad_conv = (grad_inner + product_back(grad_selected, w_select)) * silu_slope(conv_sum)
    grad_conv_b = jnp.sum(grad_conv, axis=0)
    grad_extended = jnp.zeros((rows + taps - 1, width), F32)
    kernel_rows = []
    for lag in range(taps):
        at = taps - 1 - lag
        weighted = valid[lag][:, None] * grad_conv
        kernel_rows.append(jnp.sum(weighted * extended[at : at + rows], axis=0))
        grad_extended = grad_extended + jnp.pad(weighted * conv_f[at], ((at, lag), (0, 0)))
    grad_kernel = jnp.stack(kernel_rows[::-1])
    returned_edge = shifted(grad_extended[: taps - 1], "expert", -1)
    grad_conv_in = grad_extended[taps - 1 :].at[rows - taps + 1 :].add(returned_edge * edge_keep)
    grad_mixed = jnp.concatenate([grad_conv_in.astype(BF16), grad_gate_in], 1)
    grad_input_w = contract(norm_low, grad_mixed)
    sum_input = lax.psum_scatter(grad_input_w.astype(BF16), "dp", scatter_dimension=1, tiled=True)
    grad_norm_one = product_back(grad_mixed, w_input)
    grad_norm_gain = jnp.sum(grad_norm_one * hidden_in * norm_r, axis=0)
    scaled_one = norm_f * grad_norm_one
    grad_tokens = (
        grad_hidden
        + norm_r * scaled_one
        - hidden_in * (norm_r * norm_r * norm_r) * jnp.mean(hidden_in * scaled_one, axis=-1, keepdims=True)
    ).astype(BF16)
    (
        sum_kernel, sum_conv_b, sum_select, sum_step, sum_step_b, sum_decay, sum_skip, sum_norm, sum_ffn, sum_router,
    ) = scatter_small(
        [
            (grad_kernel, 1), (grad_conv_b, 0), (grad_select_w, 0), (grad_step_w, 1), (grad_step_bias, 0),
            (grad_decay_t.T, 0), (grad_skip[0], 0), (grad_norm_gain, 0), (grad_ffn_gain, 0), (grad_router, 0),
        ]
    )
    sum_input = lax.psum(sum_input, "expert").astype(F32)
    sum_output = lax.psum(sum_output, "expert").astype(F32)
    return (
        output, grad_tokens, sum_input, sum_kernel, sum_conv_b, sum_select, sum_step, sum_step_b,
        sum_decay, sum_skip, sum_output, sum_norm, sum_ffn, sum_router,
        sum_up.astype(F32)[None], sum_down.astype(F32)[None],
    )


def solution(mesh):
    placed = (
        P(("dp", "expert"), None),
        P(("dp", "expert"), None),
        P(("dp", "expert"), None),
        P(("dp", "expert")),
        P(None, "dp"),
        P(None, "dp"),
        P("dp"),
        P("dp", None),
        P(None, "dp"),
        P("dp"),
        P("dp", None),
        P("dp"),
        P("dp", None),
        P("dp"),
        P("dp"),
        P("dp", None),
        P("expert", None, "dp"),
        P("expert", "dp", None),
    )
    return jax.shard_map(
        body,
        mesh=mesh,
        in_specs=placed,
        out_specs=(
            P(("dp", "expert"), None),
            P(("dp", "expert"), None),
            P(None, "dp"),
            P(None, "dp"),
            P("dp"),
            P("dp", None),
            P(None, "dp"),
            P("dp"),
            P("dp", None),
            P("dp"),
            P("dp", None),
            P("dp"),
            P("dp"),
            P("dp", None),
            P("expert", None, "dp"),
            P("expert", "dp", None),
        ),
        check_vma=False,
    )
```

time: 5800 us -> 1440 us (0.25)
  other arithmetic: 3930 us -> 53 us
  local copies, waits for them, and re-layouts: 692 us -> 143 us
  Pallas kernels: 0 us -> 305 us
  blocking collectives: 221 us -> 48.2 us
    reduce_sum x991 -> x4, other arithmetic: 3130 us -> 2.2 us  [the longest x1 1.15 us: body(): grad_step_bias = jnp.sum(grad_pre_step.astype(F32), axis=0)]
    add_any x24 -> x0, other arithmetic: 548 us -> none  [run_scan(): lax.scan(jax.checkpoint(partial(scan_block, rate)), state, blocks)]
    pallas_call x0 -> x4, Pallas kernels: none -> 305 us  [the longest x1 172 us: backward_scan(): pl.pallas_call(backward_kernel, grid=(width // cb,), in_specs=[tok(s.shap...]
    slice x272 -> x20, local copies, waits for them, and re-layouts: 295 us -> 23.9 us  [the longest x10 13.2 us: scatter_small(): out.append(mine[at:at + count].reshape(shape))]
    squeeze x120 -> x0, local copies, waits for them, and re-layouts: 106 us -> none  [the longest x96 84.3 us: body(): lax.scan(partial(end_terms, rate, total), (zero_run, zero_state), (delta_...]
    all_to_all x1 -> x0, blocking collectives: 81.6 us -> none  [body(): lax.all_to_all(send_back[:-1].reshape(groups, capacity, model), 'expert',...]
    mul x312 -> x4, local copies, waits for them, and re-layouts: 81 us -> 3.54 us  [body(): valid[lag][:, None] * conv_f[at] * extended[at:at + rows]]
    dynamic_update_slice x96 -> x0, other arithmetic: 75.4 us -> none  [run_scan(): lax.scan(jax.checkpoint(partial(scan_block, rate)), state, blocks)]
where the time goes in v1:
time: 1440 us; the launch traced here: 1420 us
  waiting for transfers between devices  563 us (39%)
  Pallas kernels  305 us (21%)
  matrix products  270 us (19%)
  local copies, waits for them, and re-layouts  143 us (10%)
  other arithmetic  53 us (4%)
  blocking collectives  48.2 us (3%)
  starting transfers between devices  26.2 us (2%)
  between operations  16.9 us (1%)
    all_to_all x4, waiting for transfers between devices, exchange(): lax.all_to_all(x.reshape(groups, capacity, model), 'expert', split_axis=0...  200 us
    pallas_call x1, Pallas kernels, backward_scan(): pl.pallas_call(backward_kernel, grid=(width // cb,), in_specs=[tok(s.shap...  172 us
    dot_general x6, matrix products, product_back(): lax.dot_general(left, right, (((1,), (1,)), ((), ())), preferred_element_...  103 us
    psum x1, waiting for transfers between devices, scatter_small(): mine = lax.psum(mine, 'expert').astype(F32).reshape(-1)  88.6 us
    reduce_scatter x1, waiting for transfers between devices, body(): lax.psum_scatter(grad_input_w.astype(BF16), 'dp', scatter_dimension=1, ti...  86.1 us
    dot_general x8, matrix products, contract(): lax.dot_general(left, right, (((0,), (0,)), ((), ())), preferred_element_...  82.3 us
    dot_general x8, matrix products, dot(): return jnp.dot(a, b, preferred_element_type=F32)  75.8 us
    unnamed x12, waiting for transfers between devices  67.4 us
  transfers between devices with their start and end apart: 16, of which 10 were waited for; matrix products, arithmetic and copies ran while one was open for 22% of the time, Pallas kernels for 6%

profile of v1, /device:TPU:4, one launch (start us, length us, event | category | flops | bytes accessed | tf_op | source)
XLA Modules:
  0.0 1424.6 jit_solution(16740942578411128317)
XLA Ops:
  19.7 15.4 %all_gather.23 = bf16[8,456,128]{2,1,0:T(8,128)(2,1)S(1)} all-gather(bf16[1,456,128]{2,1,0:T(8,128)(2,1)S(1)} %pad_bitcast_fusion.1), channel_id=1, replica_groups=mesh['dp'=8,'expert'=4] {'dp'}, dimensions={0}, use_global_device_ids=true | all-gather | bytes 1050624 | tf_op jit(solution)/shard_map/all_gather | solution.py:380
  43.8 34.4 %all-gather.7.cloned.1.call-done = bf16[1152,4608]{0,1:T(8,128)(2,1)} async-done(((bf16[1152,576]{0,1:T(8,128)(2,1)}), bf16[1152,4608]{0,1:T(8,128)(2,1)}) %all-gather.7.cloned.1.call-update) | async-done | bytes 10616848 | tf_op jit(solution)/shard_map/all_gather | solution.py:418
  78.3 12.4 convolution_convert_fusion.4.z_ref
  137.6 37.7 %end_states.1 = (f32[16,2304]{1,0:T(8,128)}, f32[1,2304]{1,0:T(1,128)}) custom-call(bf16[768,72]{1,0:T(8,128)(2,1)} %copy.132.s_ref, bf16[72,2304]{1,0:T(8,128)(2,1)} %reshape.480.w_ref, bf16[1,2304]{1,0:T(2,128)(2,1)} %broadcast_in_dim_reshape.6.b_ref, f32[768,1]{1,0:T(8,128)} %broadcast_in_dim.118.st_ref, bf16[768,2304]{1,0:T(8,128)(2,1)} %copy-done.3, ...), custom_call_target="tpu_custom_call" | custom-call | flops 169869312 | bytes 3538944 | tf_op jit(solution)/shard_map/end_states/pallas_call | solution.py:251
  180.9 16.5 %all_gather.25 = bf16[4,2,16,2304]{3,2,1,0:T(8,128)(2,1)S(1)} all-gather(bf16[1,2,16,2304]{3,2,1,0:T(8,128)(2,1)S(1)} %pad_maximum_fusion.4), channel_id=1, replica_groups=mesh['dp'=8,'expert'=4] {'expert'}, dimensions={0}, use_global_device_ids=true | all-gather | bytes 737280 | tf_op jit(solution)/shard_map/all_gather | solution.py:347
  199.3 54.7 %forward_scan.1 = (bf16[768,2304]{1,0:T(8,128)(2,1)}, bf16[768,2304]{1,0:T(8,128)(2,1)}, f32[48,16,2304]{2,1,0:T(8,128)}) custom-call(bf16[768,72]{1,0:T(8,128)(2,1)} %copy.132.s_ref, bf16[72,2304]{1,0:T(8,128)(2,1)} %reshape.480.w_ref, bf16[1,2304]{1,0:T(2,128)(2,1)} %broadcast_in_dim_reshape.6.b_ref, f32[768,1]{1,0:T(8,128)} %broadcast_in_dim.118.st_ref, ...), custom_call_target="tpu_custom_call" | custom-call | flops 254803968 | bytes 21233664 | tf_op jit(solution)/shard_map/forward_scan/pallas_call | solution.py:269
  254.0 8.9 multiply_reduce_fusion.6
  287.1 61.8 %all-to-all-done = bf16[4,384,1152]{2,1,0:T(8,128)(2,1)} async-done(((bf16[4,384,1152]{2,1,0:T(8,128)(2,1)}), bf16[4,384,1152]{2,1,0:T(8,128)(2,1)}, u32[]{:S(2)}, u32[]{:S(2)}) %all-to-all-start) | async-done | bytes 3538976 | tf_op jit(solution)/shard_map/all_to_all | solution.py:501
  354.1 18.1 %fusion.13 = f32[1536,3072]{1,0:T(8,128)} fusion(bf16[1536,1152]{1,0:T(8,128)(2,1)} %bitcast.15, bf16[1,1152,3072]{2,1,0:T(8,128)(2,1)} %all-gather.11.cloned.1.call-done), kind=kOutput, calls=%fused_computation.31 | convolution fusion | flops 10871635968 | bytes 29491200 | tf_op jit(solution)/shard_map/dot_general | solution.py:32
  372.2 23.0 %convolution_convert_fusion.7 = bf16[1536,1152]{1,0:T(8,128)(2,1)} fusion(bf16[1,3072,1152]{2,1,0:T(8,128)(2,1)} %all-gather.13.cloned.1.call-done, f32[1536,3072]{1,0:T(8,128)} %fusion.13), kind=kOutput, calls=%fused_computation.23 | convolution fusion | flops 10915872768 | bytes 29491200 | tf_op jit(solution)/shard_map/dot_general | solution.py:32
  395.2 37.4 %all-to-all-done.2 = bf16[4,384,1152]{2,1,0:T(8,128)(2,1)} async-done(((bf16[4,384,1152]{2,1,0:T(8,128)(2,1)}), bf16[4,384,1152]{2,1,0:T(8,128)(2,1)}, u32[]{:S(2)}, u32[]{:S(2)}) %all-to-all-start.2) | async-done | bytes 3538976 | tf_op jit(solution)/shard_map/all_to_all | solution.py:501
  437.6 27.7 %fusion.6 = bf16[1536,3072]{1,0:T(8,128)(2,1)S(1)} fusion(f32[1536,3072]{1,0:T(8,128)} %fusion.13, bf16[1536,1152]{1,0:T(8,128)(2,1)} %bitcast.21, bf16[1,3072,1152]{2,1,0:T(8,128)(2,1)} %all-gather.13.cloned.1.call-done), kind=kOutput, calls=%fused_computation.9 | convolution fusion | flops 10966007808 | bytes 38928384 | tf_op jit(solution)/shard_map/dot_general | solution.py:358
  468.9 16.8 %convolution_convert_fusion.5 = bf16[1536,1152]{1,0:T(8,128)(2,1)} fusion(bf16[1536,3072]{1,0:T(8,128)(2,1)S(1)} %fusion.6, bf16[1,1152,3072]{2,1,0:T(8,128)(2,1)} %all-gather.11.cloned.1.call-done), kind=kOutput, calls=%fused_computation.21 | convolution fusion | flops 10873405440 | bytes 20054016 | tf_op jit(solution)/shard_map/dot_general | solution.py:358
  485.8 30.5 %all-to-all-done.1 = bf16[4,384,1152]{2,1,0:T(8,128)(2,1)} async-done(((bf16[4,384,1152]{2,1,0:T(8,128)(2,1)}), bf16[4,384,1152]{2,1,0:T(8,128)(2,1)}, u32[]{:S(2)}, u32[]{:S(2)}) %all-to-all-start.1) | async-done | bytes 3538976 | tf_op jit(solution)/shard_map/all_to_all | solution.py:501
  529.8 69.9 %all-to-all-done.3 = bf16[4,384,1152]{2,1,0:T(8,128)(2,1)} async-done(((bf16[4,384,1152]{2,1,0:T(8,128)(2,1)}), bf16[4,384,1152]{2,1,0:T(8,128)(2,1)}, u32[]{:S(2)}, u32[]{:S(2)}) %all-to-all-start.3) | async-done | bytes 3538976 | tf_op jit(solution)/shard_map/all_to_all | solution.py:501
  625.2 40.7 %start_grads.1 = f32[16,2304]{1,0:T(8,128)} custom-call(bf16[768,72]{1,0:T(8,128)(2,1)} %copy.132.s_ref, bf16[72,2304]{1,0:T(8,128)(2,1)} %reshape.480.w_ref, bf16[1,2304]{1,0:T(2,128)(2,1)} %broadcast_in_dim_reshape.6.b_ref, f32[768,1]{1,0:T(8,128)} %broadcast_in_dim.118.st_ref, f32[768,2304]{1,0:T(8,128)} %fusion.51.dg_ref, bf16[768,4608]{1,0:T(8,128)(2,1)} %copy-done.8, ...), custom_call_target="tpu_custom_call" | custom-call | flops 169869312 | bytes 10616832 | tf_op jit(solution)/shard_map/start_grads/pallas_call | solution.py:287
  666.9 16.3 %all_gather.29 = bf16[4,2,16,2304]{3,2,1,0:T(8,128)(2,1)S(1)} all-gather(bf16[1,2,16,2304]{3,2,1,0:T(8,128)(2,1)S(1)} %pad_maximum_fusion.3), channel_id=1, replica_groups=mesh['dp'=8,'expert'=4] {'expert'}, dimensions={0}, use_global_device_ids=true | all-gather | bytes 737280 | tf_op jit(solution)/shard_map/all_gather | solution.py:347
  683.9 172.3 %backward_scan.1 = (bf16[768,2304]{1,0:T(8,128)(2,1)}, bf16[768,2304]{1,0:T(8,128)(2,1)}, f32[768,2304]{1,0:T(8,128)}, f32[16,2304]{1,0:T(8,128)}, f32[1,2304]{1,0:T(1,128)}, /*index=5*/bf16[768,128]{1,0:T(8,128)(2,1)}) custom-call(bf16[768,72]{1,0:T(8,128)(2,1)} %copy.132.s_ref, bf16[72,2304]{1,0:T(8,128)(2,1)} %reshape.480.w_ref, ...), custom_call_target="tpu_custom_call" | custom-call | flops 707788800 | bytes 42467328 | tf_op jit(solution)/shard_map/backward_scan/pallas_call | solution.py:305
  867.9 29.7 %multiply_reduce_fusion.3 = (bf16[2304]{0:T(1024)(128)(2,1)}, bf16[2304]{0:T(1024)(128)(2,1)}, bf16[2304]{0:T(1024)(128)(2,1)}, bf16[2304]{0:T(1024)(128)(2,1)},...) fusion(f32[771,2304]{1,0:T(8,128)} %copy-done, ...), kind=kOutput, calls=%fused_computation.36 | convolution fusion | flops 412594944 | bytes 71486976 | tf_op jit(solution)/shard_map/dot_general | solution.py:358
  902.7 7.9 pad_add_fusion
  960.0 17.0 %fusion.29 = (bf16[1152]{0:T(1024)(128)(2,1)}, f32[768]{0:T(1024)}, f32[768,1152]{1,0:T(8,128)}) fusion(bf16[768,1152]{1,0:T(8,128)(2,1)} %param.20, f32[768]{0:T(1024)S(1)} %copy-done.54, f32[1152]{0:T(1024)} %copy-done.50, bf16[1152,4608]{0,1:T(8,128)(2,1)} %all-gather.7.cloned.1.call-done, bf16[768,2304]{1,0:T(8,128)(2,1)} %get-tuple-element.47, ...), kind=kOutput, calls=%fused_computation.65 | convolution fusion | flops 8174073856 | bytes 23016192 | tf_op jit(solution)/shard_map/dot_general | solution.py:358
  984.3 9.5 convolution_convert_fusion.2
  994.5 15.3 %convolution_convert_fusion = bf16[1152,4608]{0,1:T(8,128)(2,1)} fusion(bf16[768,2304]{1,0:T(8,128)(2,1)} %get-tuple-element.47, bf16[768,2304]{1,0:T(8,128)(2,1)} %copy-done.12, bf16[768,1152]{1,0:T(8,128)(2,1)} %param.20, f32[1152]{0:T(1024)S(1)} %copy-done.51, f32[768]{0:T(1024)S(1)} %copy-done.54), kind=kOutput, calls=%fused_computation.2 | convolution fusion | flops 8176730112 | bytes 19471872 | tf_op jit(solution)/shard_map/dot_general | solution.py:362
  1009.8 16.8 %convolution_convert_fusion.3 = bf16[1152,3072]{1,0:T(8,128)(2,1)} fusion(bf16[1536,1152]{1,0:T(8,128)(2,1)} %bitcast.15, bf16[1536,3072]{1,0:T(8,128)(2,1)} %copy-done.66), kind=kOutput, calls=%fused_computation.13 | convolution fusion | flops 10875174912 | bytes 20054016 | tf_op jit(solution)/shard_map/dot_general | solution.py:362
  1026.6 10.6 copy.130
  1037.6 21.8 %convolution_convert_fusion.1 = bf16[3072,1152]{1,0:T(8,128)(2,1)} fusion(bf16[1536,1152]{1,0:T(8,128)(2,1)} %bitcast.21, f32[1536,3072]{1,0:T(8,128)} %fusion.13), kind=kOutput, calls=%fused_computation.11 | convolution fusion | flops 10917642240 | bytes 29491200 | tf_op jit(solution)/shard_map/dot_general | solution.py:362
  1059.5 20.5 %reduce-scatter.12.cloned.1.call-done = bf16[288,1152]{1,0:T(8,128)(2,1)} async-done(((bf16[2304,1152]{1,0:T(8,128)(2,1)}), bf16[288,1152]{1,0:T(8,128)(2,1)}) %reduce-scatter.12.cloned.1.call-update) | async-done | bytes 663568 | tf_op jit(solution)/shard_map/reduce_scatter | solution.py:540
  1079.9 86.1 %reduce-scatter.10.cloned.1.call-done = bf16[1152,576]{0,1:T(8,128)(2,1)} async-done(((bf16[1152,4608]{0,1:T(8,128)(2,1)}), bf16[1152,576]{0,1:T(8,128)(2,1)}) %reduce-scatter.10.cloned.1.call-update) | async-done | bytes 1327120 | tf_op jit(solution)/shard_map/reduce_scatter | solution.py:567
  1170.8 64.7 %reduce-scatter.16.cloned.1.call-done = bf16[384,1152]{1,0:T(8,128)(2,1)} async-done(((bf16[3072,1152]{1,0:T(8,128)(2,1)}), bf16[384,1152]{1,0:T(8,128)(2,1)}) %reduce-scatter.16.cloned.1.call-update) | async-done | bytes 884752
  1238.6 66.0 %reduce-scatter.14.cloned.1.call-done = bf16[384,1152]{1,0:T(8,128)(2,1)} async-done(((bf16[3072,1152]{1,0:T(8,128)(2,1)}), bf16[384,1152]{1,0:T(8,128)(2,1)}) %reduce-scatter.14.cloned.1.call-update) | async-done | bytes 884752 | tf_op jit(solution)/shard_map/reduce_scatter | solution.py:516
  1307.0 88.6 %all-reduce.11.cloned.1.call-done = (bf16[1,456,128]{2,1,0:T(8,128)(2,1)}, bf16[1152,576]{0,1:T(8,128)(2,1)}, bf16[288,1152]{1,0:T(8,128)(2,1)}) async-done(((bf16[1,456,128]{2,1,0:T(8,128)(2,1)}, bf16[1152,576]{0,1:T(8,128)(2,1)}, bf16[288,1152]{1,0:T(8,128)(2,1)}), (bf16[1,456,128]{2,1,0:T(8,128)(2,1)}, bf16[1152,576]{0,1:T(8,128)(2,1)}, bf16[288,1152]{1,0:T(8,128)(2,1)})) %all-reduce.11.cloned.1.call-update) | async-done | bytes 2107408 | tf_op jit(solution)/shard_map/psum | solution.py:403
  1400.1 9.6 slice.266
  (324 shorter events, 249.2 us)
Async XLA Ops:
  7.2 29.1 %copy-start.49 = (s32[768]{0:T(1024)S(1)}, s32[768]{0:T(1024)}, u32[]{:S(2)}) copy-start(s32[768]{0:T(1024)} %param.23) | copy-start | bytes 9220
  7.2 29.7 %copy-start.65 = (s32[768,1]{0,1:T(1,128)S(1)}, s32[768,1]{0,1:T(1,128)}, u32[]{:S(2)}) copy-start(s32[768,1]{0,1:T(1,128)} %param.22) | copy-start | bytes 9220
  7.2 30.7 %copy-start.9 = (bf16[768,1152]{1,0:T(8,128)(2,1)S(1)}, bf16[768,1152]{1,0:T(8,128)(2,1)}, u32[]{:S(2)}) copy-start(bf16[768,1152]{1,0:T(8,128)(2,1)} %param.20) | copy-start | bytes 5308420
  7.2 71.1 %all-gather.7.cloned.1.call-start = ((), (), s32[]{:S(2)}) async-start(), calls=%async_computation.9 | async-start | bytes 11943936 | tf_op jit(solution)/shard_map/all_gather | solution.py:418
  7.9 246.0 %all-gather.9.cloned.1.call-start = ((), (), s32[]{:S(2)}) async-start(), calls=%async_computation.10 | async-start | bytes 5971968 | tf_op jit(solution)/shard_map/all_gather | solution.py:427
  8.7 345.4 %all-gather.11.cloned.1.call-start = ((), (), s32[]{:S(2)}) async-start(), calls=%async_computation.14 | async-start | bytes 7962624 | tf_op jit(solution)/shard_map/all_gather | solution.py:428
  9.4 362.8 %all-gather.13.cloned.1.call-start = ((), (), s32[]{:S(2)}) async-start(), calls=%async_computation.15 | async-start | bytes 7962624 | tf_op jit(solution)/shard_map/all_gather | solution.py:429
  36.3 82.6 %copy-start.31 = (f32[768]{0:T(1024)}, f32[768]{0:T(1024)S(1)}, u32[]{:S(2)}) copy-start(f32[768]{0:T(1024)S(1)} %broadcast_subtract_fusion) | copy-start | bytes 9220
  38.9 51.8 %copy-start.53 = (f32[768]{0:T(1024)}, f32[768]{0:T(1024)S(1)}, u32[]{:S(2)}) copy-start(f32[768]{0:T(1024)S(1)} %get-tuple-element.155) | copy-start | bytes 9220
  39.6 51.2 %copy-start.50 = (f32[1152]{0:T(1024)}, f32[1152]{0:T(1024)S(1)}, u32[]{:S(2)}) copy-start(f32[1152]{0:T(1024)S(1)} %reshape.499) | copy-start | bytes 13828
  40.4 50.3 %copy-start.22 = (f32[2304,16]{0,1:T(8,128)}, f32[2304,16]{0,1:T(8,128)S(1)}, u32[]{:S(2)}) copy-start(f32[2304,16]{0,1:T(8,128)S(1)} %copy.111) | copy-start | bytes 442372
  43.2 47.6 %copy-start.63 = (f32[3]{0:T(128)}, f32[3]{0:T(128)S(1)}, u32[]{:S(2)}) copy-start(f32[3]{0:T(128)S(1)} %pad_maximum_fusion.8) | copy-start | bytes 40
  94.3 23.0 %collective-permute-start = (bf16[3,2304]{1,0:T(4,128)(2,1)}, bf16[3,2304]{1,0:T(4,128)(2,1)}, u32[]{:S(2)}, u32[]{:S(2)}) collective-permute-start(bf16[3,2304]{1,0:T(4,128)(2,1)} %multiply_convert_fusion.2), channel_id=1, source_target_pairs={{0,1},{1,2},{2,3},{4,5},{5,6},{6,7},{8,9},{9,10},{10,11},{12,13},{... | collective-permute-start | bytes 41480 | tf_op jit(solution)/shard_map/ppermute | solution.py:342
  137.6 59.9 %copy-start.57 = (pred[16,256]{1,0:T(8,128)(4,1)S(1)}, pred[16,256]{1,0:T(8,128)(4,1)}, u32[]{:S(2)}) copy-start(pred[16,256]{1,0:T(8,128)(4,1)} %get-tuple-element.163) | copy-start | bytes 12292
  178.3 75.6 %copy-start.14 = (f32[768,16]{1,0:T(8,128)}, f32[768,16]{1,0:T(8,128)S(1)}, u32[]{:S(2)}) copy-start(f32[768,16]{1,0:T(8,128)S(1)} %copy.113) | copy-start | bytes 147460
  268.7 80.2 %all-to-all-start = ((bf16[4,384,1152]{2,1,0:T(8,128)(2,1)}), bf16[4,384,1152]{2,1,0:T(8,128)(2,1)}, u32[]{:S(2)}, u32[]{:S(2)}) async-start(bf16[4,384,1152]{2,1,0:T(8,128)(2,1)} %bitcast.160), calls=%async_computation | async-start | bytes 7077888 | tf_op jit(solution)/shard_map/all_to_all | solution.py:501
  348.9 83.8 %all-to-all-start.2 = ((bf16[4,384,1152]{2,1,0:T(8,128)(2,1)}), bf16[4,384,1152]{2,1,0:T(8,128)(2,1)}, u32[]{:S(2)}, u32[]{:S(2)}) async-start(bf16[4,384,1152]{2,1,0:T(8,128)(2,1)} %bitcast.161), calls=%async_computation.2 | async-start | bytes 7077888 | tf_op jit(solution)/shard_map/all_to_all | solution.py:501
  432.7 83.6 %all-to-all-start.1 = ((bf16[4,384,1152]{2,1,0:T(8,128)(2,1)}), bf16[4,384,1152]{2,1,0:T(8,128)(2,1)}, u32[]{:S(2)}, u32[]{:S(2)}) async-start(bf16[4,384,1152]{2,1,0:T(8,128)(2,1)} %bitcast.162), calls=%async_computation.1 | async-start | bytes 7077888 | tf_op jit(solution)/shard_map/all_to_all | solution.py:501
  516.3 83.4 %all-to-all-start.3 = ((bf16[4,384,1152]{2,1,0:T(8,128)(2,1)}), bf16[4,384,1152]{2,1,0:T(8,128)(2,1)}, u32[]{:S(2)}, u32[]{:S(2)}) async-start(bf16[4,384,1152]{2,1,0:T(8,128)(2,1)} %bitcast.159), calls=%async_computation.3 | async-start | bytes 7077888 | tf_op jit(solution)/shard_map/all_to_all | solution.py:501
  521.0 538.5 %reduce-scatter.18.cloned.1.call-start = ((), (), s32[]{:S(2)}) async-start(), calls=%async_computation.17 | async-start | bytes 1050624
  625.2 41.6 %copy-start.26 = (bf16[1,1,16,2304]{3,2,1,0:T(8,128)(2,1)S(1)}, bf16[1,1,16,2304]{3,2,1,0:T(8,128)(2,1)}, u32[]{:S(2)}) copy-start(bf16[1,1,16,2304]{3,2,1,0:T(8,128)(2,1)} %copy-done.25) | copy-start | bytes 221188
  683.9 172.3 %copy-start.24 = (bf16[72,2304]{1,0:T(8,128)(2,1)S(1)}, bf16[72,2304]{1,0:T(8,128)(2,1)}, u32[]{:S(2)}) copy-start(bf16[72,2304]{1,0:T(8,128)(2,1)} %reshape.480.w_ref) | copy-start | bytes 995332
  902.7 23.1 %copy-start.56 = (bf16[1152]{0:T(1024)(128)(2,1)S(1)}, bf16[1152]{0:T(1024)(128)(2,1)}, u32[]{:S(2)}) copy-start(bf16[1152]{0:T(1024)(128)(2,1)} %get-tuple-element.118) | copy-start | bytes 6916
  902.7 25.2 %copy-start.5 = (bf16[768,2304]{1,0:T(8,128)(2,1)S(1)}, bf16[768,2304]{1,0:T(8,128)(2,1)}, u32[]{:S(2)}) copy-start(bf16[768,2304]{1,0:T(8,128)(2,1)} %get-tuple-element.45) | copy-start | bytes 10616836
  919.6 36.1 %collective-permute-start.1 = (f32[3,2304]{1,0:T(4,128)}, f32[3,2304]{1,0:T(4,128)}, u32[]{:S(2)}, u32[]{:S(2)}) collective-permute-start(f32[3,2304]{1,0:T(4,128)} %pad_add_fusion.1), channel_id=1, source_target_pairs={{1,0},{2,1},{3,2},{5,4},{6,5},{7,6},{9,8},{10,9},{11,10},{13,12},{... | collective-permute-start | bytes 82952 | tf_op jit(solution)/shard_map/ppermute | solution.py:342
  960.0 24.3 %copy-start.7 = (f32[768,1152]{1,0:T(8,128)S(1)}, f32[768,1152]{1,0:T(8,128)}, u32[]{:S(2)}) copy-start(f32[768,1152]{1,0:T(8,128)} %copy-done.6) | copy-start | bytes 10616836
  984.2 95.7 %reduce-scatter.12.cloned.1.call-start = ((), (), s32[]{:S(2)}) async-start(), calls=%async_computation.12 | async-start | bytes 5971968 | tf_op jit(solution)/shard_map/reduce_scatter | solution.py:540
  993.8 172.2 %reduce-scatter.10.cloned.1.call-start = ((), (), s32[]{:S(2)}) async-start(), calls=%async_computation.11 | async-start | bytes 11943936 | tf_op jit(solution)/shard_map/reduce_scatter | solution.py:567
  1009.8 225.7 %reduce-scatter.16.cloned.1.call-start = ((), (), s32[]{:S(2)}) async-start(), calls=%async_computation.16 | async-start | bytes 7962624
  1037.3 267.3 %reduce-scatter.14.cloned.1.call-start = ((), (), s32[]{:S(2)}) async-start(), calls=%async_computation.13 | async-start | bytes 7962624 | tf_op jit(solution)/shard_map/reduce_scatter | solution.py:516
  1059.4 107.4 %copy-start.52 = (f32[768]{0:T(1024)S(1)}, f32[768]{0:T(1024)}, u32[]{:S(2)}) copy-start(f32[768]{0:T(1024)} %get-tuple-element.154) | copy-start | bytes 9220
  1059.4 336.2 %all-reduce.11.cloned.1.call-start = ((), (), s32[]{:S(2)}) async-start(), calls=%async_computation.18 | async-start | bytes 4214784 | tf_op jit(solution)/shard_map/psum | solution.py:403
  (55 other events, 283.6 us)
Sparse Core Ops, SparseCore 0:
  9.9 68.2 all-gather.6
  80.1 41.6 all-gather.8
  123.7 49.1 all-gather.10
  174.7 49.8 all-gather.12
  984.3 35.3 reduce-scatter.17
  1023.0 56.8 reduce-scatter.11
  1083.9 82.1 reduce-scatter.9
  1169.9 65.5 reduce-scatter.15
  1239.0 65.4 reduce-scatter.13
  1307.1 88.3 all-reduce.10

commit v2 on v1

v2 whole, which is shorter than its diff:
```python
from functools import partial

import jax
import jax.numpy as jnp
from jax import lax
from jax.experimental import pallas as pl
from jax.experimental.pallas import tpu as pltpu
from jax.sharding import PartitionSpec as P

TC = 16
ROWS = 256
CONV_ROWS = 128
PAD = 16
UNROLL = 8
FAR = 1e4
LOG2E = 1.4426950408889634
LN2 = 0.6931471805599453
F32 = jnp.float32
BF16 = jnp.bfloat16


def tiled(x, n):
    return jnp.concatenate([x] * n, axis=1) if n > 1 else x


def folded(x):
    n = x.shape[1] // 128
    out = x[:, :128]
    for i in range(1, n):
        out = out + x[:, i * 128 : (i + 1) * 128]
    return out


def dot(a, b):
    return jnp.dot(a, b, preferred_element_type=F32)


def prepare(s_ref, w_ref, b_ref, st_ref, u_ref, dk_ref, dv_ref, pre_ref=None):
    size = min(s_ref.shape[0], ROWS)

    def block(i, carry):
        r = pl.ds(pl.multiple_of(i * size, size), size)
        pre = dot(s_ref[r, :], w_ref[...]) + b_ref[...].astype(F32)
        delta = jnp.maximum(pre, 0.0) + jnp.log1p(jnp.exp(-jnp.abs(pre)))
        dk = jnp.where(st_ref[r, :] > 0.0, FAR, delta)
        dk_ref[r, :] = dk
        if u_ref is not None:
            dv_ref[r, :] = delta * u_ref[r, :].astype(F32)
        if pre_ref is not None:
            pre_ref[r, :] = pre
        return carry + jnp.sum(dk, axis=0, keepdims=True)

    return lax.fori_loop(
        0, s_ref.shape[0] // size, block, jnp.zeros((1, w_ref.shape[1]), F32)
    )


def end_kernel(s_ref, w_ref, b_ref, st_ref, u_ref, a_ref, bb_ref, low_ref, dk_ref, dv_ref, out_ref):
    reps = w_ref.shape[1] // 128
    states = a_ref.shape[0]
    first = pl.program_id(1) == 0
    total = prepare(s_ref, w_ref, b_ref, st_ref, u_ref, dk_ref, dv_ref)
    a = a_ref[...]

    @pl.when(first)
    def _():
        out_ref[...] = jnp.zeros_like(out_ref)

    def chunk(c, h):
        t0 = pl.multiple_of(c * TC, TC)
        for i in range(TC):
            f = jnp.exp2(a * dk_ref[pl.ds(t0 + i, 1), :])
            h = f * h + dv_ref[pl.ds(t0 + i, 1), :] * tiled(bb_ref[t0 + i], reps)
        return h

    out_ref[:states, :] = lax.fori_loop(0, s_ref.shape[0] // TC, chunk, out_ref[:states, :])
    out_ref[states : states + 1, :] += total

    @pl.when(pl.program_id(1) == pl.num_programs(1) - 1)
    def _():
        low_ref[:states, :] = out_ref[:states, :].astype(BF16)
        sums = out_ref[states : states + 1, :]
        high = sums.astype(BF16).astype(F32)
        row = lax.broadcasted_iota(jnp.int32, (states, sums.shape[1]), 0)
        both = jnp.where(row == 0, high, jnp.where(row == 1, sums - high, 0.0))
        low_ref[states:, :] = both.astype(BF16)


def forward_kernel(
    s_ref, w_ref, b_ref, st_ref, u_ref, z_ref, a_ref, skip_ref, bb_ref, cm_ref, h0_ref,
    g_ref, y_ref, hs_ref, ck_ref, dk_ref, dv_ref, ys_ref, h_ref,
):
    reps = w_ref.shape[1] // 128
    states = a_ref.shape[0]
    chunks = s_ref.shape[0] // TC
    prepare(s_ref, w_ref, b_ref, st_ref, u_ref, dk_ref, dv_ref)
    a = a_ref[...]

    @pl.when(pl.program_id(1) == 0)
    def _():
        h_ref[...] = h0_ref[...]

    def scan(c, h):
        t0 = pl.multiple_of(c * TC, TC)
        r0 = pl.multiple_of(c * TC * states, TC * states)
        ck_ref[c] = h.astype(BF16)
        for i in range(TC):
            f = jnp.exp2(a * dk_ref[pl.ds(t0 + i, 1), :])
            h = f * h + dv_ref[pl.ds(t0 + i, 1), :] * tiled(bb_ref[t0 + i], reps)
            hs_ref[pl.ds(r0 + i * states, states), :] = h.astype(BF16)
        return h

    def emit(c):
        t0 = pl.multiple_of(c * TC, TC)
        r0 = pl.multiple_of(c * TC * states, TC * states)
        ys_ref[pl.ds(t0, TC), :] = dot(cm_ref[c], hs_ref[pl.ds(r0, TC * states), :])

    def group(j, h):
        for m in range(UNROLL):
            h = scan(UNROLL * j + m, h)
            emit(UNROLL * j + m)
        return h

    h_ref[...] = lax.fori_loop(0, chunks // UNROLL, group, h_ref[...])

    size = min(s_ref.shape[0], ROWS)

    def finish(i, carry):
        r = pl.ds(pl.multiple_of(i * size, size), size)
        y = ys_ref[r, :] + skip_ref[...].astype(F32) * u_ref[r, :].astype(F32)
        z = z_ref[r, :].astype(F32)
        y_ref[r, :] = y.astype(BF16)
        g_ref[r, :] = (y * (z / (1.0 + jnp.exp(-z)))).astype(BF16)
        return carry

    lax.fori_loop(0, s_ref.shape[0] // size, finish, 0)


def start_kernel(s_ref, w_ref, b_ref, st_ref, dy_ref, a_ref, cb_ref, low_ref, dk_ref, out_ref):
    reps = w_ref.shape[1] // 128
    chunks = s_ref.shape[0] // TC
    prepare(s_ref, w_ref, b_ref, st_ref, None, dk_ref, None)
    a = a_ref[...]

    @pl.when(pl.program_id(1) == 0)
    def _():
        out_ref[...] = jnp.zeros_like(out_ref)

    def chunk(j, grad):
        t0 = pl.multiple_of((chunks - 1 - j) * TC, TC)
        for i in range(TC - 1, -1, -1):
            f = jnp.exp2(a * dk_ref[pl.ds(t0 + i, 1), :])
            lam = grad + dy_ref[pl.ds(t0 + i, 1), :] * tiled(cb_ref[t0 + i], reps)
            grad = f * lam
        return grad

    out_ref[...] = lax.fori_loop(0, chunks, chunk, out_ref[...])

    @pl.when(pl.program_id(1) == pl.num_programs(1) - 1)
    def _():
        low_ref[...] = out_ref[...].astype(BF16)


def backward_kernel(
    s_ref, w_ref, b_ref, st_ref, u_ref, dy_ref, a_ref, skip_ref, cb_ref, bm_ref, om_ref, hs_ref, ck_ref, g0_ref,
    ds_ref, du_ref, da_ref, dskip_ref, db_ref, dc_ref,
    pre_ref, dk_ref, dv_ref, q_ref, p_ref, lb0, lb1, wb0, wb1, grad_ref, accb_ref, accc_ref,
):
    step, seg = pl.program_id(0), pl.program_id(1)
    last = pl.num_programs(1) - 1 - seg
    reps = w_ref.shape[1] // 128
    states = a_ref.shape[0]
    rows = s_ref.shape[0]
    chunks = rows // TC
    prepare(s_ref, w_ref, b_ref, st_ref, u_ref, dk_ref, dv_ref, pre_ref)
    token0 = pl.multiple_of(last * rows, rows)

    @pl.when((step == 0) & (seg == 0))
    def _():
        accb_ref[...] = jnp.zeros_like(accb_ref)
        accc_ref[...] = jnp.zeros_like(accc_ref)

    @pl.when(seg == 0)
    def _():
        grad_ref[...] = g0_ref[...]
        da_ref[...] = jnp.zeros_like(da_ref)
        dskip_ref[...] = jnp.zeros_like(dskip_ref)

    a = a_ref[...]
    a_low = a.astype(BF16)

    def scan(c, grad, lb, wb):
        t0 = pl.multiple_of(c * TC, TC)
        r0 = pl.multiple_of(c * TC * states, TC * states)
        da, four = None, None
        for i in range(TC - 1, -1, -1):
            d = dk_ref[pl.ds(t0 + i, 1), :]
            f = jnp.exp2(a * d)
            lam = grad + dy_ref[pl.ds(t0 + i, 1), :] * tiled(cb_ref[t0 + i], reps)
            grad = f * lam
            lb[pl.ds(i * states, states), :] = lam.astype(BF16)
            h = ck_ref[c] if i == 0 else hs_ref[pl.ds(r0 + (i - 1) * states, states), :]
            w = grad.astype(BF16) * h
            wb[pl.ds(i * states, states), :] = w * a_low
            wd = w * jnp.broadcast_to(d, w.shape).astype(BF16)
            four = wd if four is None else four + wd
            if i % 4 == 0:
                da = four.astype(F32) if da is None else da + four.astype(F32)
                four = None
            accb_ref[token0 + t0 + i] += folded(lam * dv_ref[pl.ds(t0 + i, 1), :])
        da_ref[...] += da
        return grad

    def emit(c, lb, wb):
        t0 = pl.multiple_of(c * TC, TC)
        r0 = pl.multiple_of(c * TC * states, TC * states)
        q_ref[pl.ds(t0, TC), :] = dot(bm_ref[c], lb[...])
        p_ref[pl.ds(t0, TC), :] = dot(om_ref[...], wb[...])
        accc_ref[last * chunks + c] += lax.dot_general(
            dy_ref[pl.ds(t0, TC), :].astype(BF16), hs_ref[pl.ds(r0, TC * states), :],
            (((1,), (1,)), ((), ())), preferred_element_type=F32,
        )

    def pair(j, grad):
        c = chunks - 1 - 2 * j
        grad = scan(c, grad, lb0, wb0)
        emit(c, lb0, wb0)
        grad = scan(c - 1, grad, lb1, wb1)
        emit(c - 1, lb1, wb1)
        return grad

    grad_ref[...] = lax.fori_loop(0, chunks // 2, pair, grad_ref[...])

    @pl.when(last == 0)
    def _():
        da_ref[...] = da_ref[...] * a * LN2

    size = min(s_ref.shape[0], ROWS)

    def finish(i, carry):
        r = pl.ds(pl.multiple_of(i * size, size), size)
        u = u_ref[r, :].astype(F32)
        q = q_ref[r, :]
        dy = dy_ref[r, :]
        pre = pre_ref[r, :]
        delta = jnp.maximum(pre, 0.0) + jnp.log1p(jnp.exp(-jnp.abs(pre)))
        dd = p_ref[r, :] * LN2 + u * q
        ds_ref[r, :] = (dd / (1.0 + jnp.exp(-pre))).astype(BF16)
        du_ref[r, :] = delta * q + dy * skip_ref[...].astype(F32)
        return carry + jnp.sum(dy * u, axis=0, keepdims=True)

    dskip_ref[...] += lax.fori_loop(0, rows // size, finish, jnp.zeros(dskip_ref.shape, F32))

    @pl.when((step == pl.num_programs(0) - 1) & (last == 0))
    def _():
        ones = jnp.ones((128, 128), BF16)
        row = lax.broadcasted_iota(jnp.int32, (TC * states, 128), 0) % states
        lane = lax.broadcasted_iota(jnp.int32, (TC * states, 128), 1)

        def gather(c, carry):
            t0 = pl.multiple_of(c * TC, TC)
            b = dot(accb_ref[pl.ds(t0, TC)].reshape(TC * states, 128).astype(BF16), ones)
            db_ref[pl.ds(t0, TC), :] = dot(om_ref[...], jnp.where(lane == row, b, 0.0).astype(BF16)).astype(BF16)
            own = om_ref[...].astype(F32) * accc_ref[c]
            dc_ref[c] = jnp.broadcast_to(jnp.sum(own, axis=0, keepdims=True), dc_ref.shape[1:])
            return carry

        lax.fori_loop(0, accc_ref.shape[0], gather, 0)


def conv_kernel_back(xs_ref, du_ref, slope_ref, dp_ref, sel_ref, k_ref, ok_ref, dxs_ref, dk_ref, db_ref, dc_ref):
    taps = k_ref.shape[0]
    rows = du_ref.shape[0]
    k = k_ref[...].astype(F32)
    dc_ref[:PAD, :] = jnp.zeros((PAD, dc_ref.shape[1]), F32)
    dc_ref[pl.ds(rows + PAD, PAD), :] = jnp.zeros((PAD, dc_ref.shape[1]), F32)

    def first(i, carry):
        t0 = pl.multiple_of(i * CONV_ROWS, CONV_ROWS)
        at = pl.ds(t0, CONV_ROWS)
        du = du_ref[at, :] + dot(dp_ref[at, :], sel_ref[...])
        dc = du * slope_ref[at, :].astype(F32)
        dc_ref[pl.ds(t0 + PAD, CONV_ROWS), :] = dc
        slab = xs_ref[pl.ds(t0, CONV_ROWS + PAD), :].astype(F32)
        sums = [jnp.sum(dc, axis=0, keepdims=True)]
        for lag in range(taps):
            x = slab[PAD - lag : PAD - lag + CONV_ROWS]
            part = dc * x
            if lag:
                part = part * ok_ref[pl.ds(t0 + PAD, CONV_ROWS), lag : lag + 1]
            sums.append(jnp.sum(part, axis=0, keepdims=True))
        return tuple(a + b for a, b in zip(carry, sums))

    size = max(n for n in range(PAD, 129, PAD) if (rows + PAD) % n == 0)
    zero = jnp.zeros((1, k.shape[1]), F32)
    sums = lax.fori_loop(0, rows // CONV_ROWS, first, (zero,) * (taps + 1))
    db_ref[...] = sums[0]
    for lag in range(taps):
        dk_ref[taps - 1 - lag : taps - lag, :] = sums[1 + lag]

    def second(i, carry):
        r0 = pl.multiple_of(i * size, PAD)
        slab = dc_ref[pl.ds(r0, size + PAD), :]
        ok = ok_ref[pl.ds(r0, size + PAD), :]
        out = k[taps - 1 : taps] * slab[:size]
        for lag in range(1, taps):
            part = (ok[:, lag : lag + 1] * slab)[lag : lag + size]
            out = out + k[taps - 1 - lag : taps - lag] * part
        dxs_ref[pl.ds(r0, size), :] = out.astype(BF16)
        return carry

    lax.fori_loop(0, (rows + PAD) // size, second, 0)


def conv_back(xs, du, slope, dp, sel, k, ok):
    rows, width = du.shape
    cb = scan_width(width, 768)
    col = lambda n: pl.BlockSpec((n, cb), lambda i: (0, i))
    whole = lambda x: pl.BlockSpec(x.shape, lambda i: (0, 0))
    taps = k.shape[0]
    return pl.pallas_call(
        conv_kernel_back,
        grid=(width // cb,),
        in_specs=[col(rows + PAD), col(rows), col(rows), whole(dp), col(sel.shape[0]), col(taps), whole(ok)],
        out_specs=[col(rows + PAD), col(taps), col(1)],
        out_shape=[sds((rows + PAD, width), BF16), sds((taps, width), F32), sds((1, width), F32)],
        scratch_shapes=[pltpu.VMEM((rows + 2 * PAD, cb), F32)],
        compiler_params=params(),
        cost_estimate=pl.CostEstimate(flops=rows * width * 300, bytes_accessed=rows * width * 8, transcendentals=0),
        name="conv_back",
    )(xs, du, slope, dp, sel, k, ok)


def scan_width(width, limit):
    n = width // 128
    best = max(d for d in range(1, n + 1) if n % d == 0 and d * 128 <= limit)
    return best * 128


def params():
    return pltpu.CompilerParams(vmem_limit_bytes=60 * 2**20)


def sds(*a):
    return jax.ShapeDtypeStruct(*a)


class Blocks:
    def __init__(self, rows, width, cb, parts, reverse=False, first=0):
        self.first = first
        self.grid = (width // cb, parts)
        self.cb, self.rows, self.seg = cb, rows, rows // parts
        self.at = (lambda s: parts - 1 - s) if reverse else (lambda s: s)

    def token(self, n):
        return pl.BlockSpec((self.seg, n), lambda k, s: (self.at(s), 0))

    def channel(self, n):
        return pl.BlockSpec((n, self.cb), lambda k, s: (0, k + self.first))

    def both(self, times=1, off=0):
        return pl.BlockSpec((self.seg * times, self.cb), lambda k, s: (self.at(s), k + self.first + off))

    def lead(self, n, *rest):
        return pl.BlockSpec((n, *rest), lambda k, s: (self.at(s),) + (0,) * len(rest))

    def marks(self, states):
        return pl.BlockSpec((self.seg // TC, states, self.cb), lambda k, s: (self.at(s), 0, k))

    def whole(self, shape):
        return pl.BlockSpec(shape, lambda k, s: (0,) * len(shape))


def estimate(rows, width, states, ops, size):
    return pl.CostEstimate(
        flops=ops * rows * width * states, bytes_accessed=rows * width * size, transcendentals=rows * width * states
    )


END, FORWARD, START, BACKWARD = (1152, 3), (1152, 6), (1152, 3), (2304, 24)


def end_states(s, w, b, st, u, a, bb, part, of):
    rows, width, states = s.shape[0], w.shape[1] // of, a.shape[0]
    cb = min(END[0], width)
    k = Blocks(rows, width, cb, END[1], first=part * (width // cb))
    return pl.pallas_call(
        end_kernel,
        grid=k.grid,
        in_specs=[k.token(s.shape[1]), k.channel(w.shape[0]), k.channel(1), k.token(1), k.both(), k.channel(states), k.lead(k.seg, states, 128)],
        out_specs=pl.BlockSpec((2 * states, cb), lambda i, j: (0, i)),
        out_shape=sds((2 * states, width), BF16),
        scratch_shapes=[pltpu.VMEM((k.seg, k.cb), F32)] * 2 + [pltpu.VMEM((states + 8, k.cb), F32)],
        compiler_params=params(),
        cost_estimate=estimate(rows, width, states, 6, 8),
        name="end_states",
    )(s, w, b, st, u, a, bb)


def forward_scan(s, w, b, st, u, z, a, skip, bb, cm, h0):
    rows, width, states = s.shape[0], w.shape[1], a.shape[0]
    k = Blocks(rows, width, *FORWARD)
    return pl.pallas_call(
        forward_kernel,
        grid=k.grid,
        in_specs=[k.token(s.shape[1]), k.channel(w.shape[0]), k.channel(1), k.token(1), k.both(), k.both(), k.channel(states), k.channel(1),
                  k.lead(k.seg, states, 128), k.lead(k.seg // TC, *cm.shape[1:]), k.channel(states)],
        out_specs=[k.both(), k.both(), k.both(states), k.marks(states)],
        out_shape=[sds((rows, width), BF16), sds((rows, width), BF16), sds((rows * states, width), BF16), sds((rows // TC, states, width), BF16)],
        scratch_shapes=[pltpu.VMEM((k.seg, k.cb), F32)] * 3 + [pltpu.VMEM((states, k.cb), F32)],
        compiler_params=params(),
        cost_estimate=estimate(rows, width, states, 9, 44),
        name="forward_scan",
    )(s, w, b, st, u, z, a, skip, bb, cm, h0)


def start_grads(s, w, b, st, dy, a, cb_wide, part, of):
    rows, width, states = s.shape[0], w.shape[1] // of, a.shape[0]
    cb = min(START[0], width)
    k = Blocks(rows, width, cb, START[1], reverse=True, first=part * (width // cb))
    return pl.pallas_call(
        start_kernel,
        grid=k.grid,
        in_specs=[k.token(s.shape[1]), k.channel(w.shape[0]), k.channel(1), k.token(1), k.both(), k.channel(states), k.lead(k.seg, states, 128)],
        out_specs=pl.BlockSpec((states, cb), lambda i, j: (0, i)),
        out_shape=sds((states, width), BF16),
        scratch_shapes=[pltpu.VMEM((k.seg, k.cb), F32), pltpu.VMEM((states, k.cb), F32)],
        compiler_params=params(),
        cost_estimate=estimate(rows, width, states, 6, 8),
        name="start_grads",
    )(s, w, b, st, dy, a, cb_wide)


def backward_scan(s, w, b, st, u, dy, a, skip, cb, bm, om, hs, ck, g0):
    rows, width, states = s.shape[0], w.shape[1], a.shape[0]
    k = Blocks(rows, width, *BACKWARD, reverse=True)
    chunks = rows // TC
    return pl.pallas_call(
        backward_kernel,
        grid=k.grid,
        in_specs=[k.token(s.shape[1]), k.channel(w.shape[0]), k.channel(1), k.token(1), k.both(), k.both(), k.channel(states), k.channel(1),
                  k.lead(k.seg, states, 128), k.lead(k.seg // TC, *bm.shape[1:]), k.whole(om.shape), k.both(states), k.marks(states), k.channel(states)],
        out_specs=[k.both(), k.both(), k.channel(states), k.channel(1), k.whole((rows, 128)), k.whole((chunks, 8, TC * states))],
        out_shape=[sds((rows, width), BF16), sds((rows, width), F32), sds((states, width), F32), sds((1, width), F32),
                   sds((rows, 128), BF16), sds((chunks, 8, TC * states), F32)],
        scratch_shapes=[pltpu.VMEM((k.seg, k.cb), F32)] * 5
        + [pltpu.VMEM((TC * states, k.cb), BF16)] * 4
        + [pltpu.VMEM((states, k.cb), F32), pltpu.VMEM((rows, states, 128), F32), pltpu.VMEM((chunks, TC, TC * states), F32)],
        compiler_params=params(),
        cost_estimate=estimate(rows, width, states, 18, 44),
        name="backward_scan",
    )(s, w, b, st, u, dy, a, skip, cb, bm, om, hs, ck, g0)


def spread(coeff):
    return jnp.broadcast_to(coeff[:, :, None], (*coeff.shape, 128))


def block_rows(coeff):
    rows, states = coeff.shape
    mask = jnp.arange(TC * states)[None, None] // states == jnp.arange(TC)[None, :, None]
    return jnp.where(mask, coeff.reshape(rows // TC, 1, TC * states), 0.0).astype(BF16)


epsilon = 1e-05
HALVES = 2


def shifted(array, axis, by):
    length = lax.axis_size(axis)
    pairs = [(i, i + by) for i in range(length) if 0 <= i + by < length]
    return lax.ppermute(array, axis, pairs)


def entering(came, sums, rate2):
    state, decay = jnp.zeros_like(rate2), jnp.zeros((1, rate2.shape[1]), F32)
    for end, total in zip(came, sums):
        state = state + jnp.exp2(rate2 * decay) * end.astype(F32)
        decay = decay + total
    return state


def product_back(left, right):
    return lax.dot_general(left, right, (((1,), (1,)), ((), ())), preferred_element_type=F32)


def contract(left, right):
    return lax.dot_general(left, right, (((0,), (0,)), ((), ())), preferred_element_type=F32)


def silu_slope(values):
    sigma = jax.nn.sigmoid(values)
    return sigma * (1.0 + values * (1.0 - sigma))


def inverse_rms(values):
    return lax.rsqrt(jnp.mean(values * values, axis=-1, keepdims=True) + epsilon)


def paired_rows(rows, devices):
    r, d = rows.shape
    split = rows.reshape(r // 2, 2, devices, d // devices)
    return split.transpose(0, 2, 1, 3).reshape(r // 2, 2 * d)


def single_rows(rows, devices):
    r, d = rows.shape
    split = rows.reshape(r, devices, 2, d // (2 * devices))
    return split.transpose(0, 2, 1, 3).reshape(2 * r, d // 2)


def stacked(parts):
    whole = jnp.concatenate([p.astype(BF16) for p in parts], axis=0)
    return jnp.pad(whole, ((0, -whole.shape[0] % 16), (0, 0)))


def cut(whole, counts):
    out, at = [], 0
    for n in counts:
        out.append(whole[at : at + n])
        at += n
    return out


def body(
    tokens, cotangent, routes, starts, input_proj, conv_kernel, conv_bias, select_proj, step_proj,
    step_bias, decay_log, skip_gain, output_proj, norm_gain, ffn_gain, router, expert_up, expert_down,
):
    devices = lax.axis_size("dp")
    groups = lax.axis_size("expert")
    rows, model = tokens.shape
    taps, rank, states = conv_kernel.shape[0], step_proj.shape[0], decay_log.shape[1]
    capacity = 2 * rows // groups
    w_input = lax.all_gather(input_proj, "dp", axis=1, tiled=True)
    small = stacked(
        [
            select_proj.T, step_proj, decay_log.T, conv_kernel, conv_bias[None], step_bias[None], skip_gain[None],
            paired_rows(jnp.concatenate([norm_gain[None], ffn_gain[None], router.T], 0), 1),
        ]
    )
    counts = (select_proj.shape[1], rank, states, taps, 1, 1, 1, (groups + 2) // 2)
    w_select, w_step, w_decay, w_conv, b_conv, bias2, skip2, singles = cut(
        lax.all_gather(small, "dp", axis=1, tiled=True), counts
    )
    singles = single_rows(singles, devices).astype(F32)
    norm_f, ffn_f, router_f = singles[0], singles[1], singles[2:]
    w_output = lax.all_gather(output_proj, "dp", axis=0, tiled=True)
    w_up = lax.all_gather(expert_up[0], "dp", axis=1, tiled=True)
    w_down = lax.all_gather(expert_down[0], "dp", axis=0, tiled=True)
    width = w_select.shape[1]
    conv_f = w_conv.astype(F32)

    route = routes[:, 0]
    chosen = (route[:, None] == jnp.arange(groups, dtype=jnp.int32)[None, :]).astype(F32)
    before = (jnp.arange(rows)[:, None] > jnp.arange(rows)[None, :]).astype(BF16)
    ranks = dot(before, chosen.astype(BF16))
    slot = jnp.sum(ranks * chosen, axis=1).astype(jnp.int32)
    distance = jnp.mod(route - lax.axis_index("expert"), groups)
    target = jnp.where(slot < capacity, distance * capacity + slot, groups * capacity)
    place = (jnp.arange(groups * capacity)[:, None] == target[None, :]).astype(BF16)

    hidden_in = tokens.astype(F32)
    norm_r = inverse_rms(hidden_in)
    norm_own = (hidden_in * norm_r * norm_f).astype(BF16)
    flag = starts.astype(F32)
    same = 1.0 - flag
    valid = [jnp.ones((rows,), F32)]
    for lag in range(1, taps):
        moved = jnp.concatenate([jnp.ones((lag - 1,), F32), same[: rows - lag + 1]])
        valid.append(valid[-1] * moved)
    edge = [jnp.ones((), F32)]
    for lag in range(1, taps - 1):
        edge.append(edge[-1] * same[rows - lag])
    edge_keep = jnp.stack(edge[::-1])[:, None]
    tail = (norm_own[rows - taps + 1 :].astype(F32) * edge_keep).astype(BF16)
    borrowed = shifted(tail, "expert", 1)
    norm_low = jnp.concatenate([jnp.zeros((PAD - taps + 1, model), BF16), borrowed, norm_own], 0)
    mixed = dot(norm_low, w_input).astype(BF16)
    conv_sum = jnp.broadcast_to(b_conv.astype(F32), (rows, width))
    for lag in range(taps):
        conv_sum = conv_sum + valid[lag][:, None] * conv_f[taps - 1 - lag] * mixed[PAD - lag : PAD - lag + rows, :width].astype(F32)
    ok = jnp.pad(jnp.stack(valid, 1), ((PAD, PAD), (0, 0)))
    inner_low = jax.nn.silu(conv_sum).astype(BF16)
    slope_low = silu_slope(conv_sum).astype(BF16)
    selected = product_back(inner_low, w_select)
    step_low = selected[:, :rank].astype(BF16)
    b_coeff = selected[:, rank : rank + states]
    c_coeff = selected[:, rank + states :]
    rate2 = -jnp.exp(w_decay.astype(F32)) * LOG2E
    gate_in = mixed[PAD:, width:]
    st = flag[:, None]
    b_wide, c_wide = spread(b_coeff), spread(c_coeff)
    b_block, c_block = block_rows(b_coeff), block_rows(c_coeff)
    one_block = (jnp.arange(TC * states)[None] // states == jnp.arange(TC)[:, None]).astype(BF16)
    hops = range(1, groups)
    own_sums, start_state = [], []
    for part in range(HALVES):
        rate_part = rate2[:, part * width // HALVES : (part + 1) * width // HALVES]
        end = end_states(step_low, w_step, bias2, st, inner_low, rate2, b_wide, part, HALVES)
        came = [shifted(end, "expert", hop) for hop in hops]
        total = lambda x: x[:1].astype(F32) + x[1:2].astype(F32)
        own_sums.append(end[states : states + 8])
        start_state.append(entering([c[:states] for c in came], [total(c[states:]) for c in came], rate_part))
    start_state = jnp.concatenate(start_state, 1)
    gated_low, scanned, history, marks = forward_scan(
        step_low, w_step, bias2, st, inner_low, gate_in, rate2, skip2, b_wide, c_block, start_state
    )
    hidden_one = hidden_in + dot(gated_low, w_output)

    r2 = inverse_rms(hidden_one)
    norm_two = hidden_one * r2 * ffn_f
    logits = lax.dot_general(
        norm_two, router_f, (((1,), (1,)), ((), ())),
        precision=lax.Precision.HIGHEST, preferred_element_type=F32,
    )
    probs = jax.nn.softmax(logits, axis=-1)
    gate_value = jnp.sum(probs * chosen, axis=-1)
    grad_out = cotangent.astype(F32)
    grad_picked = (gate_value[:, None] * grad_out).astype(BF16)

    def moved(x, by):
        return lax.ppermute(x, "expert", [(i, (i + by) % groups) for i in range(groups)]) if by else x

    places = [place[k * capacity : (k + 1) * capacity] for k in range(groups)]
    norm_two_low = norm_two.astype(BF16)
    arrived = [moved(dot(m, norm_two_low).astype(BF16), k) for k, m in enumerate(places)]
    grad_arrived = []
    for k, m in enumerate(places):
        sent = dot(m, grad_picked).astype(BF16)
        if k:
            sent, arrived[k] = lax.optimization_barrier((sent, arrived[k]))
        grad_arrived.append(moved(sent, k))
    up_low, grad_pre, outs, ins = [], [], [], []
    for k in range(groups):
        up_pre = dot(arrived[k], w_up)
        act, gelu_back = jax.vjp(jax.nn.gelu, up_pre)
        up_low.append(act.astype(BF16))
        outs.append(dot(up_low[k], w_down).astype(BF16))
        grad_pre.append(gelu_back(product_back(grad_arrived[k], w_down))[0].astype(BF16))
        ins.append(product_back(grad_pre[k], w_up).astype(BF16))
    returned = jnp.concatenate([moved(x, -k) for k, x in enumerate(outs)])
    grad_sent = jnp.concatenate([moved(x, -k) for k, x in enumerate(ins)])
    up_low, grad_pre, arrived, grad_arrived, _, _ = lax.optimization_barrier(
        (up_low, grad_pre, arrived, grad_arrived, outs, ins)
    )
    grad_up = contract(jnp.concatenate(grad_pre), jnp.concatenate(arrived)).astype(BF16)
    grad_down = contract(jnp.concatenate(up_low), jnp.concatenate(grad_arrived)).astype(BF16)
    grad_sent, grad_up, grad_down = lax.optimization_barrier((grad_sent, grad_up, grad_down))
    sum_up = lax.psum_scatter(grad_up, "dp", scatter_dimension=0, tiled=True)

    picked = contract(place, returned)
    output = (hidden_one + gate_value[:, None] * picked).astype(BF16)
    grad_gate = jnp.sum(grad_out * picked, axis=1)
    grad_logits = probs * (grad_gate[:, None] * chosen - (grad_gate * gate_value)[:, None])
    grad_router = lax.dot_general(
        grad_logits, norm_two, (((0,), (0,)), ((), ())),
        precision=lax.Precision.HIGHEST, preferred_element_type=F32,
    )
    grad_norm_two = contract(place, grad_sent) + lax.dot_general(
        grad_logits, router_f, (((1,), (0,)), ((), ())),
        precision=lax.Precision.HIGHEST, preferred_element_type=F32,
    )
    grad_ffn_gain = jnp.sum(grad_norm_two * hidden_one * r2, axis=0)
    scaled = ffn_f * grad_norm_two
    grad_hidden = (
        grad_out
        + r2 * scaled
        - hidden_one * (r2 * r2 * r2) * jnp.mean(hidden_one * scaled, axis=-1, keepdims=True)
    )

    grad_mixer = grad_hidden.astype(BF16)
    grad_output_w = contract(gated_low, grad_mixer)
    grad_gated = product_back(grad_mixer, w_output)
    gate_f = gate_in.astype(F32)
    sigma = jax.nn.sigmoid(gate_f)
    grad_scanned = grad_gated * (gate_f * sigma)
    grad_gate_in = (grad_gated * scanned.astype(F32) * (sigma * (1.0 + gate_f * (1.0 - sigma)))).astype(BF16)
    grad_scanned, sum_up, grad_down = lax.optimization_barrier((grad_scanned, sum_up, grad_down))
    sum_down = lax.psum_scatter(grad_down, "dp", scatter_dimension=0, tiled=True)
    later_grad = []
    for part in range(HALVES):
        rate_part = rate2[:, part * width // HALVES : (part + 1) * width // HALVES]
        start = start_grads(step_low, w_step, bias2, st, grad_scanned, rate2, c_wide, part, HALVES)
        start = jnp.concatenate([start, own_sums[part]])
        came = [shifted(start, "expert", -hop) for hop in hops]
        later_grad.append(entering([c[:states] for c in came], [total(c[states:]) for c in came], rate_part))
    later_grad, sum_down, grad_output_w = lax.optimization_barrier(
        (jnp.concatenate(later_grad, 1), sum_down, grad_output_w.astype(BF16))
    )
    sum_output = lax.psum_scatter(grad_output_w, "dp", scatter_dimension=0, tiled=True)
    grad_pre_step, grad_inner, grad_decay_t, grad_skip, grad_b, grad_c = backward_scan(
        step_low, w_step, bias2, st, inner_low, grad_scanned, rate2, skip2,
        c_wide, b_block, one_block, history, marks, later_grad,
    )
    grad_pre_step, sum_output = lax.optimization_barrier((grad_pre_step, sum_output))
    sum_output = lax.psum(sum_output, "expert")
    grad_step_bias = jnp.sum(grad_pre_step.astype(F32), axis=0, keepdims=True)
    grad_step_w = contract(step_low, grad_pre_step)
    grad_step_low = product_back(grad_pre_step, w_step).astype(BF16)
    grad_selected = jnp.concatenate(
        [grad_step_low, grad_b[:, :states], grad_c[:, 0].reshape(rows, states).astype(BF16)], 1
    )
    grad_select_w = contract(grad_selected, inner_low)
    summed = stacked(
        [
            grad_select_w, grad_step_w, grad_decay_t, grad_step_bias, grad_skip,
            paired_rows(jnp.concatenate([grad_ffn_gain[None], grad_ffn_gain[None], grad_router], 0), devices),
        ]
    )
    grad_conv_in, grad_kernel, grad_conv_b = conv_back(
        mixed, grad_inner, slope_low, grad_selected, w_select, w_conv, ok
    )
    grad_conv_in, summed, sum_output = lax.optimization_barrier((grad_conv_in, summed, sum_output))
    summed = lax.psum_scatter(summed, "dp", scatter_dimension=1, tiled=True)
    grad_mixed = jnp.concatenate([grad_conv_in, jnp.pad(grad_gate_in, ((PAD, 0), (0, 0)))], 1)
    grad_input_w = contract(grad_mixed, norm_low).astype(BF16)
    grad_input_w, grad_mixed, summed = lax.optimization_barrier((grad_input_w, grad_mixed, summed))
    sum_input = lax.psum_scatter(grad_input_w, "dp", scatter_dimension=0, tiled=True)
    sum_input, summed = lax.psum((sum_input, summed), "expert")
    summed = summed.astype(F32)
    grad_norm_one = product_back(grad_mixed, w_input)
    returned_edge = shifted(grad_norm_one[PAD - taps + 1 : PAD], "expert", -1) * edge_keep
    grad_norm_one = grad_norm_one[PAD:] + jnp.pad(returned_edge, ((rows - taps + 1, 0), (0, 0)))
    grad_norm_gain = jnp.sum(grad_norm_one * hidden_in * norm_r, axis=0, keepdims=True)
    scaled_one = norm_f * grad_norm_one
    grad_tokens = (
        grad_hidden
        + norm_r * scaled_one
        - hidden_in * (norm_r * norm_r * norm_r) * jnp.mean(hidden_in * scaled_one, axis=-1, keepdims=True)
    ).astype(BF16)
    tiny = jnp.concatenate([grad_kernel, grad_conv_b, jnp.pad(grad_norm_gain, ((0, 0), (0, width - model)))])
    tiny = lax.psum(tiny, ("dp", "expert"))
    here = lax.axis_index("dp")
    share, model_share = width // devices, model // devices
    own = lax.dynamic_slice(tiny, (0, here * share), (taps + 1, share))
    sum_kernel, sum_conv_b = own[:taps], own[taps]
    sum_norm = lax.dynamic_slice(tiny, (taps + 1, here * model_share), (1, model_share))[0]
    sum_select, sum_step, sum_decay, sum_step_b, sum_skip, singles = cut(
        summed, (w_select.shape[0], rank, states, 1, 1, (groups + 2) // 2)
    )
    singles = single_rows(singles, 1)
    sum_input, sum_output = sum_input.astype(F32).T, sum_output.astype(F32)
    return (
        output, grad_tokens, sum_input, sum_kernel, sum_conv_b, sum_select.T, sum_step, sum_step_b[0],
        sum_decay.T, sum_skip[0], sum_output, sum_norm, singles[1], singles[2:].T,
        sum_up.astype(F32).T[None], sum_down.astype(F32)[None],
    )


def solution(mesh):
    placed = (
        P(("dp", "expert"), None),
        P(("dp", "expert"), None),
        P(("dp", "expert"), None),
        P(("dp", "expert")),
        P(None, "dp"),
        P(None, "dp"),
        P("dp"),
        P("dp", None),
        P(None, "dp"),
        P("dp"),
        P("dp", None),
        P("dp"),
        P("dp", None),
        P("dp"),
        P("dp"),
        P("dp", None),
        P("expert", None, "dp"),
        P("expert", "dp", None),
    )
    return jax.shard_map(
        body,
        mesh=mesh,
        in_specs=placed,
        out_specs=(
            P(("dp", "expert"), None),
            P(("dp", "expert"), None),
            P(None, "dp"),
            P(None, "dp"),
            P("dp"),
            P("dp", None),
            P(None, "dp"),
            P("dp"),
            P("dp", None),
            P("dp"),
            P("dp", None),
            P("dp"),
            P("dp"),
            P("dp", None),
            P("expert", None, "dp"),
            P("expert", "dp", None),
        ),
        check_vma=False,
    )
```

time: 1440 us -> 1050 us (0.73)
  waiting for transfers between devices: 563 us -> 239 us
  Pallas kernels: 305 us -> 227 us
  starting transfers between devices: 26.2 us -> 96.4 us
  local copies, waits for them, and re-layouts: 143 us -> 86.1 us
  matrix products: 270 us -> 240 us
  other arithmetic: 53 us -> 73 us
    all_to_all x4 -> x0, waiting for transfers between devices: 200 us -> none  [exchange(): lax.all_to_all(x.reshape(groups, capacity, model), 'expert', split_axis=0...]
    reduce_scatter x3 -> x4, waiting for transfers between devices: 173 us -> 60.1 us  [the longest x1 60.1 us: body(): lax.psum_scatter(grad_input_w, 'dp', scatter_dimension=0, tiled=True)]
    ppermute x0 -> x12, waiting for transfers between devices: none -> 85.4 us  [moved(): lax.ppermute(x, 'expert', [(i, (i + by) % groups) for i in range(groups)])]
    pallas_call x4 -> x7, Pallas kernels: 305 us -> 227 us  [the longest x1 96.4 us: backward_scan(): pl.pallas_call(backward_kernel, grid=k.grid, in_specs=[k.token(s.shape[1]...]
    ppermute x0 -> x12, starting transfers between devices: none -> 69.4 us  [moved(): lax.ppermute(x, 'expert', [(i, (i + by) % groups) for i in range(groups)])]
    psum x1 -> x2, waiting for transfers between devices: 88.6 us -> 28.5 us  [the longest x1 20.5 us: body(): sum_input, summed = lax.psum((sum_input, summed), 'expert')]
    unnamed x12, waiting for transfers between devices: 67.4 us -> 16.5 us
    psum x0 -> x1, blocking collectives: none -> 44.1 us  [body(): tiny = lax.psum(tiny, ('dp', 'expert'))]
  transfers between devices with their start and end apart: 16 -> 37, of which waited for: 10 -> 15; matrix products, arithmetic and copies ran while one was open for 22% -> 35% of each run, Pallas kernels for 6% -> 22%
where the time goes in v2:
time: 1050 us; the launch traced here: 1040 us
  matrix products  240 us (23%)
  waiting for transfers between devices  239 us (23%)
  Pallas kernels  227 us (22%)
  starting transfers between devices  96.4 us (9%)
  local copies, waits for them, and re-layouts  86.1 us (8%)
  other arithmetic  73 us (7%)
  blocking collectives  61.4 us (6%)
  between operations  16.7 us (2%)
    pallas_call x1, Pallas kernels, backward_scan(): pl.pallas_call(backward_kernel, grid=k.grid, in_specs=[k.token(s.shape[1]...  96.4 us
    ppermute x12, waiting for transfers between devices, moved(): lax.ppermute(x, 'expert', [(i, (i + by) % groups) for i in range(groups)])  85.4 us
    dot_general x19, matrix products, dot(): return jnp.dot(a, b, preferred_element_type=F32)  83.3 us
    dot_general x8, matrix products, contract(): lax.dot_general(left, right, (((0,), (0,)), ((), ())), preferred_element_...  77.7 us
    dot_general x12, matrix products, product_back(): lax.dot_general(left, right, (((1,), (1,)), ((), ())), preferred_element_...  70.5 us
    ppermute x12, starting transfers between devices, moved(): lax.ppermute(x, 'expert', [(i, (i + by) % groups) for i in range(groups)])  69.4 us
    reduce_scatter x1, waiting for transfers between devices, body(): lax.psum_scatter(grad_input_w, 'dp', scatter_dimension=0, tiled=True)  60.1 us
    psum x1, blocking collectives, body(): tiny = lax.psum(tiny, ('dp', 'expert'))  44.1 us
  transfers between devices with their start and end apart: 37, of which 15 were waited for; matrix products, arithmetic and copies ran while one was open for 35% of the time, Pallas kernels for 22%

profile of v2, /device:TPU:4, one launch (start us, length us, event | category | flops | bytes accessed | tf_op | source)
XLA Modules:
  0.0 1039.8 jit_solution(16411325122350468020)
XLA Ops:
  17.8 17.2 %all_gather.15 = bf16[208,2304]{0,1:T(8,128)(2,1)S(1)} all-gather(bf16[208,288]{0,1:T(8,128)(2,1)S(1)} %pad.25), channel_id=1, replica_groups=mesh['dp'=8,'expert'=4] {'dp'}, dimensions={1}, use_global_device_ids=true | all-gather | bytes 1078272 | tf_op jit(solution)/shard_map/all_gather | solution.py:543
  61.5 17.7 %all-gather.7.cloned.1.call-done = bf16[1152,4608]{0,1:T(8,128)(2,1)} async-done(((bf16[1152,576]{0,1:T(8,128)(2,1)}), bf16[1152,4608]{0,1:T(8,128)(2,1)}) %all-gather.7.cloned.1.call-update) | async-done | bytes 10616848 | tf_op jit(solution)/shard_map/all_gather | solution.py:534
  79.3 13.1 %convolution_convert_fusion.4.xs_ref = bf16[784,4608]{1,0:T(8,128)(2,1)S(1)} fusion(bf16[1152,4608]{0,1:T(8,128)(2,1)} %all-gather.7.cloned.1.call-done, bf16[768,1152]{1,0:T(8,128)(2,1)} %copy-done.19, bf16[3,1152]{1,0:T(4,128)(2,1)} %collective-permute-done, bf16[784]{0:T(1024)(128)(2,1)S(1)} %pad.80.clone), kind=kOutput, calls=%fused_computation.23 | convolution fusion | flops 8332627968 | bytes 19620128 | tf_op jit(solution)/shard_map/dot_general | solution.py:35
  92.4 8.2 multiply_convert_fusion
  116.9 17.7 %end_states.2 = bf16[32,1152]{1,0:T(8,128)(2,1)} custom-call(bf16[768,72]{1,0:T(8,128)(2,1)} %copy.152.s_ref, bf16[72,2304]{1,0:T(8,128)(2,1)} %copy.153.w_ref, bf16[1,2304]{1,0:T(2,128)(2,1)} %copy.154.b_ref, f32[768,1]{1,0:T(8,128)} %broadcast_in_dim.168.st_ref, bf16[768,2304]{1,0:T(8,128)(2,1)} %copy-done.3, f32[16,2304]{1,0:T(8,128)} %negate_multiply_fusion.a_ref, ...), custom_call_target="tpu_custom_call" | custom-call | flops 84934656 | bytes 7077888 | tf_op jit(solution)/shard_map/end_states/pallas_call | solution.py:387
  150.9 17.8 %end_states.3 = bf16[32,1152]{1,0:T(8,128)(2,1)} custom-call(bf16[768,72]{1,0:T(8,128)(2,1)} %copy.152.s_ref, bf16[72,2304]{1,0:T(8,128)(2,1)} %copy.153.w_ref, bf16[1,2304]{1,0:T(2,128)(2,1)} %copy.154.b_ref, f32[768,1]{1,0:T(8,128)} %broadcast_in_dim.168.st_ref, bf16[768,2304]{1,0:T(8,128)(2,1)} %copy-done.3, f32[16,2304]{1,0:T(8,128)} %negate_multiply_fusion.a_ref, ...), custom_call_target="tpu_custom_call" | custom-call | flops 84934656 | bytes 7077888 | tf_op jit(solution)/shard_map/end_states/pallas_call | solution.py:387
  176.6 42.5 %forward_scan.1 = (bf16[768,2304]{1,0:T(8,128)(2,1)}, bf16[768,2304]{1,0:T(8,128)(2,1)}, bf16[12288,2304]{1,0:T(8,128)(2,1)}, bf16[48,16,2304]{2,1,0:T(8,128)(2,1)}) custom-call(bf16[768,72]{1,0:T(8,128)(2,1)} %copy.152.s_ref, bf16[72,2304]{1,0:T(8,128)(2,1)} %copy.153.w_ref, bf16[1,2304]{1,0:T(2,128)(2,1)} %copy.154.b_ref, ...), custom_call_target="tpu_custom_call" | custom-call | flops 254803968 | bytes 77856768 | tf_op jit(solution)/shard_map/forward_scan/pallas_call | solution.py:403
  219.1 8.5 multiply_reduce_fusion.2
  251.9 10.2 multiply_convert_fusion.5
  262.2 8.8 fusion.62
  284.0 29.8 %collective-permute-done.9 = bf16[384,1152]{1,0:T(8,128)(2,1)} collective-permute-done((bf16[384,1152]{1,0:T(8,128)(2,1)}, bf16[384,1152]{1,0:T(8,128)(2,1)}, u32[]{:S(2)}, u32[]{:S(2)}) %collective-permute-start.9) | collective-permute-done | bytes 884768 | tf_op jit(solution)/shard_map/ppermute | solution.py:622
  313.8 36.6 %collective-permute-start.13 = (bf16[384,1152]{1,0:T(8,128)(2,1)S(1)}, bf16[384,1152]{1,0:T(8,128)(2,1)S(1)}, u32[]{:S(2)}, u32[]{:S(2)}) collective-permute-start(bf16[384,1152]{1,0:T(8,128)(2,1)S(1)} %convolution_convert_fusion.13), channel_id=1, source_target_pairs={{0,1},{1,2},{2,3},{3,0},{4,5},{5,6},{6,7},{7,4},{8,9},{9,10},{10,1... | collective-permute-start | bytes 2654216 | tf_op jit(solution)/shard_map/ppermute | solution.py:622
  383.5 7.3 fusion.83
  423.9 17.8 %convolution_convert_fusion.3 = bf16[3072,1152]{1,0:T(8,128)(2,1)} fusion(bf16[384,3072]{1,0:T(8,128)(2,1)} %copy-done.82, bf16[384,3072]{1,0:T(8,128)(2,1)} %fusion.76, bf16[384,3072]{1,0:T(8,128)(2,1)} %copy-done.83, bf16[384,3072]{1,0:T(8,128)(2,1)} %copy-done.81, bf16[384,1152]{1,0:T(8,128)(2,1)} %collective-permute-done.11, ...), kind=kOutput, calls=%fused_computation.5 | convolution fusion | flops 10927079424 | bytes 20054016 | tf_op jit(solution)/shard_map/dot_general | solution.py:488
  441.8 18.2 %convolution_convert_fusion.2 = bf16[3072,1152]{1,0:T(8,128)(2,1)} fusion(bf16[384,3072]{1,0:T(8,128)(2,1)} %copy-done.85, bf16[384,3072]{1,0:T(8,128)(2,1)} %copy-done.86, bf16[384,3072]{1,0:T(8,128)(2,1)} %copy-done.87, bf16[384,3072]{1,0:T(8,128)(2,1)} %get-tuple-element.83, bf16[384,1152]{1,0:T(8,128)(2,1)} %copy-done.75, ...), kind=kOutput, calls=%fused_computation.4 | convolution fusion | flops 10927079424 | bytes 20054016 | tf_op jit(solution)/shard_map/dot_general | solution.py:488
  461.6 7.7 pad_maximum_fusion
  469.4 15.5 %collective-permute-start.12 = (bf16[384,1152]{1,0:T(8,128)(2,1)}, bf16[384,1152]{1,0:T(8,128)(2,1)S(1)}, u32[]{:S(2)}, u32[]{:S(2)}) collective-permute-start(bf16[384,1152]{1,0:T(8,128)(2,1)} %fusion.147), channel_id=1, source_target_pairs={{0,1},{1,2},{2,3},{3,0},{4,5},{5,6},{6,7},{7,4},{8,9},{9,10},{10,1... | collective-permute-start | bytes 2654216 | tf_op jit(solution)/shard_map/ppermute | solution.py:622
  488.7 17.8 %collective-permute-done.12 = bf16[384,1152]{1,0:T(8,128)(2,1)S(1)} collective-permute-done((bf16[384,1152]{1,0:T(8,128)(2,1)}, bf16[384,1152]{1,0:T(8,128)(2,1)S(1)}, u32[]{:S(2)}, u32[]{:S(2)}) %collective-permute-start.12) | collective-permute-done | bytes 884768 | tf_op jit(solution)/shard_map/ppermute | solution.py:622
  506.5 36.2 %collective-permute-done.10 = bf16[384,1152]{1,0:T(8,128)(2,1)S(1)} collective-permute-done((bf16[384,1152]{1,0:T(8,128)(2,1)S(1)}, bf16[384,1152]{1,0:T(8,128)(2,1)S(1)}, u32[]{:S(2)}, u32[]{:S(2)}) %collective-permute-start.10) | collective-permute-done | bytes 884768 | tf_op jit(solution)/shard_map/ppermute | solution.py:622
  572.3 10.2 convolution_convert_fusion.1
  587.5 17.0 %start_grads.2 = bf16[16,1152]{1,0:T(8,128)(2,1)} custom-call(bf16[768,72]{1,0:T(8,128)(2,1)} %copy.152.s_ref, bf16[72,2304]{1,0:T(8,128)(2,1)} %copy.153.w_ref, bf16[1,2304]{1,0:T(2,128)(2,1)} %copy.154.b_ref, f32[768,1]{1,0:T(8,128)} %broadcast_in_dim.168.st_ref, f32[768,2304]{1,0:T(8,128)} %get-tuple-element.94.dy_ref, ...), custom_call_target="tpu_custom_call" | custom-call | flops 84934656 | bytes 7077888 | tf_op jit(solution)/shard_map/start_grads/pallas_call | solution.py:421
  609.4 17.2 %start_grads.3 = bf16[16,1152]{1,0:T(8,128)(2,1)} custom-call(bf16[768,72]{1,0:T(8,128)(2,1)} %copy.152.s_ref, bf16[72,2304]{1,0:T(8,128)(2,1)} %copy.153.w_ref, bf16[1,2304]{1,0:T(2,128)(2,1)} %copy.154.b_ref, f32[768,1]{1,0:T(8,128)} %broadcast_in_dim.168.st_ref, f32[768,2304]{1,0:T(8,128)} %get-tuple-element.94.dy_ref, ...), custom_call_target="tpu_custom_call" | custom-call | flops 84934656 | bytes 7077888 | tf_op jit(solution)/shard_map/start_grads/pallas_call | solution.py:421
  632.2 21.8 %collective-permute-done.22 = bf16[24,1152]{1,0:T(8,128)(2,1)S(1)} collective-permute-done((bf16[24,1152]{1,0:T(8,128)(2,1)S(1)}, bf16[24,1152]{1,0:T(8,128)(2,1)S(1)}, u32[]{:S(2)}, u32[]{:S(2)}) %collective-permute-start.22) | collective-permute-done | bytes 55328 | tf_op jit(solution)/shard_map/ppermute | solution.py:472
  674.5 96.4 %backward_scan.1 = (bf16[768,2304]{1,0:T(8,128)(2,1)}, f32[768,2304]{1,0:T(8,128)}, f32[16,2304]{1,0:T(8,128)}, f32[1,2304]{1,0:T(1,128)}, bf16[768,128]{1,0:T(8,128)(2,1)}, /*index=5*/f32[48,8,256]{2,1,0:T(8,128)}) custom-call(bf16[768,72]{1,0:T(8,128)(2,1)} %copy.152.s_ref, bf16[72,2304]{1,0:T(8,128)(2,1)} %copy.153.w_ref, bf16[1,2304]{1,0:T(2,128)(2,1)} %copy.154.b_ref, ...), custom_call_target="tpu_custom_call" | custom-call | flops 509607936 | bytes 77856768 | tf_op jit(solution)/shard_map/backward_scan/pallas_call | solution.py:438
  798.8 18.7 %conv_back.1 = (bf16[784,2304]{1,0:T(8,128)(2,1)}, f32[4,2304]{1,0:T(4,128)}, f32[1,2304]{1,0:T(1,128)}) custom-call(bf16[784,4608]{1,0:T(8,128)(2,1)} %copy-done, f32[768,2304]{1,0:T(8,128)} %get-tuple-element.99.du_ref, bf16[768,2304]{1,0:T(8,128)(2,1)} %get-tuple-element.222.slope_ref, bf16[768,104]{1,0:T(8,128)(2,1)} %copy-done.21, ...), custom_call_target="tpu_custom_call" | custom-call | flops 530841600 | bytes 14155776 | tf_op jit(solution)/shard_map/conv_back/pallas_call | solution.py:321
  817.5 8.1 all-reduce.11.cloned.1.call-done
  833.6 17.7 %convolution_convert_fusion = bf16[4608,1152]{1,0:T(8,128)(2,1)} fusion(bf16[768,1152]{1,0:T(8,128)(2,1)S(1)} %copy-done.20, bf16[3,1152]{1,0:T(4,128)(2,1)} %collective-permute-done, bf16[784]{0:T(1024)(128)(2,1)S(1)} %copy-done.70, bf16[768,2304]{1,0:T(8,128)(2,1)S(1)} %copy-done.12, bf16[784,2304]{1,0:T(8,128)(2,1)} %get-tuple-element.109), kind=kOutput, calls=%fused_computation | convolution fusion | flops 8355999744 | bytes 19546400 | tf_op jit(solution)/shard_map/dot_general | solution.py:488
  851.2 14.3 %reduce-scatter.16.cloned.1.call-done = bf16[288,208]{1,0:T(8,128)(2,1)} async-done(((bf16[2304,208]{1,0:T(8,128)(2,1)}), bf16[288,208]{1,0:T(8,128)(2,1)}) %reduce-scatter.16.cloned.1.call-update) | async-done | bytes 119824
  870.5 13.4 %fusion.235 = f32[784,1152]{1,0:T(8,128)S(1)} fusion(bf16[784,4608]{1,0:T(8,128)(2,1)} %fusion.15, bf16[1152,4608]{0,1:T(8,128)(2,1)} %all-gather.7.cloned.1.call-done), kind=kOutput, calls=%fused_computation.342 | convolution fusion | flops 8323596288 | bytes 21454848 | tf_op jit(solution)/shard_map/dot_general | solution.py:484
  891.3 60.1 %reduce-scatter.14.cloned.1.call-done = bf16[576,1152]{1,0:T(8,128)(2,1)} async-done(((bf16[4608,1152]{1,0:T(8,128)(2,1)}), bf16[576,1152]{1,0:T(8,128)(2,1)}) %reduce-scatter.14.cloned.1.call-update) | async-done | bytes 1327120 | tf_op jit(solution)/shard_map/reduce_scatter | solution.py:718
  951.5 44.1 %psum.30 = f32[6,2304]{1,0:T(8,128)S(1)} all-reduce(f32[6,2304]{1,0:T(8,128)S(1)} %select_maximum_fusion), channel_id=1, replica_groups=mesh['dp'=8,'expert'=4] {'dp','expert'}, use_global_device_ids=true, to_apply=%region_19.20 | all-reduce | flops 13824 | bytes 110592 | tf_op jit(solution)/shard_map/psum | solution.py:732
  1002.5 20.5 %all-reduce.13.cloned.1.call-done = (bf16[1152,576]{0,1:T(8,128)(2,1)}, bf16[208,288]{1,0:T(8,128)(2,1)}) async-done(((bf16[1152,576]{0,1:T(8,128)(2,1)}, bf16[208,288]{1,0:T(8,128)(2,1)}), (bf16[1152,576]{0,1:T(8,128)(2,1)}, bf16[208,288]{1,0:T(8,128)(2,1)})) %all-reduce.13.cloned.1.call-update) | async-done | bytes 1446928 | tf_op jit(solution)/shard_map/psum | solution.py:719
  (422 shorter events, 314.9 us)
Async XLA Ops:
  7.2 72.0 %all-gather.7.cloned.1.call-start = ((), (), s32[]{:S(2)}) async-start(), calls=%async_computation.5 | async-start | bytes 11943936 | tf_op jit(solution)/shard_map/all_gather | solution.py:534
  7.9 211.2 %all-gather.9.cloned.1.call-start = ((), (), s32[]{:S(2)}) async-start(), calls=%async_computation.6 | async-start | bytes 5971968 | tf_op jit(solution)/shard_map/all_gather | solution.py:547
  8.7 243.2 %all-gather.11.cloned.1.call-start = ((), (), s32[]{:S(2)}) async-start(), calls=%async_computation.12 | async-start | bytes 7962624 | tf_op jit(solution)/shard_map/all_gather | solution.py:548
  9.4 252.7 %all-gather.13.cloned.1.call-start = ((), (), s32[]{:S(2)}) async-start(), calls=%async_computation.13 | async-start | bytes 7962624 | tf_op jit(solution)/shard_map/all_gather | solution.py:549
  47.3 522.3 %reduce-scatter.8.cloned.1.call-start = ((), (), s32[]{:S(2)}) async-start(), calls=%async_computation.7 | async-start | bytes 7962624 | tf_op jit(solution)/shard_map/reduce_scatter | solution.py:649
  134.7 36.7 %collective-permute-start.2 = (bf16[32,1152]{1,0:T(8,128)(2,1)}, bf16[32,1152]{1,0:T(8,128)(2,1)S(1)}, u32[]{:S(2)}, u32[]{:S(2)}) collective-permute-start(bf16[32,1152]{1,0:T(8,128)(2,1)} %end_states.2), channel_id=1, source_target_pairs={{0,2},{1,3},{4,6},{5,7},{8,10},{9,11},{12,14},{13,15},{16,18},{17,... | collective-permute-start | bytes 221192 | tf_op jit(solution)/shard_map/ppermute | solution.py:472
  139.1 33.6 %collective-permute-start.1 = (bf16[32,1152]{1,0:T(8,128)(2,1)}, bf16[32,1152]{1,0:T(8,128)(2,1)S(1)}, u32[]{:S(2)}, u32[]{:S(2)}) collective-permute-start(bf16[32,1152]{1,0:T(8,128)(2,1)} %end_states.2), channel_id=1, source_target_pairs={{0,1},{1,2},{2,3},{4,5},{5,6},{6,7},{8,9},{9,10},{10,11},{12,13},{... | collective-permute-start | bytes 221192 | tf_op jit(solution)/shard_map/ppermute | solution.py:472
  149.5 26.3 %collective-permute-start.3 = (bf16[32,1152]{1,0:T(8,128)(2,1)S(1)}, bf16[32,1152]{1,0:T(8,128)(2,1)S(1)}, u32[]{:S(2)}, u32[]{:S(2)}) collective-permute-start(bf16[32,1152]{1,0:T(8,128)(2,1)S(1)} %copy-done.68), channel_id=1, source_target_pairs={{0,3},{4,7},{8,11},{12,15},{16,19},{20,23},{24,27},{28,31}} | collective-permute-start | bytes 221192 | tf_op jit(solution)/shard_map/ppermute | solution.py:472
  231.7 49.4 %collective-permute-start.11 = (bf16[384,1152]{1,0:T(8,128)(2,1)}, bf16[384,1152]{1,0:T(8,128)(2,1)}, u32[]{:S(2)}, u32[]{:S(2)}) collective-permute-start(bf16[384,1152]{1,0:T(8,128)(2,1)} %convolution_convert_fusion.8), channel_id=1, source_target_pairs={{0,3},{1,0},{2,1},{3,2},{4,7},{5,4},{6,5},{7,6},{8,11},{9,8},{10,9... | collective-permute-start | bytes 2654216 | tf_op jit(solution)/shard_map/ppermute | solution.py:622
  238.0 75.8 %collective-permute-start.9 = (bf16[384,1152]{1,0:T(8,128)(2,1)}, bf16[384,1152]{1,0:T(8,128)(2,1)}, u32[]{:S(2)}, u32[]{:S(2)}) collective-permute-start(bf16[384,1152]{1,0:T(8,128)(2,1)} %convolution_convert_fusion.10), channel_id=1, source_target_pairs={{0,2},{1,3},{2,0},{3,1},{4,6},{5,7},{6,4},{7,5},{8,10},{9,11},{10,... | collective-permute-start | bytes 2654216 | tf_op jit(solution)/shard_map/ppermute | solution.py:622
  240.0 73.9 %collective-permute-start.7 = (bf16[384,1152]{1,0:T(8,128)(2,1)}, bf16[384,1152]{1,0:T(8,128)(2,1)}, u32[]{:S(2)}, u32[]{:S(2)}) collective-permute-start(bf16[384,1152]{1,0:T(8,128)(2,1)} %convolution_convert_fusion.12), channel_id=1, source_target_pairs={{0,1},{1,2},{2,3},{3,0},{4,5},{5,6},{6,7},{7,4},{8,9},{9,10},{10,1... | collective-permute-start | bytes 2654216 | tf_op jit(solution)/shard_map/ppermute | solution.py:622
  281.1 101.5 %collective-permute-start.17 = (bf16[384,1152]{1,0:T(8,128)(2,1)S(1)}, bf16[384,1152]{1,0:T(8,128)(2,1)S(1)}, u32[]{:S(2)}, u32[]{:S(2)}) collective-permute-start(bf16[384,1152]{1,0:T(8,128)(2,1)S(1)} %copy-done.79), channel_id=1, source_target_pairs={{0,3},{1,0},{2,1},{3,2},{4,7},{5,4},{6,5},{7,6},{8,11},{9,8},{10,9... | collective-permute-start | bytes 2654216 | tf_op jit(solution)/shard_map/ppermute | solution.py:622
  313.8 85.0 %collective-permute-start.15 = (bf16[384,1152]{1,0:T(8,128)(2,1)S(1)}, bf16[384,1152]{1,0:T(8,128)(2,1)S(1)}, u32[]{:S(2)}, u32[]{:S(2)}) collective-permute-start(bf16[384,1152]{1,0:T(8,128)(2,1)S(1)} %copy-done.78), channel_id=1, source_target_pairs={{0,2},{1,3},{2,0},{3,1},{4,6},{5,7},{6,4},{7,5},{8,10},{9,11},{10,... | collective-permute-start | bytes 2654216 | tf_op jit(solution)/shard_map/ppermute | solution.py:622
  313.8 97.7 %collective-permute-start.13 = (bf16[384,1152]{1,0:T(8,128)(2,1)S(1)}, bf16[384,1152]{1,0:T(8,128)(2,1)S(1)}, u32[]{:S(2)}, u32[]{:S(2)}) collective-permute-start(bf16[384,1152]{1,0:T(8,128)(2,1)S(1)} %convolution_convert_fusion.13), channel_id=1, source_target_pairs={{0,1},{1,2},{2,3},{3,0},{4,5},{5,6},{6,7},{7,4},{8,9},{9,10},{10,1... | collective-permute-start | bytes 2654216 | tf_op jit(solution)/shard_map/ppermute | solution.py:622
  396.4 63.6 %collective-permute-start.18 = (bf16[384,1152]{1,0:T(8,128)(2,1)}, bf16[384,1152]{1,0:T(8,128)(2,1)S(1)}, u32[]{:S(2)}, u32[]{:S(2)}) collective-permute-start(bf16[384,1152]{1,0:T(8,128)(2,1)} %fusion.135), channel_id=1, source_target_pairs={{0,1},{1,2},{2,3},{3,0},{4,5},{5,6},{6,7},{7,4},{8,9},{9,10},{10,1... | collective-permute-start | bytes 2654216 | tf_op jit(solution)/shard_map/ppermute | solution.py:622
  411.5 48.4 %collective-permute-start.16 = (bf16[384,1152]{1,0:T(8,128)(2,1)}, bf16[384,1152]{1,0:T(8,128)(2,1)S(1)}, u32[]{:S(2)}, u32[]{:S(2)}) collective-permute-start(bf16[384,1152]{1,0:T(8,128)(2,1)} %fusion.132), channel_id=1, source_target_pairs={{0,2},{1,3},{2,0},{3,1},{4,6},{5,7},{6,4},{7,5},{8,10},{9,11},{10,... | collective-permute-start | bytes 2654216 | tf_op jit(solution)/shard_map/ppermute | solution.py:622
  421.6 40.0 %collective-permute-start.14 = (bf16[384,1152]{1,0:T(8,128)(2,1)}, bf16[384,1152]{1,0:T(8,128)(2,1)S(1)}, u32[]{:S(2)}, u32[]{:S(2)}) collective-permute-start(bf16[384,1152]{1,0:T(8,128)(2,1)} %fusion.129), channel_id=1, source_target_pairs={{0,3},{1,0},{2,1},{3,2},{4,7},{5,4},{6,5},{7,6},{8,11},{9,8},{10,9... | collective-permute-start | bytes 2654216 | tf_op jit(solution)/shard_map/ppermute | solution.py:622
  469.3 189.4 %reduce-scatter.10.cloned.1.call-start = ((), (), s32[]{:S(2)}) async-start(), calls=%async_computation.8 | async-start | bytes 7962624 | tf_op jit(solution)/shard_map/reduce_scatter | solution.py:679
  469.4 37.1 %collective-permute-start.12 = (bf16[384,1152]{1,0:T(8,128)(2,1)}, bf16[384,1152]{1,0:T(8,128)(2,1)S(1)}, u32[]{:S(2)}, u32[]{:S(2)}) collective-permute-start(bf16[384,1152]{1,0:T(8,128)(2,1)} %fusion.147), channel_id=1, source_target_pairs={{0,1},{1,2},{2,3},{3,0},{4,5},{5,6},{6,7},{7,4},{8,9},{9,10},{10,1... | collective-permute-start | bytes 2654216 | tf_op jit(solution)/shard_map/ppermute | solution.py:622
  484.9 57.8 %collective-permute-start.10 = (bf16[384,1152]{1,0:T(8,128)(2,1)S(1)}, bf16[384,1152]{1,0:T(8,128)(2,1)S(1)}, u32[]{:S(2)}, u32[]{:S(2)}) collective-permute-start(bf16[384,1152]{1,0:T(8,128)(2,1)S(1)} %copy-done.74), channel_id=1, source_target_pairs={{0,2},{1,3},{2,0},{3,1},{4,6},{5,7},{6,4},{7,5},{8,10},{9,11},{10,... | collective-permute-start | bytes 2654216 | tf_op jit(solution)/shard_map/ppermute | solution.py:622
  486.2 56.6 %collective-permute-start.8 = (bf16[384,1152]{1,0:T(8,128)(2,1)S(1)}, bf16[384,1152]{1,0:T(8,128)(2,1)S(1)}, u32[]{:S(2)}, u32[]{:S(2)}) collective-permute-start(bf16[384,1152]{1,0:T(8,128)(2,1)S(1)} %copy-done.73), channel_id=1, source_target_pairs={{0,3},{1,0},{2,1},{3,2},{4,7},{5,4},{6,5},{7,6},{8,11},{9,8},{10,9... | collective-permute-start | bytes 2654216 | tf_op jit(solution)/shard_map/ppermute | solution.py:622
  569.6 205.5 %reduce-scatter.12.cloned.1.call-start = ((), (), s32[]{:S(2)}) async-start(), calls=%async_computation.9 | async-start | bytes 5971968 | tf_op jit(solution)/shard_map/reduce_scatter | solution.py:690
  605.3 51.8 %collective-permute-start.21 = (bf16[24,1152]{1,0:T(8,128)(2,1)S(1)}, bf16[24,1152]{1,0:T(8,128)(2,1)}, u32[]{:S(2)}, u32[]{:S(2)}) collective-permute-start(bf16[24,1152]{1,0:T(8,128)(2,1)S(1)} %pad_maximum_fusion.7), channel_id=1, source_target_pairs={{3,0},{7,4},{11,8},{15,12},{19,16},{23,20},{27,24},{31,28}} | collective-permute-start | bytes 165896 | tf_op jit(solution)/shard_map/ppermute | solution.py:472
  606.8 23.2 %collective-permute-start.20 = (bf16[24,1152]{1,0:T(8,128)(2,1)S(1)}, bf16[24,1152]{1,0:T(8,128)(2,1)S(1)}, u32[]{:S(2)}, u32[]{:S(2)}) collective-permute-start(bf16[24,1152]{1,0:T(8,128)(2,1)S(1)} %pad_maximum_fusion.7), channel_id=1, source_target_pairs={{2,0},{3,1},{6,4},{7,5},{10,8},{11,9},{14,12},{15,13},{18,16},{19,... | collective-permute-start | bytes 165896 | tf_op jit(solution)/shard_map/ppermute | solution.py:472
  608.1 24.1 %collective-permute-start.19 = (bf16[24,1152]{1,0:T(8,128)(2,1)S(1)}, bf16[24,1152]{1,0:T(8,128)(2,1)S(1)}, u32[]{:S(2)}, u32[]{:S(2)}) collective-permute-start(bf16[24,1152]{1,0:T(8,128)(2,1)S(1)} %pad_maximum_fusion.7), channel_id=1, source_target_pairs={{1,0},{2,1},{3,2},{5,4},{6,5},{7,6},{9,8},{10,9},{11,10},{13,12},{... | collective-permute-start | bytes 165896 | tf_op jit(solution)/shard_map/ppermute | solution.py:472
  627.4 29.7 %collective-permute-start.24 = (bf16[24,1152]{1,0:T(8,128)(2,1)S(1)}, bf16[24,1152]{1,0:T(8,128)(2,1)S(1)}, u32[]{:S(2)}, u32[]{:S(2)}) collective-permute-start(bf16[24,1152]{1,0:T(8,128)(2,1)S(1)} %pad_maximum_fusion.8), channel_id=1, source_target_pairs={{3,0},{7,4},{11,8},{15,12},{19,16},{23,20},{27,24},{31,28}} | collective-permute-start | bytes 165896 | tf_op jit(solution)/shard_map/ppermute | solution.py:472
  628.7 25.3 %collective-permute-start.22 = (bf16[24,1152]{1,0:T(8,128)(2,1)S(1)}, bf16[24,1152]{1,0:T(8,128)(2,1)S(1)}, u32[]{:S(2)}, u32[]{:S(2)}) collective-permute-start(bf16[24,1152]{1,0:T(8,128)(2,1)S(1)} %pad_maximum_fusion.8), channel_id=1, source_target_pairs={{1,0},{2,1},{3,2},{5,4},{6,5},{7,6},{9,8},{10,9},{11,10},{13,12},{... | collective-permute-start | bytes 165896 | tf_op jit(solution)/shard_map/ppermute | solution.py:472
  630.0 27.1 %collective-permute-start.23 = (bf16[24,1152]{1,0:T(8,128)(2,1)S(1)}, bf16[24,1152]{1,0:T(8,128)(2,1)S(1)}, u32[]{:S(2)}, u32[]{:S(2)}) collective-permute-start(bf16[24,1152]{1,0:T(8,128)(2,1)S(1)} %pad_maximum_fusion.8), channel_id=1, source_target_pairs={{2,0},{3,1},{6,4},{7,5},{10,8},{11,9},{14,12},{15,13},{18,16},{19,... | collective-permute-start | bytes 165896 | tf_op jit(solution)/shard_map/ppermute | solution.py:472
  658.7 166.8 %all-reduce.11.cloned.1.call-start = ((), (), s32[]{:S(2)}) async-start(), calls=%async_computation.10 | async-start | bytes 1327104 | tf_op jit(solution)/shard_map/psum | solution.py:696
  785.4 80.1 %reduce-scatter.16.cloned.1.call-start = ((), (), s32[]{:S(2)}) async-start(), calls=%async_computation.14 | async-start | bytes 1327104
  827.9 123.6 %reduce-scatter.14.cloned.1.call-start = ((), (), s32[]{:S(2)}) async-start(), calls=%async_computation.11 | async-start | bytes 11943936 | tf_op jit(solution)/shard_map/reduce_scatter | solution.py:718
  867.3 155.7 %all-reduce.13.cloned.1.call-start = ((), (), s32[]{:S(2)}) async-start(), calls=%async_computation.15 | async-start | bytes 2973696 | tf_op jit(solution)/shard_map/psum | solution.py:719
  (95 other events, 2193.5 us)
Sparse Core Ops, SparseCore 0:
  9.9 69.2 all-gather.6
  81.1 41.6 all-gather.8
  124.7 49.1 all-gather.10
  175.7 49.7 all-gather.12
  469.4 79.8 reduce-scatter.7
  569.8 85.1 reduce-scatter.9
  658.8 56.3 reduce-scatter.11
  785.5 39.9 all-reduce.10
  829.3 36.1 reduce-scatter.15
  869.3 82.0 reduce-scatter.13
  954.6 68.2 all-reduce.12

commit v3 on v2

--- a/solution.py
+++ b/solution.py
@@ -514,6 +514,38 @@
     return jnp.pad(whole, ((0, -whole.shape[0] % 16), (0, 0)))
 
 
+def expert_sum(*arrays):
+    n, here = lax.axis_size("expert"), lax.axis_index("expert")
+    split = [x.reshape(n, x.shape[0] // n, x.shape[1]) for x in arrays]
+    padded = [jnp.pad(x, ((0, 0), (0, -x.shape[1] % 8), (0, 0))) for x in split]
+    parts = jnp.concatenate(padded, axis=1) if len(padded) > 1 else padded[0]
+    moved = lambda x, k: lax.ppermute(x, "expert", [(i, (i + k) % n) for i in range(n)])
+    part = lambda k: lax.dynamic_index_in_dim(parts, jnp.mod(here + k, n), 0, keepdims=False)
+    total = part(0).astype(F32)
+    for x in [moved(part(k), k) for k in range(1, n)]:
+        total = total + x.astype(F32)
+    total = total.astype(BF16)
+    came = [total] + [moved(total, k) for k in range(1, n)]
+    twice = jnp.stack(came[::-1] * 2)
+    every = lax.dynamic_slice_in_dim(twice, n - 1 - here, n, 0)
+    out, at = [], 0
+    for x, p in zip(split, padded):
+        out.append(every[:, at : at + x.shape[1]].reshape(n * x.shape[1], x.shape[2]))
+        at += p.shape[1]
+    return out
+
+
+def shares(rows, devices):
+    r, columns = rows.shape
+    return rows.reshape(r, devices, columns // devices).transpose(1, 0, 2).reshape(devices, -1)
+
+
+def halved(grads, devices):
+    rows, columns = grads.shape
+    split = grads.reshape(devices // 2, 2, rows // devices, columns)
+    return split.transpose(1, 0, 2, 3).reshape(devices, rows // devices, columns)
+
+
 def cut(whole, counts):
     out, at = [], 0
     for n in counts:
@@ -555,7 +587,8 @@
     before = (jnp.arange(rows)[:, None] > jnp.arange(rows)[None, :]).astype(BF16)
     ranks = dot(before, chosen.astype(BF16))
     slot = jnp.sum(ranks * chosen, axis=1).astype(jnp.int32)
-    distance = jnp.mod(route - lax.axis_index("expert"), groups)
+    assert groups & (groups - 1) == 0
+    distance = jnp.bitwise_xor(route, lax.axis_index("expert"))
     target = jnp.where(slot < capacity, distance * capacity + slot, groups * capacity)
     place = (jnp.arange(groups * capacity)[:, None] == target[None, :]).astype(BF16)
 
@@ -618,28 +651,35 @@
     grad_out = cotangent.astype(F32)
     grad_picked = (gate_value[:, None] * grad_out).astype(BF16)
 
-    def moved(x, by):
-        return lax.ppermute(x, "expert", [(i, (i + by) % groups) for i in range(groups)]) if by else x
+    def swapped(x, k):
+        return lax.ppermute(x, "expert", [(i, i ^ k) for i in range(groups)]) if k else x
 
     places = [place[k * capacity : (k + 1) * capacity] for k in range(groups)]
     norm_two_low = norm_two.astype(BF16)
-    arrived = [moved(dot(m, norm_two_low).astype(BF16), k) for k, m in enumerate(places)]
-    grad_arrived = []
-    for k, m in enumerate(places):
-        sent = dot(m, grad_picked).astype(BF16)
+    arrived, grad_arrived = [None] * groups, [None] * groups
+    far_first = list(range(groups - 1, 0, -1))
+    for k in far_first + [0]:
+        arrived[k] = swapped(dot(places[k], norm_two_low).astype(BF16), k)
+    for k in far_first + [0]:
+        sent = dot(places[k], grad_picked).astype(BF16)
         if k:
             sent, arrived[k] = lax.optimization_barrier((sent, arrived[k]))
-        grad_arrived.append(moved(sent, k))
-    up_low, grad_pre, outs, ins = [], [], [], []
-    for k in range(groups):
+        grad_arrived[k] = swapped(sent, k)
+    up_low, grad_pre, outs, ins = ([None] * groups for _ in range(4))
+    for k in [0] + far_first:
         up_pre = dot(arrived[k], w_up)
         act, gelu_back = jax.vjp(jax.nn.gelu, up_pre)
-        up_low.append(act.astype(BF16))
-        outs.append(dot(up_low[k], w_down).astype(BF16))
-        grad_pre.append(gelu_back(product_back(grad_arrived[k], w_down))[0].astype(BF16))
-        ins.append(product_back(grad_pre[k], w_up).astype(BF16))
-    returned = jnp.concatenate([moved(x, -k) for k, x in enumerate(outs)])
-    grad_sent = jnp.concatenate([moved(x, -k) for k, x in enumerate(ins)])
+        up_low[k] = act.astype(BF16)
+        outs[k] = dot(up_low[k], w_down).astype(BF16)
+        grad_pre[k] = gelu_back(product_back(grad_arrived[k], w_down))[0].astype(BF16)
+        ins[k] = product_back(grad_pre[k], w_up).astype(BF16)
+    returned = [None] * groups
+    grad_sent = [None] * groups
+    for k in far_first + [0]:
+        returned[k] = swapped(outs[k], k)
+    for k in far_first + [0]:
+        grad_sent[k] = swapped(ins[k], k)
+    returned, grad_sent = jnp.concatenate(returned), jnp.concatenate(grad_sent)
     up_low, grad_pre, arrived, grad_arrived, _, _ = lax.optimization_barrier(
         (up_low, grad_pre, arrived, grad_arrived, outs, ins)
     )
@@ -647,6 +687,7 @@
     grad_down = contract(jnp.concatenate(up_low), jnp.concatenate(grad_arrived)).astype(BF16)
     grad_sent, grad_up, grad_down = lax.optimization_barrier((grad_sent, grad_up, grad_down))
     sum_up = lax.psum_scatter(grad_up, "dp", scatter_dimension=0, tiled=True)
+    sum_down = lax.psum_scatter(grad_down, "dp", scatter_dimension=0, tiled=True)
 
     picked = contract(place, returned)
     output = (hidden_one + gate_value[:, None] * picked).astype(BF16)
@@ -675,8 +716,7 @@
     sigma = jax.nn.sigmoid(gate_f)
     grad_scanned = grad_gated * (gate_f * sigma)
     grad_gate_in = (grad_gated * scanned.astype(F32) * (sigma * (1.0 + gate_f * (1.0 - sigma)))).astype(BF16)
-    grad_scanned, sum_up, grad_down = lax.optimization_barrier((grad_scanned, sum_up, grad_down))
-    sum_down = lax.psum_scatter(grad_down, "dp", scatter_dimension=0, tiled=True)
+    grad_scanned, sum_up = lax.optimization_barrier((grad_scanned, sum_up))
     later_grad = []
     for part in range(HALVES):
         rate_part = rate2[:, part * width // HALVES : (part + 1) * width // HALVES]
@@ -684,16 +724,18 @@
         start = jnp.concatenate([start, own_sums[part]])
         came = [shifted(start, "expert", -hop) for hop in hops]
         later_grad.append(entering([c[:states] for c in came], [total(c[states:]) for c in came], rate_part))
-    later_grad, sum_down, grad_output_w = lax.optimization_barrier(
-        (jnp.concatenate(later_grad, 1), sum_down, grad_output_w.astype(BF16))
+    grad_input_z = halved(contract(grad_gate_in, norm_own).astype(BF16), devices).reshape(width, model)
+    grad_norm_z = product_back(grad_gate_in, w_input[:, width:])
+    later_grad, sum_down, grad_output_w, grad_input_z, grad_norm_z = lax.optimization_barrier(
+        (jnp.concatenate(later_grad, 1), sum_down, grad_output_w.astype(BF16), grad_input_z, grad_norm_z)
     )
     sum_output = lax.psum_scatter(grad_output_w, "dp", scatter_dimension=0, tiled=True)
+    sum_input_z = lax.psum_scatter(grad_input_z, "dp", scatter_dimension=0, tiled=True)
     grad_pre_step, grad_inner, grad_decay_t, grad_skip, grad_b, grad_c = backward_scan(
         step_low, w_step, bias2, st, inner_low, grad_scanned, rate2, skip2,
         c_wide, b_block, one_block, history, marks, later_grad,
     )
-    grad_pre_step, sum_output = lax.optimization_barrier((grad_pre_step, sum_output))
-    sum_output = lax.psum(sum_output, "expert")
+    grad_pre_step, sum_output, sum_input_z = lax.optimization_barrier((grad_pre_step, sum_output, sum_input_z))
     grad_step_bias = jnp.sum(grad_pre_step.astype(F32), axis=0, keepdims=True)
     grad_step_w = contract(step_low, grad_pre_step)
     grad_step_low = product_back(grad_pre_step, w_step).astype(BF16)
@@ -707,34 +749,48 @@
             paired_rows(jnp.concatenate([grad_ffn_gain[None], grad_ffn_gain[None], grad_router], 0), devices),
         ]
     )
+    share, norm_share = width // devices, model // devices
+    summed_shape = (summed.shape[0], share)
+    summed = shares(summed, devices)
+    grad_inner, summed = lax.optimization_barrier((grad_inner, summed))
     grad_conv_in, grad_kernel, grad_conv_b = conv_back(
         mixed, grad_inner, slope_low, grad_selected, w_select, w_conv, ok
     )
-    grad_conv_in, summed, sum_output = lax.optimization_barrier((grad_conv_in, summed, sum_output))
-    summed = lax.psum_scatter(summed, "dp", scatter_dimension=1, tiled=True)
-    grad_mixed = jnp.concatenate([grad_conv_in, jnp.pad(grad_gate_in, ((PAD, 0), (0, 0)))], 1)
-    grad_input_w = contract(grad_mixed, norm_low).astype(BF16)
-    grad_input_w, grad_mixed, summed = lax.optimization_barrier((grad_input_w, grad_mixed, summed))
-    sum_input = lax.psum_scatter(grad_input_w, "dp", scatter_dimension=0, tiled=True)
-    sum_input, summed = lax.psum((sum_input, summed), "expert")
-    summed = summed.astype(F32)
-    grad_norm_one = product_back(grad_mixed, w_input)
-    returned_edge = shifted(grad_norm_one[PAD - taps + 1 : PAD], "expert", -1) * edge_keep
-    grad_norm_one = grad_norm_one[PAD:] + jnp.pad(returned_edge, ((rows - taps + 1, 0), (0, 0)))
+    grad_norm_x = product_back(grad_conv_in, w_input[:, :width])
+    returned_edge = shifted(grad_norm_x[PAD - taps + 1 : PAD], "expert", -1) * edge_keep
+    grad_norm_one = grad_norm_x[PAD:] + grad_norm_z + jnp.pad(returned_edge, ((rows - taps + 1, 0), (0, 0)))
     grad_norm_gain = jnp.sum(grad_norm_one * hidden_in * norm_r, axis=0, keepdims=True)
+    grad_input_x = halved(contract(grad_conv_in, norm_low).astype(BF16), devices)
+    tiny = jnp.concatenate([shares(jnp.concatenate([grad_kernel, grad_conv_b]), devices), shares(grad_norm_gain, devices)], 1)
+    rest = jnp.concatenate([summed, tiny.astype(BF16)], 1)
+    more = -(-rest.shape[1] // model)
+    more += -(more + share) % (8 * groups)
+    rest = jnp.pad(rest, ((0, 0), (0, more * model - rest.shape[1]))).reshape(devices, more, model)
+    packed = jnp.concatenate([grad_input_x, rest], axis=1).reshape(devices * (share + more), model)
+    packed, sum_output, sum_input_z = lax.optimization_barrier((packed, sum_output, sum_input_z))
+    packed = lax.psum_scatter(packed, "dp", scatter_dimension=0, tiled=True)
+    sum_output, sum_input_z = expert_sum(sum_output, sum_input_z)
     scaled_one = norm_f * grad_norm_one
     grad_tokens = (
         grad_hidden
         + norm_r * scaled_one
         - hidden_in * (norm_r * norm_r * norm_r) * jnp.mean(hidden_in * scaled_one, axis=-1, keepdims=True)
     ).astype(BF16)
-    tiny = jnp.concatenate([grad_kernel, grad_conv_b, jnp.pad(grad_norm_gain, ((0, 0), (0, width - model)))])
-    tiny = lax.psum(tiny, ("dp", "expert"))
-    here = lax.axis_index("dp")
-    share, model_share = width // devices, model // devices
-    own = lax.dynamic_slice(tiny, (0, here * share), (taps + 1, share))
-    sum_kernel, sum_conv_b = own[:taps], own[taps]
-    sum_norm = lax.dynamic_slice(tiny, (taps + 1, here * model_share), (1, model_share))[0]
+    packed, sum_output, sum_input_z, grad_tokens = lax.optimization_barrier((packed, sum_output, sum_input_z, grad_tokens))
+    (packed,) = expert_sum(packed)
+    sum_input_x, tiny = packed[:share], packed[share:].astype(F32).reshape(-1)
+    summed = tiny[: summed_shape[0] * share].reshape(summed_shape)
+    tiny = tiny[summed_shape[0] * share :]
+    half = devices // 2
+    low = lax.axis_index("dp") < half
+    other = lax.ppermute(
+        jnp.where(low, sum_input_z, sum_input_x), "dp", [(i, (i + half) % devices) for i in range(devices)]
+    )
+    own_half = jnp.where(low, sum_input_x, sum_input_z)
+    sum_input = jnp.concatenate([jnp.where(low, own_half, other), jnp.where(low, other, own_half)])
+    sum_kernel = tiny[: taps * share].reshape(taps, share)
+    sum_conv_b = tiny[taps * share : (taps + 1) * share]
+    sum_norm = tiny[(taps + 1) * share : (taps + 1) * share + norm_share]
     sum_select, sum_step, sum_decay, sum_step_b, sum_skip, singles = cut(
         summed, (w_select.shape[0], rank, states, 1, 1, (groups + 2) // 2)
     )

time: 1050 us -> 1010 us (0.962)
  blocking collectives: 61.4 us -> 16.8 us
  starting transfers between devices: 96.4 us -> 65.7 us
  waiting for transfers between devices: 239 us -> 255 us
    ppermute x12 -> x25, waiting for transfers between devices: 85.4 us -> 225 us  [the longest x12 141 us: swapped(): lax.ppermute(x, 'expert', [(i, i ^ k) for i in range(groups)])]
    reduce_scatter x1 -> x2, waiting for transfers between devices: 60.1 us -> 0.04 us  [the longest x1 0.02 us: body(): packed = lax.psum_scatter(packed, 'dp', scatter_dimension=0, tiled=True)]
    psum x1 -> x0, blocking collectives: 44.1 us -> none  [body(): tiny = lax.psum(tiny, ('dp', 'expert'))]
    ppermute x12 -> x25, starting transfers between devices: 69.4 us -> 38.8 us  [the longest x12 21.4 us: swapped(): lax.ppermute(x, 'expert', [(i, i ^ k) for i in range(groups)])]
    psum x2 -> x0, waiting for transfers between devices: 28.5 us -> none  [the longest x1 20.5 us: body(): sum_input, summed = lax.psum((sum_input, summed), 'expert')]
    ppermute x14, waiting for transfers between devices: 30.8 us -> 9.27 us  [shifted(): return lax.ppermute(array, axis, pairs)]
    unnamed x12 -> x9, waiting for transfers between devices: 16.5 us -> 2.84 us
    reshape x0 -> x10, local copies, waits for them, and re-layouts: none -> 12.9 us  [the longest x2 8.34 us: halved(): split = grads.reshape(devices // 2, 2, rows // devices, columns)]
  transfers between devices with their start and end apart: 37 -> 48, of which waited for: 15 -> 17; matrix products, arithmetic and copies ran while one was open for 35% -> 35% of each run, Pallas kernels for 22% -> 21%
where the time goes in v3:
time: 1010 us; the launch traced here: 998 us
  waiting for transfers between devices  255 us (25%)
  matrix products  239 us (24%)
  Pallas kernels  227 us (22%)
  local copies, waits for them, and re-layouts  93.1 us (9%)
  other arithmetic  83.4 us (8%)
  starting transfers between devices  65.7 us (7%)
  between operations  17.2 us (2%)
  blocking collectives  16.8 us (2%)
    ppermute x12, waiting for transfers between devices, swapped(): lax.ppermute(x, 'expert', [(i, i ^ k) for i in range(groups)])  141 us
    pallas_call x1, Pallas kernels, backward_scan(): pl.pallas_call(backward_kernel, grid=k.grid, in_specs=[k.token(s.shape[1]...  96.4 us
    dot_general x19, matrix products, dot(): return jnp.dot(a, b, preferred_element_type=F32)  83.2 us
    dot_general x13, matrix products, product_back(): lax.dot_general(left, right, (((1,), (1,)), ((), ())), preferred_element_...  76.4 us
    ppermute x12, waiting for transfers between devices, expert_sum(): lax.ppermute(x, 'expert', [(i, (i + k) % n) for i in range(n)])  74.4 us
    dot_general x9, matrix products, contract(): lax.dot_general(left, right, (((0,), (0,)), ((), ())), preferred_element_...  71.1 us
    pallas_call x1, Pallas kernels, forward_scan(): pl.pallas_call(forward_kernel, grid=k.grid, in_specs=[k.token(s.shape[1])...  42.7 us
    pallas_call x2, Pallas kernels, end_states(): pl.pallas_call(end_kernel, grid=k.grid, in_specs=[k.token(s.shape[1]), k....  35.7 us
  transfers between devices with their start and end apart: 48, of which 17 were waited for; matrix products, arithmetic and copies ran while one was open for 35% of the time, Pallas kernels for 21%

profile of v3, /device:TPU:4, one launch (start us, length us, event | category | flops | bytes accessed | tf_op | source)
XLA Modules:
  0.0 997.5 jit_solution(357529144260977556)
XLA Ops:
  17.0 16.8 %all_gather.15 = bf16[208,2304]{0,1:T(8,128)(2,1)S(1)} all-gather(bf16[208,288]{0,1:T(8,128)(2,1)S(1)} %pad.21), channel_id=1, replica_groups=mesh['dp'=8,'expert'=4] {'dp'}, dimensions={1}, use_global_device_ids=true | all-gather | bytes 1078272 | tf_op jit(solution)/shard_map/all_gather | solution.py:575
  60.5 18.2 %all-gather.7.cloned.1.call-done = bf16[1152,4608]{0,1:T(8,128)(2,1)} async-done(((bf16[1152,576]{0,1:T(8,128)(2,1)}), bf16[1152,4608]{0,1:T(8,128)(2,1)}) %all-gather.7.cloned.1.call-update) | async-done | bytes 10616848 | tf_op jit(solution)/shard_map/all_gather | solution.py:566
  78.7 13.1 %convolution_convert_fusion.5.xs_ref = bf16[784,4608]{1,0:T(8,128)(2,1)S(1)} fusion(bf16[1152,4608]{0,1:T(8,128)(2,1)} %all-gather.7.cloned.1.call-done, bf16[768,1152]{1,0:T(8,128)(2,1)} %copy-done.22, bf16[3,1152]{1,0:T(4,128)(2,1)} %collective-permute-done, bf16[784]{0:T(1024)(128)(2,1)S(1)} %pad.78.clone), kind=kOutput, calls=%fused_computation.22 | convolution fusion | flops 8332627968 | bytes 19620128 | tf_op jit(solution)/shard_map/dot_general | solution.py:35
  91.9 8.1 multiply_convert_fusion
  116.4 17.7 %end_states.2 = bf16[32,1152]{1,0:T(8,128)(2,1)} custom-call(bf16[768,72]{1,0:T(8,128)(2,1)} %copy.169.s_ref, bf16[72,2304]{1,0:T(8,128)(2,1)} %copy.170.w_ref, bf16[1,2304]{1,0:T(2,128)(2,1)} %copy.171.b_ref, f32[768,1]{1,0:T(8,128)} %broadcast_in_dim.164.st_ref, bf16[768,2304]{1,0:T(8,128)(2,1)} %copy-done.3, f32[16,2304]{1,0:T(8,128)} %negate_multiply_fusion.a_ref, ...), custom_call_target="tpu_custom_call" | custom-call | flops 84934656 | bytes 7077888 | tf_op jit(solution)/shard_map/end_states/pallas_call | solution.py:387
  150.3 17.9 %end_states.3 = bf16[32,1152]{1,0:T(8,128)(2,1)} custom-call(bf16[768,72]{1,0:T(8,128)(2,1)} %copy.169.s_ref, bf16[72,2304]{1,0:T(8,128)(2,1)} %copy.170.w_ref, bf16[1,2304]{1,0:T(2,128)(2,1)} %copy.171.b_ref, f32[768,1]{1,0:T(8,128)} %broadcast_in_dim.164.st_ref, bf16[768,2304]{1,0:T(8,128)(2,1)} %copy-done.3, f32[16,2304]{1,0:T(8,128)} %negate_multiply_fusion.a_ref, ...), custom_call_target="tpu_custom_call" | custom-call | flops 84934656 | bytes 7077888 | tf_op jit(solution)/shard_map/end_states/pallas_call | solution.py:387
  176.1 42.7 %forward_scan.1 = (bf16[768,2304]{1,0:T(8,128)(2,1)}, bf16[768,2304]{1,0:T(8,128)(2,1)}, bf16[12288,2304]{1,0:T(8,128)(2,1)}, bf16[48,16,2304]{2,1,0:T(8,128)(2,1)}) custom-call(bf16[768,72]{1,0:T(8,128)(2,1)} %copy.169.s_ref, bf16[72,2304]{1,0:T(8,128)(2,1)} %copy.170.w_ref, bf16[1,2304]{1,0:T(2,128)(2,1)} %copy.171.b_ref, ...), custom_call_target="tpu_custom_call" | custom-call | flops 254803968 | bytes 77856768 | tf_op jit(solution)/shard_map/forward_scan/pallas_call | solution.py:403
  218.8 8.5 multiply_reduce_fusion.2
  251.0 10.1 %multiply_convert_fusion.5 = (bf16[384,3072]{1,0:T(8,128)(2,1)}, f32[384,3072]{1,0:T(8,128)}) fusion(bf16[384,1152]{1,0:T(8,128)(2,1)} %convolution_convert_fusion.15, bf16[1,1152,3072]{2,1,0:T(8,128)(2,1)} %all-gather.11.cloned.1.call-done), kind=kOutput, calls=%fused_computation.120 | convolution fusion | flops 2728525824 | bytes 15040512 | tf_op jit(solution)/shard_map/dot_general | solution.py:35
  261.1 8.6 fusion.64
  283.7 47.0 %collective-permute-done.9 = bf16[384,1152]{1,0:T(8,128)(2,1)} collective-permute-done((bf16[384,1152]{1,0:T(8,128)(2,1)}, bf16[384,1152]{1,0:T(8,128)(2,1)}, u32[]{:S(2)}, u32[]{:S(2)}) %collective-permute-start.9) | collective-permute-done | bytes 884768 | tf_op jit(solution)/shard_map/ppermute | solution.py:655
  334.5 7.3 multiply_convert_fusion.2
  367.5 7.3 fusion.85
  380.9 25.5 %collective-permute-done.15 = bf16[384,1152]{1,0:T(8,128)(2,1)S(1)} collective-permute-done((bf16[384,1152]{1,0:T(8,128)(2,1)S(1)}, bf16[384,1152]{1,0:T(8,128)(2,1)S(1)}, u32[]{:S(2)}, u32[]{:S(2)}) %collective-permute-start.15) | collective-permute-done | bytes 884768 | tf_op jit(solution)/shard_map/ppermute | solution.py:655
  433.0 17.7 %convolution_convert_fusion.4 = bf16[3072,1152]{1,0:T(8,128)(2,1)} fusion(bf16[384,3072]{1,0:T(8,128)(2,1)} %copy-done.84, bf16[384,3072]{1,0:T(8,128)(2,1)} %fusion.78, bf16[384,3072]{1,0:T(8,128)(2,1)} %copy-done.85, bf16[384,3072]{1,0:T(8,128)(2,1)} %copy-done.83, bf16[384,1152]{1,0:T(8,128)(2,1)} %collective-permute-done.11, ...), kind=kOutput, calls=%fused_computation.4 | convolution fusion | flops 10927079424 | bytes 20054016 | tf_op jit(solution)/shard_map/dot_general | solution.py:488
  450.8 18.4 %convolution_convert_fusion.3 = bf16[3072,1152]{1,0:T(8,128)(2,1)} fusion(bf16[384,3072]{1,0:T(8,128)(2,1)} %copy-done.87, bf16[384,3072]{1,0:T(8,128)(2,1)} %copy-done.88, bf16[384,3072]{1,0:T(8,128)(2,1)} %copy-done.89, bf16[384,3072]{1,0:T(8,128)(2,1)} %get-tuple-element.88, bf16[384,1152]{1,0:T(8,128)(2,1)} %copy-done.77, ...), kind=kOutput, calls=%fused_computation.3 | convolution fusion | flops 10927079424 | bytes 20054016 | tf_op jit(solution)/shard_map/dot_general | solution.py:488
  469.8 7.7 pad_maximum_fusion.1
  484.9 17.6 %collective-permute-done.12 = bf16[384,1152]{1,0:T(8,128)(2,1)} collective-permute-done((bf16[384,1152]{1,0:T(8,128)(2,1)}, bf16[384,1152]{1,0:T(8,128)(2,1)}, u32[]{:S(2)}, u32[]{:S(2)}) %collective-permute-start.12) | collective-permute-done | bytes 884768 | tf_op jit(solution)/shard_map/ppermute | solution.py:655
  502.4 50.7 %collective-permute-done.10 = bf16[384,1152]{1,0:T(8,128)(2,1)} collective-permute-done((bf16[384,1152]{1,0:T(8,128)(2,1)S(1)}, bf16[384,1152]{1,0:T(8,128)(2,1)}, u32[]{:S(2)}, u32[]{:S(2)}) %collective-permute-start.10) | collective-permute-done | bytes 884768 | tf_op jit(solution)/shard_map/ppermute | solution.py:655
  574.2 7.4 fusion.21
  597.0 10.7 %fusion.56 = f32[768,1152]{1,0:T(8,128)} fusion(bf16[768,2304]{1,0:T(8,128)(2,1)} %copy-done.15, bf16[1152,4608]{0,1:T(8,128)(2,1)} %all-gather.7.cloned.1.call-done), kind=kOutput, calls=%fused_computation.84 | convolution fusion | flops 4076863488 | bytes 12386304 | tf_op jit(solution)/shard_map/dot_general | solution.py:484
  612.7 17.0 %start_grads.2 = bf16[16,1152]{1,0:T(8,128)(2,1)} custom-call(bf16[768,72]{1,0:T(8,128)(2,1)} %copy.169.s_ref, bf16[72,2304]{1,0:T(8,128)(2,1)} %copy.170.w_ref, bf16[1,2304]{1,0:T(2,128)(2,1)} %copy.171.b_ref, f32[768,1]{1,0:T(8,128)} %broadcast_in_dim.164.st_ref, f32[768,2304]{1,0:T(8,128)} %get-tuple-element.98.dy_ref, ...), custom_call_target="tpu_custom_call" | custom-call | flops 84934656 | bytes 7077888 | tf_op jit(solution)/shard_map/start_grads/pallas_call | solution.py:421
  634.7 17.0 %start_grads.3 = bf16[16,1152]{1,0:T(8,128)(2,1)} custom-call(bf16[768,72]{1,0:T(8,128)(2,1)} %copy.169.s_ref, bf16[72,2304]{1,0:T(8,128)(2,1)} %copy.170.w_ref, bf16[1,2304]{1,0:T(2,128)(2,1)} %copy.171.b_ref, f32[768,1]{1,0:T(8,128)} %broadcast_in_dim.164.st_ref, f32[768,2304]{1,0:T(8,128)} %get-tuple-element.98.dy_ref, ...), custom_call_target="tpu_custom_call" | custom-call | flops 84934656 | bytes 7077888 | tf_op jit(solution)/shard_map/start_grads/pallas_call | solution.py:421
  680.8 96.4 %backward_scan.1 = (bf16[768,2304]{1,0:T(8,128)(2,1)}, f32[768,2304]{1,0:T(8,128)}, f32[16,2304]{1,0:T(8,128)}, f32[1,2304]{1,0:T(1,128)}, bf16[768,128]{1,0:T(8,128)(2,1)}, /*index=5*/f32[48,8,256]{2,1,0:T(8,128)}) custom-call(bf16[768,72]{1,0:T(8,128)(2,1)} %copy.169.s_ref, bf16[72,2304]{1,0:T(8,128)(2,1)} %copy.170.w_ref, bf16[1,2304]{1,0:T(2,128)(2,1)} %copy.171.b_ref, ...), custom_call_target="tpu_custom_call" | custom-call | flops 509607936 | bytes 77856768 | tf_op jit(solution)/shard_map/backward_scan/pallas_call | solution.py:438
  805.1 18.6 %conv_back.1 = (bf16[784,2304]{1,0:T(8,128)(2,1)}, f32[4,2304]{1,0:T(4,128)}, f32[1,2304]{1,0:T(1,128)}) custom-call(bf16[784,4608]{1,0:T(8,128)(2,1)} %copy-done, f32[768,2304]{1,0:T(8,128)} %get-tuple-element.113.du_ref, bf16[768,2304]{1,0:T(8,128)(2,1)} %get-tuple-element.231.slope_ref, bf16[768,104]{1,0:T(8,128)(2,1)} %copy-done.25, ...), custom_call_target="tpu_custom_call" | custom-call | flops 530841600 | bytes 14155776 | tf_op jit(solution)/shard_map/conv_back/pallas_call | solution.py:321
  825.2 8.6 fusion.54
  835.1 8.9 convolution_convert_fusion
  876.9 19.9 %collective-permute-done.27 = bf16[144,1152]{1,0:T(8,128)(2,1)} collective-permute-done((bf16[144,1152]{1,0:T(8,128)(2,1)}, bf16[144,1152]{1,0:T(8,128)(2,1)}, u32[]{:S(2)}, u32[]{:S(2)}) %collective-permute-start.27) | collective-permute-done | bytes 331808 | tf_op jit(solution)/shard_map/ppermute | solution.py:522
  907.5 21.7 %collective-permute-done.30 = bf16[144,1152]{1,0:T(8,128)(2,1)S(1)} collective-permute-done((bf16[144,1152]{1,0:T(8,128)(2,1)S(1)}, bf16[144,1152]{1,0:T(8,128)(2,1)S(1)}, u32[]{:S(2)}, u32[]{:S(2)}) %collective-permute-start.30) | collective-permute-done | bytes 331808 | tf_op jit(solution)/shard_map/ppermute | solution.py:522
  938.1 12.2 %collective-permute-done.33 = bf16[88,1152]{1,0:T(8,128)(2,1)} collective-permute-done((bf16[88,1152]{1,0:T(8,128)(2,1)}, bf16[88,1152]{1,0:T(8,128)(2,1)}, u32[]{:S(2)}, u32[]{:S(2)}) %collective-permute-start.33) | collective-permute-done | bytes 202784 | tf_op jit(solution)/shard_map/ppermute | solution.py:522
  959.1 12.6 %collective-permute-done.36 = bf16[88,1152]{1,0:T(8,128)(2,1)S(1)} collective-permute-done((bf16[88,1152]{1,0:T(8,128)(2,1)S(1)}, bf16[88,1152]{1,0:T(8,128)(2,1)S(1)}, u32[]{:S(2)}, u32[]{:S(2)}) %collective-permute-start.36) | collective-permute-done | bytes 202784 | tf_op jit(solution)/shard_map/ppermute | solution.py:522
  980.0 8.9 collective-permute-done.38
  (494 shorter events, 359.3 us)
Async XLA Ops:
  7.2 71.5 %all-gather.7.cloned.1.call-start = ((), (), s32[]{:S(2)}) async-start(), calls=%async_computation.5 | async-start | bytes 11943936 | tf_op jit(solution)/shard_map/all_gather | solution.py:566
  7.9 210.9 %all-gather.9.cloned.1.call-start = ((), (), s32[]{:S(2)}) async-start(), calls=%async_computation.6 | async-start | bytes 5971968 | tf_op jit(solution)/shard_map/all_gather | solution.py:579
  8.7 242.3 %all-gather.11.cloned.1.call-start = ((), (), s32[]{:S(2)}) async-start(), calls=%async_computation.12 | async-start | bytes 7962624 | tf_op jit(solution)/shard_map/all_gather | solution.py:580
  9.4 251.7 %all-gather.13.cloned.1.call-start = ((), (), s32[]{:S(2)}) async-start(), calls=%async_computation.13 | async-start | bytes 7962624 | tf_op jit(solution)/shard_map/all_gather | solution.py:581
  46.3 561.4 %reduce-scatter.6.cloned.1.call-start = ((), (), s32[]{:S(2)}) async-start(), calls=%async_computation.7 | async-start | bytes 7962624 | tf_op jit(solution)/shard_map/reduce_scatter | solution.py:689
  134.1 36.8 %collective-permute-start.2 = (bf16[32,1152]{1,0:T(8,128)(2,1)}, bf16[32,1152]{1,0:T(8,128)(2,1)S(1)}, u32[]{:S(2)}, u32[]{:S(2)}) collective-permute-start(bf16[32,1152]{1,0:T(8,128)(2,1)} %end_states.2), channel_id=1, source_target_pairs={{0,2},{1,3},{4,6},{5,7},{8,10},{9,11},{12,14},{13,15},{16,18},{17,... | collective-permute-start | bytes 221192 | tf_op jit(solution)/shard_map/ppermute | solution.py:472
  138.4 33.8 %collective-permute-start.1 = (bf16[32,1152]{1,0:T(8,128)(2,1)}, bf16[32,1152]{1,0:T(8,128)(2,1)S(1)}, u32[]{:S(2)}, u32[]{:S(2)}) collective-permute-start(bf16[32,1152]{1,0:T(8,128)(2,1)} %end_states.2), channel_id=1, source_target_pairs={{0,1},{1,2},{2,3},{4,5},{5,6},{6,7},{8,9},{9,10},{10,11},{12,13},{... | collective-permute-start | bytes 221192 | tf_op jit(solution)/shard_map/ppermute | solution.py:472
  148.9 26.4 %collective-permute-start.3 = (bf16[32,1152]{1,0:T(8,128)(2,1)S(1)}, bf16[32,1152]{1,0:T(8,128)(2,1)S(1)}, u32[]{:S(2)}, u32[]{:S(2)}) collective-permute-start(bf16[32,1152]{1,0:T(8,128)(2,1)S(1)} %copy-done.69), channel_id=1, source_target_pairs={{0,3},{4,7},{8,11},{12,15},{16,19},{20,23},{24,27},{28,31}} | collective-permute-start | bytes 221192 | tf_op jit(solution)/shard_map/ppermute | solution.py:472
  231.4 48.5 %collective-permute-start.11 = (bf16[384,1152]{1,0:T(8,128)(2,1)}, bf16[384,1152]{1,0:T(8,128)(2,1)}, u32[]{:S(2)}, u32[]{:S(2)}) collective-permute-start(bf16[384,1152]{1,0:T(8,128)(2,1)} %convolution_convert_fusion.9), channel_id=1, source_target_pairs={{0,3},{1,2},{2,1},{3,0},{4,7},{5,6},{6,5},{7,4},{8,11},{9,10},{10,... | collective-permute-start | bytes 2654216 | tf_op jit(solution)/shard_map/ppermute | solution.py:655
  237.7 93.0 %collective-permute-start.9 = (bf16[384,1152]{1,0:T(8,128)(2,1)}, bf16[384,1152]{1,0:T(8,128)(2,1)}, u32[]{:S(2)}, u32[]{:S(2)}) collective-permute-start(bf16[384,1152]{1,0:T(8,128)(2,1)} %convolution_convert_fusion.11), channel_id=1, source_target_pairs={{0,2},{1,3},{2,0},{3,1},{4,6},{5,7},{6,4},{7,5},{8,10},{9,11},{10,... | collective-permute-start | bytes 2654216 | tf_op jit(solution)/shard_map/ppermute | solution.py:655
  239.7 91.0 %collective-permute-start.7 = (bf16[384,1152]{1,0:T(8,128)(2,1)}, bf16[384,1152]{1,0:T(8,128)(2,1)}, u32[]{:S(2)}, u32[]{:S(2)}) collective-permute-start(bf16[384,1152]{1,0:T(8,128)(2,1)} %convolution_convert_fusion.13), channel_id=1, source_target_pairs={{0,1},{1,0},{2,3},{3,2},{4,5},{5,4},{6,7},{7,6},{8,9},{9,8},{10,11... | collective-permute-start | bytes 2654216 | tf_op jit(solution)/shard_map/ppermute | solution.py:655
  279.9 86.7 %collective-permute-start.17 = (bf16[384,1152]{1,0:T(8,128)(2,1)S(1)}, bf16[384,1152]{1,0:T(8,128)(2,1)S(1)}, u32[]{:S(2)}, u32[]{:S(2)}) collective-permute-start(bf16[384,1152]{1,0:T(8,128)(2,1)S(1)} %copy-done.81), channel_id=1, source_target_pairs={{0,3},{1,2},{2,1},{3,0},{4,7},{5,6},{6,5},{7,4},{8,11},{9,10},{10,... | collective-permute-start | bytes 2654216 | tf_op jit(solution)/shard_map/ppermute | solution.py:655
  330.7 75.7 %collective-permute-start.15 = (bf16[384,1152]{1,0:T(8,128)(2,1)S(1)}, bf16[384,1152]{1,0:T(8,128)(2,1)S(1)}, u32[]{:S(2)}, u32[]{:S(2)}) collective-permute-start(bf16[384,1152]{1,0:T(8,128)(2,1)S(1)} %copy-done.80), channel_id=1, source_target_pairs={{0,2},{1,3},{2,0},{3,1},{4,6},{5,7},{6,4},{7,5},{8,10},{9,11},{10,... | collective-permute-start | bytes 2654216 | tf_op jit(solution)/shard_map/ppermute | solution.py:655
  330.7 88.3 %collective-permute-start.13 = (bf16[384,1152]{1,0:T(8,128)(2,1)S(1)}, bf16[384,1152]{1,0:T(8,128)(2,1)S(1)}, u32[]{:S(2)}, u32[]{:S(2)}) collective-permute-start(bf16[384,1152]{1,0:T(8,128)(2,1)S(1)} %convolution_convert_fusion.14), channel_id=1, source_target_pairs={{0,1},{1,0},{2,3},{3,2},{4,5},{5,4},{6,7},{7,6},{8,9},{9,8},{10,11... | collective-permute-start | bytes 2654216 | tf_op jit(solution)/shard_map/ppermute | solution.py:655
  380.4 88.8 %collective-permute-start.18 = (bf16[384,1152]{1,0:T(8,128)(2,1)}, bf16[384,1152]{1,0:T(8,128)(2,1)S(1)}, u32[]{:S(2)}, u32[]{:S(2)}) collective-permute-start(bf16[384,1152]{1,0:T(8,128)(2,1)} %fusion.138), channel_id=1, source_target_pairs={{0,3},{1,2},{2,1},{3,0},{4,7},{5,6},{6,5},{7,4},{8,11},{9,10},{10,... | collective-permute-start | bytes 2654216 | tf_op jit(solution)/shard_map/ppermute | solution.py:655
  418.9 50.2 %collective-permute-start.16 = (bf16[384,1152]{1,0:T(8,128)(2,1)}, bf16[384,1152]{1,0:T(8,128)(2,1)S(1)}, u32[]{:S(2)}, u32[]{:S(2)}) collective-permute-start(bf16[384,1152]{1,0:T(8,128)(2,1)} %fusion.135), channel_id=1, source_target_pairs={{0,2},{1,3},{2,0},{3,1},{4,6},{5,7},{6,4},{7,5},{8,10},{9,11},{10,... | collective-permute-start | bytes 2654216 | tf_op jit(solution)/shard_map/ppermute | solution.py:655
  429.2 40.6 %collective-permute-start.14 = (bf16[384,1152]{1,0:T(8,128)(2,1)}, bf16[384,1152]{1,0:T(8,128)(2,1)S(1)}, u32[]{:S(2)}, u32[]{:S(2)}) collective-permute-start(bf16[384,1152]{1,0:T(8,128)(2,1)} %fusion.132), channel_id=1, source_target_pairs={{0,1},{1,0},{2,3},{3,2},{4,5},{5,4},{6,7},{7,6},{8,9},{9,8},{10,11... | collective-permute-start | bytes 2654216 | tf_op jit(solution)/shard_map/ppermute | solution.py:655
  477.6 186.8 %reduce-scatter.8.cloned.1.call-start = ((), (), s32[]{:S(2)}) async-start(), calls=%async_computation.8 | async-start | bytes 7962624 | tf_op jit(solution)/shard_map/reduce_scatter | solution.py:690
  477.6 24.8 %collective-permute-start.12 = (bf16[384,1152]{1,0:T(8,128)(2,1)}, bf16[384,1152]{1,0:T(8,128)(2,1)}, u32[]{:S(2)}, u32[]{:S(2)}) collective-permute-start(bf16[384,1152]{1,0:T(8,128)(2,1)} %fusion.150), channel_id=1, source_target_pairs={{0,3},{1,2},{2,1},{3,0},{4,7},{5,6},{6,5},{7,4},{8,11},{9,10},{10,... | collective-permute-start | bytes 2654216 | tf_op jit(solution)/shard_map/ppermute | solution.py:655
  479.5 73.6 %collective-permute-start.10 = (bf16[384,1152]{1,0:T(8,128)(2,1)S(1)}, bf16[384,1152]{1,0:T(8,128)(2,1)}, u32[]{:S(2)}, u32[]{:S(2)}) collective-permute-start(bf16[384,1152]{1,0:T(8,128)(2,1)S(1)} %copy-done.76), channel_id=1, source_target_pairs={{0,2},{1,3},{2,0},{3,1},{4,6},{5,7},{6,4},{7,5},{8,10},{9,11},{10,... | collective-permute-start | bytes 2654216 | tf_op jit(solution)/shard_map/ppermute | solution.py:655
  479.5 73.6 %collective-permute-start.8 = (bf16[384,1152]{1,0:T(8,128)(2,1)S(1)}, bf16[384,1152]{1,0:T(8,128)(2,1)}, u32[]{:S(2)}, u32[]{:S(2)}) collective-permute-start(bf16[384,1152]{1,0:T(8,128)(2,1)S(1)} %copy-done.75), channel_id=1, source_target_pairs={{0,1},{1,0},{2,3},{3,2},{4,5},{5,4},{6,7},{7,6},{8,9},{9,8},{10,11... | collective-permute-start | bytes 2654216 | tf_op jit(solution)/shard_map/ppermute | solution.py:655
  484.8 296.7 %reduce-scatter.10.cloned.1.call-start = ((), (), s32[]{:S(2)}) async-start(), calls=%async_computation.9 | async-start | bytes 5971968 | tf_op jit(solution)/shard_map/reduce_scatter | solution.py:732
  630.5 32.2 %collective-permute-start.21 = (bf16[24,1152]{1,0:T(8,128)(2,1)S(1)}, bf16[24,1152]{1,0:T(8,128)(2,1)}, u32[]{:S(2)}, u32[]{:S(2)}) collective-permute-start(bf16[24,1152]{1,0:T(8,128)(2,1)S(1)} %pad_maximum_fusion.8), channel_id=1, source_target_pairs={{3,0},{7,4},{11,8},{15,12},{19,16},{23,20},{27,24},{31,28}} | collective-permute-start | bytes 165896 | tf_op jit(solution)/shard_map/ppermute | solution.py:472
  632.0 23.2 %collective-permute-start.20 = (bf16[24,1152]{1,0:T(8,128)(2,1)S(1)}, bf16[24,1152]{1,0:T(8,128)(2,1)S(1)}, u32[]{:S(2)}, u32[]{:S(2)}) collective-permute-start(bf16[24,1152]{1,0:T(8,128)(2,1)S(1)} %pad_maximum_fusion.8), channel_id=1, source_target_pairs={{2,0},{3,1},{6,4},{7,5},{10,8},{11,9},{14,12},{15,13},{18,16},{19,... | collective-permute-start | bytes 165896 | tf_op jit(solution)/shard_map/ppermute | solution.py:472
  633.3 23.2 %collective-permute-start.19 = (bf16[24,1152]{1,0:T(8,128)(2,1)S(1)}, bf16[24,1152]{1,0:T(8,128)(2,1)S(1)}, u32[]{:S(2)}, u32[]{:S(2)}) collective-permute-start(bf16[24,1152]{1,0:T(8,128)(2,1)S(1)} %pad_maximum_fusion.8), channel_id=1, source_target_pairs={{1,0},{2,1},{3,2},{5,4},{6,5},{7,6},{9,8},{10,9},{11,10},{13,12},{... | collective-permute-start | bytes 165896 | tf_op jit(solution)/shard_map/ppermute | solution.py:472
  664.4 117.2 %reduce-scatter.12.cloned.1.call-start = ((), (), s32[]{:S(2)}) async-start(), calls=%async_computation.10 | async-start | bytes 5971968 | tf_op jit(solution)/shard_map/reduce_scatter | solution.py:733
  665.1 264.5 %reduce-scatter.14.cloned.1.call-start = ((), (), s32[]{:S(2)}) async-start(), calls=%async_computation.11 | async-start | bytes 7299072 | tf_op jit(solution)/shard_map/reduce_scatter | solution.py:771
  868.3 28.5 %collective-permute-start.27 = (bf16[144,1152]{1,0:T(8,128)(2,1)}, bf16[144,1152]{1,0:T(8,128)(2,1)}, u32[]{:S(2)}, u32[]{:S(2)}) collective-permute-start(bf16[144,1152]{1,0:T(8,128)(2,1)} %get-tuple-element.246), channel_id=1, source_target_pairs={{0,2},{1,3},{2,0},{3,1},{4,6},{5,7},{6,4},{7,5},{8,10},{9,11},{10,... | collective-permute-start | bytes 995336 | tf_op jit(solution)/shard_map/ppermute | solution.py:522
  868.3 28.5 %collective-permute-start.26 = (bf16[144,1152]{1,0:T(8,128)(2,1)S(1)}, bf16[144,1152]{1,0:T(8,128)(2,1)}, u32[]{:S(2)}, u32[]{:S(2)}) collective-permute-start(bf16[144,1152]{1,0:T(8,128)(2,1)S(1)} %get-tuple-element.245), channel_id=1, source_target_pairs={{0,1},{1,2},{2,3},{3,0},{4,5},{5,6},{6,7},{7,4},{8,9},{9,10},{10,1... | collective-permute-start | bytes 995336 | tf_op jit(solution)/shard_map/ppermute | solution.py:522
  902.9 26.3 %collective-permute-start.30 = (bf16[144,1152]{1,0:T(8,128)(2,1)S(1)}, bf16[144,1152]{1,0:T(8,128)(2,1)S(1)}, u32[]{:S(2)}, u32[]{:S(2)}) collective-permute-start(bf16[144,1152]{1,0:T(8,128)(2,1)S(1)} %fusion.182), channel_id=1, source_target_pairs={{0,2},{1,3},{2,0},{3,1},{4,6},{5,7},{6,4},{7,5},{8,10},{9,11},{10,... | collective-permute-start | bytes 995336 | tf_op jit(solution)/shard_map/ppermute | solution.py:522
  905.5 23.7 %collective-permute-start.31 = (bf16[144,1152]{1,0:T(8,128)(2,1)S(1)}, bf16[144,1152]{1,0:T(8,128)(2,1)S(1)}, u32[]{:S(2)}, u32[]{:S(2)}) collective-permute-start(bf16[144,1152]{1,0:T(8,128)(2,1)S(1)} %fusion.182), channel_id=1, source_target_pairs={{0,1},{1,2},{2,3},{3,0},{4,5},{5,6},{6,7},{7,4},{8,9},{9,10},{10,1... | collective-permute-start | bytes 995336 | tf_op jit(solution)/shard_map/ppermute | solution.py:522
  931.6 18.8 %collective-permute-start.33 = (bf16[88,1152]{1,0:T(8,128)(2,1)}, bf16[88,1152]{1,0:T(8,128)(2,1)}, u32[]{:S(2)}, u32[]{:S(2)}) collective-permute-start(bf16[88,1152]{1,0:T(8,128)(2,1)} %get-tuple-element.252), channel_id=1, source_target_pairs={{0,2},{1,3},{2,0},{3,1},{4,6},{5,7},{6,4},{7,5},{8,10},{9,11},{10,... | collective-permute-start | bytes 608264 | tf_op jit(solution)/shard_map/ppermute | solution.py:522
  (109 other events, 1998.2 us)
Sparse Core Ops, SparseCore 0:
  9.9 68.7 all-gather.6
  80.6 41.6 all-gather.8
  124.2 49.2 all-gather.10
  175.2 49.7 all-gather.12
  477.7 64.4 reduce-scatter.5
  546.0 65.4 reduce-scatter.7
  664.5 55.8 reduce-scatter.9
  724.2 57.0 reduce-scatter.11
  862.1 63.6 reduce-scatter.13

commit v4 on v3

--- a/solution.py
+++ b/solution.py
@@ -514,20 +514,31 @@
     return jnp.pad(whole, ((0, -whole.shape[0] % 16), (0, 0)))
 
 
+def expert_part(parts):
+    n, here = lax.axis_size("expert"), lax.axis_index("expert")
+    part = lambda k: lax.dynamic_index_in_dim(parts, jnp.mod(here + k, n), 0, keepdims=False)
+    total = part(0).astype(F32)
+    for k in range(1, n):
+        total = total + turned(part(k), k).astype(F32)
+    return total.astype(BF16)
+
+
+def turned(x, k):
+    n = lax.axis_size("expert")
+    return lax.ppermute(x, "expert", [(i, (i + k) % n) for i in range(n)]) if k else x
+
+
+def in_order(came):
+    n, here = lax.axis_size("expert"), lax.axis_index("expert")
+    return lax.dynamic_slice_in_dim(jnp.stack(came[::-1] * 2), n - 1 - here, n, 0)
+
+
 def expert_sum(*arrays):
-    n, here = lax.axis_size("expert"), lax.axis_index("expert")
+    n = lax.axis_size("expert")
     split = [x.reshape(n, x.shape[0] // n, x.shape[1]) for x in arrays]
     padded = [jnp.pad(x, ((0, 0), (0, -x.shape[1] % 8), (0, 0))) for x in split]
-    parts = jnp.concatenate(padded, axis=1) if len(padded) > 1 else padded[0]
-    moved = lambda x, k: lax.ppermute(x, "expert", [(i, (i + k) % n) for i in range(n)])
-    part = lambda k: lax.dynamic_index_in_dim(parts, jnp.mod(here + k, n), 0, keepdims=False)
-    total = part(0).astype(F32)
-    for x in [moved(part(k), k) for k in range(1, n)]:
-        total = total + x.astype(F32)
-    total = total.astype(BF16)
-    came = [total] + [moved(total, k) for k in range(1, n)]
-    twice = jnp.stack(came[::-1] * 2)
-    every = lax.dynamic_slice_in_dim(twice, n - 1 - here, n, 0)
+    total = expert_part(jnp.concatenate(padded, axis=1))
+    every = in_order([turned(total, k) for k in range(n)])
     out, at = [], 0
     for x, p in zip(split, padded):
         out.append(every[:, at : at + x.shape[1]].reshape(n * x.shape[1], x.shape[2]))
@@ -608,11 +619,12 @@
     tail = (norm_own[rows - taps + 1 :].astype(F32) * edge_keep).astype(BF16)
     borrowed = shifted(tail, "expert", 1)
     norm_low = jnp.concatenate([jnp.zeros((PAD - taps + 1, model), BF16), borrowed, norm_own], 0)
-    mixed = dot(norm_low, w_input).astype(BF16)
+    ok = jnp.pad(jnp.stack(valid, 1), ((PAD, PAD), (0, 0)))
+    norm_low, ok = lax.optimization_barrier((norm_low, ok))
+    conv_in = dot(norm_low, w_input[:, :width]).astype(BF16)
     conv_sum = jnp.broadcast_to(b_conv.astype(F32), (rows, width))
     for lag in range(taps):
-        conv_sum = conv_sum + valid[lag][:, None] * conv_f[taps - 1 - lag] * mixed[PAD - lag : PAD - lag + rows, :width].astype(F32)
-    ok = jnp.pad(jnp.stack(valid, 1), ((PAD, PAD), (0, 0)))
+        conv_sum = conv_sum + valid[lag][:, None] * conv_f[taps - 1 - lag] * conv_in[PAD - lag : PAD - lag + rows].astype(F32)
     inner_low = jax.nn.silu(conv_sum).astype(BF16)
     slope_low = silu_slope(conv_sum).astype(BF16)
     selected = product_back(inner_low, w_select)
@@ -620,7 +632,6 @@
     b_coeff = selected[:, rank : rank + states]
     c_coeff = selected[:, rank + states :]
     rate2 = -jnp.exp(w_decay.astype(F32)) * LOG2E
-    gate_in = mixed[PAD:, width:]
     st = flag[:, None]
     b_wide, c_wide = spread(b_coeff), spread(c_coeff)
     b_block, c_block = block_rows(b_coeff), block_rows(c_coeff)
@@ -635,6 +646,8 @@
         own_sums.append(end[states : states + 8])
         start_state.append(entering([c[:states] for c in came], [total(c[states:]) for c in came], rate_part))
     start_state = jnp.concatenate(start_state, 1)
+    norm_late, _ = lax.optimization_barrier((norm_own, end))
+    gate_in = dot(norm_late, w_input[:, width:]).astype(BF16)
     gated_low, scanned, history, marks = forward_scan(
         step_low, w_step, bias2, st, inner_low, gate_in, rate2, skip2, b_wide, c_block, start_state
     )
@@ -685,7 +698,9 @@
     )
     grad_up = contract(jnp.concatenate(grad_pre), jnp.concatenate(arrived)).astype(BF16)
     grad_down = contract(jnp.concatenate(up_low), jnp.concatenate(grad_arrived)).astype(BF16)
-    grad_sent, grad_up, grad_down = lax.optimization_barrier((grad_sent, grad_up, grad_down))
+    grad_sent, grad_up, grad_down, c_wide, b_block = lax.optimization_barrier(
+        (grad_sent, grad_up, grad_down, c_wide, b_block)
+    )
     sum_up = lax.psum_scatter(grad_up, "dp", scatter_dimension=0, tiled=True)
     sum_down = lax.psum_scatter(grad_down, "dp", scatter_dimension=0, tiled=True)
 
@@ -754,7 +769,7 @@
     summed = shares(summed, devices)
     grad_inner, summed = lax.optimization_barrier((grad_inner, summed))
     grad_conv_in, grad_kernel, grad_conv_b = conv_back(
-        mixed, grad_inner, slope_low, grad_selected, w_select, w_conv, ok
+        conv_in, grad_inner, slope_low, grad_selected, w_select, w_conv, ok
     )
     grad_norm_x = product_back(grad_conv_in, w_input[:, :width])
     returned_edge = shifted(grad_norm_x[PAD - taps + 1 : PAD], "expert", -1) * edge_keep
@@ -776,18 +791,26 @@
         + norm_r * scaled_one
         - hidden_in * (norm_r * norm_r * norm_r) * jnp.mean(hidden_in * scaled_one, axis=-1, keepdims=True)
     ).astype(BF16)
-    packed, sum_output, sum_input_z, grad_tokens = lax.optimization_barrier((packed, sum_output, sum_input_z, grad_tokens))
-    (packed,) = expert_sum(packed)
+    half = devices // 2
+    other_z = lax.ppermute(sum_input_z, "dp", [(d, d + half) for d in range(half)])
+    packed, sum_output, sum_input_z, other_z, grad_tokens = lax.optimization_barrier(
+        (packed, sum_output, sum_input_z, other_z, grad_tokens)
+    )
+    part = expert_part(packed.reshape(groups, -1, model))
+    across = [
+        lax.ppermute(
+            part, ("dp", "expert"),
+            [(d * groups + z, (d - half) * groups + (z + k) % groups) for d in range(half, devices) for z in range(groups)],
+        )
+        for k in range(groups)
+    ]
+    packed = in_order([turned(part, k) for k in range(groups)]).reshape(-1, model)
+    other_x = in_order(across).reshape(-1, model)[:share]
     sum_input_x, tiny = packed[:share], packed[share:].astype(F32).reshape(-1)
     summed = tiny[: summed_shape[0] * share].reshape(summed_shape)
     tiny = tiny[summed_shape[0] * share :]
-    half = devices // 2
     low = lax.axis_index("dp") < half
-    other = lax.ppermute(
-        jnp.where(low, sum_input_z, sum_input_x), "dp", [(i, (i + half) % devices) for i in range(devices)]
-    )
-    own_half = jnp.where(low, sum_input_x, sum_input_z)
-    sum_input = jnp.concatenate([jnp.where(low, own_half, other), jnp.where(low, other, own_half)])
+    sum_input = jnp.concatenate([jnp.where(low, sum_input_x, other_z), jnp.where(low, other_x, sum_input_z)])
     sum_kernel = tiny[: taps * share].reshape(taps, share)
     sum_conv_b = tiny[taps * share : (taps + 1) * share]
     sum_norm = tiny[(taps + 1) * share : (taps + 1) * share + norm_share]

time: 1010 us -> 1040 us (1.030)
  waiting for transfers between devices: 255 us -> 279 us
    ppermute x13 -> x17, waiting for transfers between devices: 83.3 us -> 109 us  [the longest x12 95 us: turned(): lax.ppermute(x, 'expert', [(i, (i + k) % n) for i in range(n)])]
    unnamed x217 -> x248, local copies, waits for them, and re-layouts: 24.4 us -> 34 us
    ppermute x13 -> x17, starting transfers between devices: 17.4 us -> 24.1 us  [the longest x12 16 us: turned(): lax.ppermute(x, 'expert', [(i, (i + k) % n) for i in range(n)])]
    dot_general x19 -> x20, matrix products: 83.2 us -> 86.9 us  [dot(): return jnp.dot(a, b, preferred_element_type=F32)]
  transfers between devices with their start and end apart: 48 -> 52, of which waited for: 17 -> 19; matrix products, arithmetic and copies ran while one was open for 35% -> 32% of each run, Pallas kernels for 21% -> 20%
where the time goes in v4:
time: 1040 us; the launch traced here: 1030 us
  waiting for transfers between devices  279 us (27%)
  matrix products  242 us (23%)
  Pallas kernels  228 us (22%)
  local copies, waits for them, and re-layouts  99 us (10%)
  other arithmetic  78.3 us (8%)
  starting transfers between devices  72 us (7%)
  between operations  17.6 us (2%)
  blocking collectives  16.8 us (2%)
    ppermute x12, waiting for transfers between devices, swapped(): lax.ppermute(x, 'expert', [(i, i ^ k) for i in range(groups)])  141 us
    pallas_call x1, Pallas kernels, backward_scan(): pl.pallas_call(backward_kernel, grid=k.grid, in_specs=[k.token(s.shape[1]...  97 us
    ppermute x12, waiting for transfers between devices, turned(): lax.ppermute(x, 'expert', [(i, (i + k) % n) for i in range(n)])  95 us
    dot_general x20, matrix products, dot(): return jnp.dot(a, b, preferred_element_type=F32)  86.9 us
    dot_general x13, matrix products, product_back(): lax.dot_general(left, right, (((1,), (1,)), ((), ())), preferred_element_...  75 us
    dot_general x9, matrix products, contract(): lax.dot_general(left, right, (((0,), (0,)), ((), ())), preferred_element_...  71.7 us
    pallas_call x1, Pallas kernels, forward_scan(): pl.pallas_call(forward_kernel, grid=k.grid, in_specs=[k.token(s.shape[1])...  42.7 us
    pallas_call x2, Pallas kernels, end_states(): pl.pallas_call(end_kernel, grid=k.grid, in_specs=[k.token(s.shape[1]), k....  35.4 us
  transfers between devices with their start and end apart: 52, of which 19 were waited for; matrix products, arithmetic and copies ran while one was open for 32% of the time, Pallas kernels for 20%

profile of v4, /device:TPU:4, one launch (start us, length us, event | category | flops | bytes accessed | tf_op | source)
XLA Modules:
  0.0 1032.5 jit_solution(1529471409961350441)
XLA Ops:
  17.0 16.8 %all_gather.15 = bf16[208,2304]{0,1:T(8,128)(2,1)S(1)} all-gather(bf16[208,288]{0,1:T(8,128)(2,1)S(1)} %pad.21), channel_id=1, replica_groups=mesh['dp'=8,'expert'=4] {'dp'}, dimensions={1}, use_global_device_ids=true | all-gather | bytes 1078272 | tf_op jit(solution)/shard_map/all_gather | solution.py:586
  68.3 10.4 %all-gather.7.cloned.1.call-done = bf16[1152,4608]{0,1:T(8,128)(2,1)} async-done(((bf16[1152,576]{0,1:T(8,128)(2,1)}), bf16[1152,4608]{0,1:T(8,128)(2,1)}) %all-gather.7.cloned.1.call-update) | async-done | bytes 10616848 | tf_op jit(solution)/shard_map/all_gather | solution.py:577
  78.7 7.9 convolution_convert_fusion.5.xs_ref
  86.7 8.3 multiply_convert_fusion
  111.4 17.7 %end_states.3 = bf16[32,1152]{1,0:T(8,128)(2,1)} custom-call(bf16[768,72]{1,0:T(8,128)(2,1)} %copy.169.s_ref, bf16[72,2304]{1,0:T(8,128)(2,1)} %copy.170.w_ref, bf16[1,2304]{1,0:T(2,128)(2,1)} %copy.171.b_ref, f32[768,1]{1,0:T(8,128)} %broadcast_in_dim.155.st_ref, bf16[768,2304]{1,0:T(8,128)(2,1)} %copy-done.3, f32[16,2304]{1,0:T(8,128)} %negate_multiply_fusion.a_ref, ...), custom_call_target="tpu_custom_call" | custom-call | flops 84934656 | bytes 7077888 | tf_op jit(solution)/shard_map/end_states/pallas_call | solution.py:387
  138.3 17.7 %end_states.2 = bf16[32,1152]{1,0:T(8,128)(2,1)} custom-call(bf16[768,72]{1,0:T(8,128)(2,1)} %copy.169.s_ref, bf16[72,2304]{1,0:T(8,128)(2,1)} %copy.170.w_ref, bf16[1,2304]{1,0:T(2,128)(2,1)} %copy.171.b_ref, f32[768,1]{1,0:T(8,128)} %broadcast_in_dim.155.st_ref, bf16[768,2304]{1,0:T(8,128)(2,1)} %copy-done.3, f32[16,2304]{1,0:T(8,128)} %negate_multiply_fusion.a_ref, ...), custom_call_target="tpu_custom_call" | custom-call | flops 84934656 | bytes 7077888 | tf_op jit(solution)/shard_map/end_states/pallas_call | solution.py:387
  159.1 8.8 convolution_convert_fusion.6.z_ref
  173.2 42.7 %forward_scan.1 = (bf16[768,2304]{1,0:T(8,128)(2,1)}, bf16[768,2304]{1,0:T(8,128)(2,1)}, bf16[12288,2304]{1,0:T(8,128)(2,1)}, bf16[48,16,2304]{2,1,0:T(8,128)(2,1)}) custom-call(bf16[768,72]{1,0:T(8,128)(2,1)} %copy.169.s_ref, bf16[72,2304]{1,0:T(8,128)(2,1)} %copy.170.w_ref, bf16[1,2304]{1,0:T(2,128)(2,1)} %copy.171.b_ref, ...), custom_call_target="tpu_custom_call" | custom-call | flops 254803968 | bytes 77856768 | tf_op jit(solution)/shard_map/forward_scan/pallas_call | solution.py:403
  216.0 8.5 multiply_reduce_fusion.2
  248.1 10.1 multiply_convert_fusion.5
  258.2 8.6 fusion.60
  280.9 46.4 %collective-permute-done.9 = bf16[384,1152]{1,0:T(8,128)(2,1)} collective-permute-done((bf16[384,1152]{1,0:T(8,128)(2,1)}, bf16[384,1152]{1,0:T(8,128)(2,1)}, u32[]{:S(2)}, u32[]{:S(2)}) %collective-permute-start.9) | collective-permute-done | bytes 884768 | tf_op jit(solution)/shard_map/ppermute | solution.py:668
  377.5 25.5 %collective-permute-done.15 = bf16[384,1152]{1,0:T(8,128)(2,1)S(1)} collective-permute-done((bf16[384,1152]{1,0:T(8,128)(2,1)S(1)}, bf16[384,1152]{1,0:T(8,128)(2,1)S(1)}, u32[]{:S(2)}, u32[]{:S(2)}) %collective-permute-start.15) | collective-permute-done | bytes 884768 | tf_op jit(solution)/shard_map/ppermute | solution.py:668
  429.2 17.6 %convolution_convert_fusion.4 = bf16[3072,1152]{1,0:T(8,128)(2,1)} fusion(bf16[384,3072]{1,0:T(8,128)(2,1)} %copy-done.96, bf16[384,3072]{1,0:T(8,128)(2,1)} %fusion.74, bf16[384,3072]{1,0:T(8,128)(2,1)} %copy-done.97, bf16[384,3072]{1,0:T(8,128)(2,1)} %copy-done.95, bf16[384,1152]{1,0:T(8,128)(2,1)} %collective-permute-done.11, ...), kind=kOutput, calls=%fused_computation.4 | convolution fusion | flops 10927079424 | bytes 20054016 | tf_op jit(solution)/shard_map/dot_general | solution.py:488
  446.9 18.3 %convolution_convert_fusion.3 = bf16[3072,1152]{1,0:T(8,128)(2,1)} fusion(bf16[384,3072]{1,0:T(8,128)(2,1)} %copy-done.99, bf16[384,3072]{1,0:T(8,128)(2,1)} %copy-done.100, bf16[384,3072]{1,0:T(8,128)(2,1)} %copy-done.101, bf16[384,3072]{1,0:T(8,128)(2,1)} %get-tuple-element.96, bf16[384,1152]{1,0:T(8,128)(2,1)} %copy-done.89, ...), kind=kOutput, calls=%fused_computation.3 | convolution fusion | flops 10927079424 | bytes 20054016 | tf_op jit(solution)/shard_map/dot_general | solution.py:488
  466.2 7.7 pad_maximum_fusion.1
  485.1 17.6 %collective-permute-done.12 = bf16[384,1152]{1,0:T(8,128)(2,1)} collective-permute-done((bf16[384,1152]{1,0:T(8,128)(2,1)}, bf16[384,1152]{1,0:T(8,128)(2,1)}, u32[]{:S(2)}, u32[]{:S(2)}) %collective-permute-start.12) | collective-permute-done | bytes 884768 | tf_op jit(solution)/shard_map/ppermute | solution.py:668
  502.7 50.5 %collective-permute-done.10 = bf16[384,1152]{1,0:T(8,128)(2,1)} collective-permute-done((bf16[384,1152]{1,0:T(8,128)(2,1)S(1)}, bf16[384,1152]{1,0:T(8,128)(2,1)}, u32[]{:S(2)}, u32[]{:S(2)}) %collective-permute-start.10) | collective-permute-done | bytes 884768 | tf_op jit(solution)/shard_map/ppermute | solution.py:668
  595.4 10.5 %fusion.82 = f32[768,1152]{1,0:T(8,128)} fusion(bf16[768,2304]{1,0:T(8,128)(2,1)} %copy-done.22, bf16[1152,4608]{0,1:T(8,128)(2,1)} %all-gather.7.cloned.1.call-done), kind=kOutput, calls=%fused_computation.119 | convolution fusion | flops 4076863488 | bytes 12386304 | tf_op jit(solution)/shard_map/dot_general | solution.py:484
  605.9 17.1 %start_grads.2 = bf16[16,1152]{1,0:T(8,128)(2,1)} custom-call(bf16[768,72]{1,0:T(8,128)(2,1)} %copy.169.s_ref, bf16[72,2304]{1,0:T(8,128)(2,1)} %copy.170.w_ref, bf16[1,2304]{1,0:T(2,128)(2,1)} %copy.171.b_ref, f32[768,1]{1,0:T(8,128)} %broadcast_in_dim.155.st_ref, f32[768,2304]{1,0:T(8,128)} %get-tuple-element.106.dy_ref, ...), custom_call_target="tpu_custom_call" | custom-call | flops 84934656 | bytes 7077888 | tf_op jit(solution)/shard_map/start_grads/pallas_call | solution.py:421
  627.8 17.2 %start_grads.3 = bf16[16,1152]{1,0:T(8,128)(2,1)} custom-call(bf16[768,72]{1,0:T(8,128)(2,1)} %copy.169.s_ref, bf16[72,2304]{1,0:T(8,128)(2,1)} %copy.170.w_ref, bf16[1,2304]{1,0:T(2,128)(2,1)} %copy.171.b_ref, f32[768,1]{1,0:T(8,128)} %broadcast_in_dim.155.st_ref, f32[768,2304]{1,0:T(8,128)} %get-tuple-element.106.dy_ref, ...), custom_call_target="tpu_custom_call" | custom-call | flops 84934656 | bytes 7077888 | tf_op jit(solution)/shard_map/start_grads/pallas_call | solution.py:421
  666.1 97.0 %backward_scan.1 = (bf16[768,2304]{1,0:T(8,128)(2,1)}, f32[768,2304]{1,0:T(8,128)}, f32[16,2304]{1,0:T(8,128)}, f32[1,2304]{1,0:T(1,128)}, bf16[768,128]{1,0:T(8,128)(2,1)}, /*index=5*/f32[48,8,256]{2,1,0:T(8,128)}) custom-call(bf16[768,72]{1,0:T(8,128)(2,1)} %copy.169.s_ref, bf16[72,2304]{1,0:T(8,128)(2,1)} %copy.170.w_ref, bf16[1,2304]{1,0:T(2,128)(2,1)} %copy.171.b_ref, ...), custom_call_target="tpu_custom_call" | custom-call | flops 509607936 | bytes 77856768 | tf_op jit(solution)/shard_map/backward_scan/pallas_call | solution.py:438
  798.1 18.6 %conv_back.1 = (bf16[784,2304]{1,0:T(8,128)(2,1)}, f32[4,2304]{1,0:T(4,128)}, f32[1,2304]{1,0:T(1,128)}) custom-call(bf16[784,2304]{1,0:T(8,128)(2,1)} %copy-done.2, f32[768,2304]{1,0:T(8,128)} %get-tuple-element.123.du_ref, bf16[768,2304]{1,0:T(8,128)(2,1)} %get-tuple-element.243.slope_ref, bf16[768,104]{1,0:T(8,128)(2,1)} %copy-done.31, ...), custom_call_target="tpu_custom_call" | custom-call | flops 530841600 | bytes 14155776 | tf_op jit(solution)/shard_map/conv_back/pallas_call | solution.py:321
  818.2 9.7 convolution_convert_fusion
  828.0 7.4 fusion.85
  864.3 7.5 collective-permute-done.28
  871.8 19.9 %collective-permute-done.27 = bf16[144,1152]{1,0:T(8,128)(2,1)} collective-permute-done((bf16[144,1152]{1,0:T(8,128)(2,1)}, bf16[144,1152]{1,0:T(8,128)(2,1)}, u32[]{:S(2)}, u32[]{:S(2)}) %collective-permute-start.27) | collective-permute-done | bytes 331808 | tf_op jit(solution)/shard_map/ppermute | solution.py:528
  901.5 22.9 %collective-permute-done.30 = bf16[144,1152]{1,0:T(8,128)(2,1)S(1)} collective-permute-done((bf16[144,1152]{1,0:T(8,128)(2,1)S(1)}, bf16[144,1152]{1,0:T(8,128)(2,1)S(1)}, u32[]{:S(2)}, u32[]{:S(2)}) %collective-permute-start.30) | collective-permute-done | bytes 331808 | tf_op jit(solution)/shard_map/ppermute | solution.py:528
  928.2 14.1 %collective-permute-done.32 = bf16[288,1152]{1,0:T(8,128)(2,1)} collective-permute-done((bf16[288,1152]{1,0:T(8,128)(2,1)S(1)}, bf16[288,1152]{1,0:T(8,128)(2,1)}, u32[]{:S(2)}, u32[]{:S(2)}) %collective-permute-start.32) | collective-permute-done | bytes 663584 | tf_op jit(solution)/shard_map/ppermute | solution.py:795
  951.2 11.5 %collective-permute-done.34 = bf16[88,1152]{1,0:T(8,128)(2,1)} collective-permute-done((bf16[88,1152]{1,0:T(8,128)(2,1)}, bf16[88,1152]{1,0:T(8,128)(2,1)}, u32[]{:S(2)}, u32[]{:S(2)}) %collective-permute-start.34) | collective-permute-done | bytes 202784 | tf_op jit(solution)/shard_map/ppermute | solution.py:528
  976.0 20.8 %collective-permute-done.37 = bf16[88,1152]{1,0:T(8,128)(2,1)S(1)} collective-permute-done((bf16[88,1152]{1,0:T(8,128)(2,1)S(1)}, bf16[88,1152]{1,0:T(8,128)(2,1)S(1)}, u32[]{:S(2)}, u32[]{:S(2)}) %collective-permute-start.37) | collective-permute-done | bytes 202784 | tf_op jit(solution)/shard_map/ppermute | solution.py:528
  998.1 8.0 collective-permute-done.38
  (536 shorter events, 391.5 us)
Async XLA Ops:
  7.2 71.5 %all-gather.7.cloned.1.call-start = ((), (), s32[]{:S(2)}) async-start(), calls=%async_computation.5 | async-start | bytes 11943936 | tf_op jit(solution)/shard_map/all_gather | solution.py:577
  7.9 208.0 %all-gather.9.cloned.1.call-start = ((), (), s32[]{:S(2)}) async-start(), calls=%async_computation.6 | async-start | bytes 5971968 | tf_op jit(solution)/shard_map/all_gather | solution.py:590
  8.7 239.4 %all-gather.11.cloned.1.call-start = ((), (), s32[]{:S(2)}) async-start(), calls=%async_computation.12 | async-start | bytes 7962624 | tf_op jit(solution)/shard_map/all_gather | solution.py:591
  9.4 248.8 %all-gather.13.cloned.1.call-start = ((), (), s32[]{:S(2)}) async-start(), calls=%async_computation.13 | async-start | bytes 7962624 | tf_op jit(solution)/shard_map/all_gather | solution.py:592
  46.3 559.6 %reduce-scatter.6.cloned.1.call-start = ((), (), s32[]{:S(2)}) async-start(), calls=%async_computation.7 | async-start | bytes 7962624 | tf_op jit(solution)/shard_map/reduce_scatter | solution.py:704
  129.1 43.3 %collective-permute-start.3 = (bf16[32,1152]{1,0:T(8,128)(2,1)}, bf16[32,1152]{1,0:T(8,128)(2,1)S(1)}, u32[]{:S(2)}, u32[]{:S(2)}) collective-permute-start(bf16[32,1152]{1,0:T(8,128)(2,1)} %end_states.3), channel_id=1, source_target_pairs={{0,3},{4,7},{8,11},{12,15},{16,19},{20,23},{24,27},{28,31}} | collective-permute-start | bytes 221192 | tf_op jit(solution)/shard_map/ppermute | solution.py:472
  134.6 34.4 %collective-permute-start.2 = (bf16[32,1152]{1,0:T(8,128)(2,1)}, bf16[32,1152]{1,0:T(8,128)(2,1)S(1)}, u32[]{:S(2)}, u32[]{:S(2)}) collective-permute-start(bf16[32,1152]{1,0:T(8,128)(2,1)} %end_states.3), channel_id=1, source_target_pairs={{0,2},{1,3},{4,6},{5,7},{8,10},{9,11},{12,14},{13,15},{16,18},{17,... | collective-permute-start | bytes 221192 | tf_op jit(solution)/shard_map/ppermute | solution.py:472
  135.9 34.6 %collective-permute-start.1 = (bf16[32,1152]{1,0:T(8,128)(2,1)}, bf16[32,1152]{1,0:T(8,128)(2,1)S(1)}, u32[]{:S(2)}, u32[]{:S(2)}) collective-permute-start(bf16[32,1152]{1,0:T(8,128)(2,1)} %end_states.3), channel_id=1, source_target_pairs={{0,1},{1,2},{2,3},{4,5},{5,6},{6,7},{8,9},{9,10},{10,11},{12,13},{... | collective-permute-start | bytes 221192 | tf_op jit(solution)/shard_map/ppermute | solution.py:472
  228.5 48.5 %collective-permute-start.11 = (bf16[384,1152]{1,0:T(8,128)(2,1)}, bf16[384,1152]{1,0:T(8,128)(2,1)}, u32[]{:S(2)}, u32[]{:S(2)}) collective-permute-start(bf16[384,1152]{1,0:T(8,128)(2,1)} %convolution_convert_fusion.10), channel_id=1, source_target_pairs={{0,3},{1,2},{2,1},{3,0},{4,7},{5,6},{6,5},{7,4},{8,11},{9,10},{10,... | collective-permute-start | bytes 2654216 | tf_op jit(solution)/shard_map/ppermute | solution.py:668
  234.7 92.6 %collective-permute-start.9 = (bf16[384,1152]{1,0:T(8,128)(2,1)}, bf16[384,1152]{1,0:T(8,128)(2,1)}, u32[]{:S(2)}, u32[]{:S(2)}) collective-permute-start(bf16[384,1152]{1,0:T(8,128)(2,1)} %convolution_convert_fusion.12), channel_id=1, source_target_pairs={{0,2},{1,3},{2,0},{3,1},{4,6},{5,7},{6,4},{7,5},{8,10},{9,11},{10,... | collective-permute-start | bytes 2654216 | tf_op jit(solution)/shard_map/ppermute | solution.py:668
  236.6 90.6 %collective-permute-start.7 = (bf16[384,1152]{1,0:T(8,128)(2,1)}, bf16[384,1152]{1,0:T(8,128)(2,1)}, u32[]{:S(2)}, u32[]{:S(2)}) collective-permute-start(bf16[384,1152]{1,0:T(8,128)(2,1)} %convolution_convert_fusion.14), channel_id=1, source_target_pairs={{0,1},{1,0},{2,3},{3,2},{4,5},{5,4},{6,7},{7,6},{8,9},{9,8},{10,11... | collective-permute-start | bytes 2654216 | tf_op jit(solution)/shard_map/ppermute | solution.py:668
  277.0 85.7 %collective-permute-start.17 = (bf16[384,1152]{1,0:T(8,128)(2,1)S(1)}, bf16[384,1152]{1,0:T(8,128)(2,1)S(1)}, u32[]{:S(2)}, u32[]{:S(2)}) collective-permute-start(bf16[384,1152]{1,0:T(8,128)(2,1)S(1)} %copy-done.93), channel_id=1, source_target_pairs={{0,3},{1,2},{2,1},{3,0},{4,7},{5,6},{6,5},{7,4},{8,11},{9,10},{10,... | collective-permute-start | bytes 2654216 | tf_op jit(solution)/shard_map/ppermute | solution.py:668
  327.3 75.7 %collective-permute-start.15 = (bf16[384,1152]{1,0:T(8,128)(2,1)S(1)}, bf16[384,1152]{1,0:T(8,128)(2,1)S(1)}, u32[]{:S(2)}, u32[]{:S(2)}) collective-permute-start(bf16[384,1152]{1,0:T(8,128)(2,1)S(1)} %copy-done.92), channel_id=1, source_target_pairs={{0,2},{1,3},{2,0},{3,1},{4,6},{5,7},{6,4},{7,5},{8,10},{9,11},{10,... | collective-permute-start | bytes 2654216 | tf_op jit(solution)/shard_map/ppermute | solution.py:668
  327.3 88.3 %collective-permute-start.13 = (bf16[384,1152]{1,0:T(8,128)(2,1)S(1)}, bf16[384,1152]{1,0:T(8,128)(2,1)S(1)}, u32[]{:S(2)}, u32[]{:S(2)}) collective-permute-start(bf16[384,1152]{1,0:T(8,128)(2,1)S(1)} %convolution_convert_fusion.15), channel_id=1, source_target_pairs={{0,1},{1,0},{2,3},{3,2},{4,5},{5,4},{6,7},{7,6},{8,9},{9,8},{10,11... | collective-permute-start | bytes 2654216 | tf_op jit(solution)/shard_map/ppermute | solution.py:668
  376.6 88.6 %collective-permute-start.18 = (bf16[384,1152]{1,0:T(8,128)(2,1)}, bf16[384,1152]{1,0:T(8,128)(2,1)S(1)}, u32[]{:S(2)}, u32[]{:S(2)}) collective-permute-start(bf16[384,1152]{1,0:T(8,128)(2,1)} %fusion.140), channel_id=1, source_target_pairs={{0,3},{1,2},{2,1},{3,0},{4,7},{5,6},{6,5},{7,4},{8,11},{9,10},{10,... | collective-permute-start | bytes 2654216 | tf_op jit(solution)/shard_map/ppermute | solution.py:668
  415.5 49.7 %collective-permute-start.16 = (bf16[384,1152]{1,0:T(8,128)(2,1)}, bf16[384,1152]{1,0:T(8,128)(2,1)S(1)}, u32[]{:S(2)}, u32[]{:S(2)}) collective-permute-start(bf16[384,1152]{1,0:T(8,128)(2,1)} %fusion.137), channel_id=1, source_target_pairs={{0,2},{1,3},{2,0},{3,1},{4,6},{5,7},{6,4},{7,5},{8,10},{9,11},{10,... | collective-permute-start | bytes 2654216 | tf_op jit(solution)/shard_map/ppermute | solution.py:668
  425.8 40.4 %collective-permute-start.14 = (bf16[384,1152]{1,0:T(8,128)(2,1)}, bf16[384,1152]{1,0:T(8,128)(2,1)S(1)}, u32[]{:S(2)}, u32[]{:S(2)}) collective-permute-start(bf16[384,1152]{1,0:T(8,128)(2,1)} %fusion.134), channel_id=1, source_target_pairs={{0,1},{1,0},{2,3},{3,2},{4,5},{5,4},{6,7},{7,6},{8,9},{9,8},{10,11... | collective-permute-start | bytes 2654216 | tf_op jit(solution)/shard_map/ppermute | solution.py:668
  477.8 179.8 %reduce-scatter.8.cloned.1.call-start = ((), (), s32[]{:S(2)}) async-start(), calls=%async_computation.8 | async-start | bytes 7962624 | tf_op jit(solution)/shard_map/reduce_scatter | solution.py:705
  479.4 73.7 %collective-permute-start.10 = (bf16[384,1152]{1,0:T(8,128)(2,1)S(1)}, bf16[384,1152]{1,0:T(8,128)(2,1)}, u32[]{:S(2)}, u32[]{:S(2)}) collective-permute-start(bf16[384,1152]{1,0:T(8,128)(2,1)S(1)} %copy-done.88), channel_id=1, source_target_pairs={{0,2},{1,3},{2,0},{3,1},{4,6},{5,7},{6,4},{7,5},{8,10},{9,11},{10,... | collective-permute-start | bytes 2654216 | tf_op jit(solution)/shard_map/ppermute | solution.py:668
  479.4 73.7 %collective-permute-start.8 = (bf16[384,1152]{1,0:T(8,128)(2,1)S(1)}, bf16[384,1152]{1,0:T(8,128)(2,1)}, u32[]{:S(2)}, u32[]{:S(2)}) collective-permute-start(bf16[384,1152]{1,0:T(8,128)(2,1)S(1)} %copy-done.87), channel_id=1, source_target_pairs={{0,1},{1,0},{2,3},{3,2},{4,5},{5,4},{6,7},{7,6},{8,9},{9,8},{10,11... | collective-permute-start | bytes 2654216 | tf_op jit(solution)/shard_map/ppermute | solution.py:668
  485.0 282.3 %reduce-scatter.10.cloned.1.call-start = ((), (), s32[]{:S(2)}) async-start(), calls=%async_computation.9 | async-start | bytes 5971968 | tf_op jit(solution)/shard_map/reduce_scatter | solution.py:747
  623.7 32.2 %collective-permute-start.21 = (bf16[24,1152]{1,0:T(8,128)(2,1)S(1)}, bf16[24,1152]{1,0:T(8,128)(2,1)}, u32[]{:S(2)}, u32[]{:S(2)}) collective-permute-start(bf16[24,1152]{1,0:T(8,128)(2,1)S(1)} %pad_maximum_fusion.6), channel_id=1, source_target_pairs={{3,0},{7,4},{11,8},{15,12},{19,16},{23,20},{27,24},{31,28}} | collective-permute-start | bytes 165896 | tf_op jit(solution)/shard_map/ppermute | solution.py:472
  657.6 117.0 %reduce-scatter.12.cloned.1.call-start = ((), (), s32[]{:S(2)}) async-start(), calls=%async_computation.10 | async-start | bytes 5971968 | tf_op jit(solution)/shard_map/reduce_scatter | solution.py:748
  658.3 284.0 %reduce-scatter.14.cloned.1.call-start = ((), (), s32[]{:S(2)}) async-start(), calls=%async_computation.11 | async-start | bytes 7299072 | tf_op jit(solution)/shard_map/reduce_scatter | solution.py:786
  863.1 28.5 %collective-permute-start.27 = (bf16[144,1152]{1,0:T(8,128)(2,1)}, bf16[144,1152]{1,0:T(8,128)(2,1)}, u32[]{:S(2)}, u32[]{:S(2)}) collective-permute-start(bf16[144,1152]{1,0:T(8,128)(2,1)} %get-tuple-element.256), channel_id=1, source_target_pairs={{0,2},{1,3},{2,0},{3,1},{4,6},{5,7},{6,4},{7,5},{8,10},{9,11},{10,... | collective-permute-start | bytes 995336 | tf_op jit(solution)/shard_map/ppermute | solution.py:528
  863.1 28.5 %collective-permute-start.26 = (bf16[144,1152]{1,0:T(8,128)(2,1)S(1)}, bf16[144,1152]{1,0:T(8,128)(2,1)}, u32[]{:S(2)}, u32[]{:S(2)}) collective-permute-start(bf16[144,1152]{1,0:T(8,128)(2,1)S(1)} %get-tuple-element.255), channel_id=1, source_target_pairs={{0,1},{1,2},{2,3},{3,0},{4,5},{5,6},{6,7},{7,4},{8,9},{9,10},{10,1... | collective-permute-start | bytes 995336 | tf_op jit(solution)/shard_map/ppermute | solution.py:528
  893.1 31.3 %collective-permute-start.30 = (bf16[144,1152]{1,0:T(8,128)(2,1)S(1)}, bf16[144,1152]{1,0:T(8,128)(2,1)S(1)}, u32[]{:S(2)}, u32[]{:S(2)}) collective-permute-start(bf16[144,1152]{1,0:T(8,128)(2,1)S(1)} %fusion.182), channel_id=1, source_target_pairs={{0,2},{1,3},{2,0},{3,1},{4,6},{5,7},{6,4},{7,5},{8,10},{9,11},{10,... | collective-permute-start | bytes 995336 | tf_op jit(solution)/shard_map/ppermute | solution.py:528
  895.9 28.6 %collective-permute-start.31 = (bf16[144,1152]{1,0:T(8,128)(2,1)S(1)}, bf16[144,1152]{1,0:T(8,128)(2,1)S(1)}, u32[]{:S(2)}, u32[]{:S(2)}) collective-permute-start(bf16[144,1152]{1,0:T(8,128)(2,1)S(1)} %fusion.182), channel_id=1, source_target_pairs={{0,1},{1,2},{2,3},{3,0},{4,5},{5,6},{6,7},{7,4},{8,9},{9,10},{10,1... | collective-permute-start | bytes 995336 | tf_op jit(solution)/shard_map/ppermute | solution.py:528
  967.7 38.7 %collective-permute-start.39 = (bf16[88,1152]{1,0:T(8,128)(2,1)S(1)}, bf16[88,1152]{1,0:T(8,128)(2,1)S(1)}, u32[]{:S(2)}, u32[]{:S(2)}) collective-permute-start(bf16[88,1152]{1,0:T(8,128)(2,1)S(1)} %fusion.185), channel_id=1, source_target_pairs={{16,3},{17,0},{18,1},{19,2},{20,7},{21,4},{22,5},{23,6},{24,11},{2... | collective-permute-start | bytes 608264 | tf_op jit(solution)/shard_map/ppermute | solution.py:801
  970.7 36.4 %collective-permute-start.40 = (bf16[88,1152]{1,0:T(8,128)(2,1)S(1)}, bf16[88,1152]{1,0:T(8,128)(2,1)S(1)}, u32[]{:S(2)}, u32[]{:S(2)}) collective-permute-start(bf16[88,1152]{1,0:T(8,128)(2,1)S(1)} %fusion.185), channel_id=1, source_target_pairs={{16,2},{17,3},{18,0},{19,1},{20,6},{21,7},{22,4},{23,5},{24,10},{2... | collective-permute-start | bytes 608264 | tf_op jit(solution)/shard_map/ppermute | solution.py:801
  972.0 39.4 %collective-permute-start.41 = (bf16[88,1152]{1,0:T(8,128)(2,1)S(1)}, bf16[88,1152]{1,0:T(8,128)(2,1)S(1)}, u32[]{:S(2)}, u32[]{:S(2)}) collective-permute-start(bf16[88,1152]{1,0:T(8,128)(2,1)S(1)} %fusion.185), channel_id=1, source_target_pairs={{16,1},{17,2},{18,3},{19,0},{20,5},{21,6},{22,7},{23,4},{24,9},{25... | collective-permute-start | bytes 608264 | tf_op jit(solution)/shard_map/ppermute | solution.py:801
  973.3 40.2 %collective-permute-start.42 = (bf16[88,1152]{1,0:T(8,128)(2,1)S(1)}, bf16[88,1152]{1,0:T(8,128)(2,1)S(1)}, u32[]{:S(2)}, u32[]{:S(2)}) collective-permute-start(bf16[88,1152]{1,0:T(8,128)(2,1)S(1)} %fusion.185), channel_id=1, source_target_pairs={{16,0},{17,1},{18,2},{19,3},{20,4},{21,5},{22,6},{23,7},{24,8},{25... | collective-permute-start | bytes 608264 | tf_op jit(solution)/shard_map/ppermute | solution.py:801
  (125 other events, 2135.6 us)
Sparse Core Ops, SparseCore 0:
  9.9 68.7 all-gather.6
  80.6 41.6 all-gather.8
  124.2 49.1 all-gather.10
  175.1 49.7 all-gather.12
  477.9 63.8 reduce-scatter.5
  545.6 65.4 reduce-scatter.7
  657.7 55.9 reduce-scatter.9
  717.5 57.0 reduce-scatter.11
  856.6 63.8 reduce-scatter.13

commit v5 on v4

--- a/solution.py
+++ b/solution.py
@@ -791,26 +791,18 @@
         + norm_r * scaled_one
         - hidden_in * (norm_r * norm_r * norm_r) * jnp.mean(hidden_in * scaled_one, axis=-1, keepdims=True)
     ).astype(BF16)
-    half = devices // 2
-    other_z = lax.ppermute(sum_input_z, "dp", [(d, d + half) for d in range(half)])
-    packed, sum_output, sum_input_z, other_z, grad_tokens = lax.optimization_barrier(
-        (packed, sum_output, sum_input_z, other_z, grad_tokens)
-    )
-    part = expert_part(packed.reshape(groups, -1, model))
-    across = [
-        lax.ppermute(
-            part, ("dp", "expert"),
-            [(d * groups + z, (d - half) * groups + (z + k) % groups) for d in range(half, devices) for z in range(groups)],
-        )
-        for k in range(groups)
-    ]
-    packed = in_order([turned(part, k) for k in range(groups)]).reshape(-1, model)
-    other_x = in_order(across).reshape(-1, model)[:share]
+    packed, sum_output, sum_input_z, grad_tokens = lax.optimization_barrier((packed, sum_output, sum_input_z, grad_tokens))
+    (packed,) = expert_sum(packed)
     sum_input_x, tiny = packed[:share], packed[share:].astype(F32).reshape(-1)
     summed = tiny[: summed_shape[0] * share].reshape(summed_shape)
     tiny = tiny[summed_shape[0] * share :]
+    half = devices // 2
     low = lax.axis_index("dp") < half
-    sum_input = jnp.concatenate([jnp.where(low, sum_input_x, other_z), jnp.where(low, other_x, sum_input_z)])
+    other = lax.ppermute(
+        jnp.where(low, sum_input_z, sum_input_x), "dp", [(i, (i + half) % devices) for i in range(devices)]
+    )
+    own_half = jnp.where(low, sum_input_x, sum_input_z)
+    sum_input = jnp.concatenate([jnp.where(low, own_half, other), jnp.where(low, other, own_half)])
     sum_kernel = tiny[: taps * share].reshape(taps, share)
     sum_conv_b = tiny[taps * share : (taps + 1) * share]
     sum_norm = tiny[(taps + 1) * share : (taps + 1) * share + norm_share]

time: 1040 us -> 1000 us (0.962)
  waiting for transfers between devices: 279 us -> 254 us
    ppermute x12, waiting for transfers between devices: 95 us -> 75.2 us  [turned(): lax.ppermute(x, 'expert', [(i, (i + k) % n) for i in range(n)])]
    unnamed x248 -> x237, local copies, waits for them, and re-layouts: 34 us -> 29.1 us
  transfers between devices with their start and end apart: 52 -> 48, of which waited for: 19 -> 17; matrix products, arithmetic and copies ran while one was open for 32% -> 33% of each run, Pallas kernels for 20% -> 21%
where the time goes in v5:
time: 1000 us; the launch traced here: 992 us
  waiting for transfers between devices  254 us (25%)
  matrix products  242 us (24%)
  Pallas kernels  228 us (23%)
  local copies, waits for them, and re-layouts  89.3 us (9%)
  other arithmetic  80.8 us (8%)
  starting transfers between devices  64.4 us (6%)
  between operations  17.5 us (2%)
  blocking collectives  16.8 us (2%)
    ppermute x12, waiting for transfers between devices, swapped(): lax.ppermute(x, 'expert', [(i, i ^ k) for i in range(groups)])  141 us
    pallas_call x1, Pallas kernels, backward_scan(): pl.pallas_call(backward_kernel, grid=k.grid, in_specs=[k.token(s.shape[1]...  97 us
    dot_general x20, matrix products, dot(): return jnp.dot(a, b, preferred_element_type=F32)  87 us
    ppermute x12, waiting for transfers between devices, turned(): lax.ppermute(x, 'expert', [(i, (i + k) % n) for i in range(n)])  75.2 us
    dot_general x13, matrix products, product_back(): lax.dot_general(left, right, (((1,), (1,)), ((), ())), preferred_element_...  75.1 us
    dot_general x9, matrix products, contract(): lax.dot_general(left, right, (((0,), (0,)), ((), ())), preferred_element_...  71.8 us
    pallas_call x1, Pallas kernels, forward_scan(): pl.pallas_call(forward_kernel, grid=k.grid, in_specs=[k.token(s.shape[1])...  42.7 us
    pallas_call x2, Pallas kernels, end_states(): pl.pallas_call(end_kernel, grid=k.grid, in_specs=[k.token(s.shape[1]), k....  35.4 us
  transfers between devices with their start and end apart: 48, of which 17 were waited for; matrix products, arithmetic and copies ran while one was open for 33% of the time, Pallas kernels for 21%

profile of v5, /device:TPU:4, one launch (start us, length us, event | category | flops | bytes accessed | tf_op | source)
XLA Modules:
  0.0 992.4 jit_solution(1184017330125429135)
XLA Ops:
  17.0 16.8 %all_gather.15 = bf16[208,2304]{0,1:T(8,128)(2,1)S(1)} all-gather(bf16[208,288]{0,1:T(8,128)(2,1)S(1)} %pad.21), channel_id=1, replica_groups=mesh['dp'=8,'expert'=4] {'dp'}, dimensions={1}, use_global_device_ids=true | all-gather | bytes 1078272 | tf_op jit(solution)/shard_map/all_gather | solution.py:586
  68.3 10.5 %all-gather.7.cloned.1.call-done = bf16[1152,4608]{0,1:T(8,128)(2,1)} async-done(((bf16[1152,576]{0,1:T(8,128)(2,1)}), bf16[1152,4608]{0,1:T(8,128)(2,1)}) %all-gather.7.cloned.1.call-update) | async-done | bytes 10616848 | tf_op jit(solution)/shard_map/all_gather | solution.py:577
  78.7 7.9 convolution_convert_fusion.5.xs_ref
  86.7 8.3 multiply_convert_fusion
  111.4 17.7 %end_states.3 = bf16[32,1152]{1,0:T(8,128)(2,1)} custom-call(bf16[768,72]{1,0:T(8,128)(2,1)} %copy.169.s_ref, bf16[72,2304]{1,0:T(8,128)(2,1)} %copy.170.w_ref, bf16[1,2304]{1,0:T(2,128)(2,1)} %copy.171.b_ref, f32[768,1]{1,0:T(8,128)} %broadcast_in_dim.155.st_ref, bf16[768,2304]{1,0:T(8,128)(2,1)} %copy-done.3, f32[16,2304]{1,0:T(8,128)} %negate_multiply_fusion.a_ref, ...), custom_call_target="tpu_custom_call" | custom-call | flops 84934656 | bytes 7077888 | tf_op jit(solution)/shard_map/end_states/pallas_call | solution.py:387
  138.3 17.7 %end_states.2 = bf16[32,1152]{1,0:T(8,128)(2,1)} custom-call(bf16[768,72]{1,0:T(8,128)(2,1)} %copy.169.s_ref, bf16[72,2304]{1,0:T(8,128)(2,1)} %copy.170.w_ref, bf16[1,2304]{1,0:T(2,128)(2,1)} %copy.171.b_ref, f32[768,1]{1,0:T(8,128)} %broadcast_in_dim.155.st_ref, bf16[768,2304]{1,0:T(8,128)(2,1)} %copy-done.3, f32[16,2304]{1,0:T(8,128)} %negate_multiply_fusion.a_ref, ...), custom_call_target="tpu_custom_call" | custom-call | flops 84934656 | bytes 7077888 | tf_op jit(solution)/shard_map/end_states/pallas_call | solution.py:387
  159.1 8.8 convolution_convert_fusion.6.z_ref
  173.3 42.7 %forward_scan.1 = (bf16[768,2304]{1,0:T(8,128)(2,1)}, bf16[768,2304]{1,0:T(8,128)(2,1)}, bf16[12288,2304]{1,0:T(8,128)(2,1)}, bf16[48,16,2304]{2,1,0:T(8,128)(2,1)}) custom-call(bf16[768,72]{1,0:T(8,128)(2,1)} %copy.169.s_ref, bf16[72,2304]{1,0:T(8,128)(2,1)} %copy.170.w_ref, bf16[1,2304]{1,0:T(2,128)(2,1)} %copy.171.b_ref, ...), custom_call_target="tpu_custom_call" | custom-call | flops 254803968 | bytes 77856768 | tf_op jit(solution)/shard_map/forward_scan/pallas_call | solution.py:403
  216.0 8.5 multiply_reduce_fusion.2
  248.1 10.2 %multiply_convert_fusion.5 = (bf16[384,3072]{1,0:T(8,128)(2,1)}, f32[384,3072]{1,0:T(8,128)}) fusion(bf16[384,1152]{1,0:T(8,128)(2,1)} %convolution_convert_fusion.16, bf16[1,1152,3072]{2,1,0:T(8,128)(2,1)} %all-gather.11.cloned.1.call-done), kind=kOutput, calls=%fused_computation.117 | convolution fusion | flops 2728525824 | bytes 15040512 | tf_op jit(solution)/shard_map/dot_general | solution.py:35
  258.3 8.6 fusion.60
  280.9 46.4 %collective-permute-done.9 = bf16[384,1152]{1,0:T(8,128)(2,1)} collective-permute-done((bf16[384,1152]{1,0:T(8,128)(2,1)}, bf16[384,1152]{1,0:T(8,128)(2,1)}, u32[]{:S(2)}, u32[]{:S(2)}) %collective-permute-start.9) | collective-permute-done | bytes 884768 | tf_op jit(solution)/shard_map/ppermute | solution.py:668
  363.7 7.3 fusion.81
  377.5 25.5 %collective-permute-done.15 = bf16[384,1152]{1,0:T(8,128)(2,1)S(1)} collective-permute-done((bf16[384,1152]{1,0:T(8,128)(2,1)S(1)}, bf16[384,1152]{1,0:T(8,128)(2,1)S(1)}, u32[]{:S(2)}, u32[]{:S(2)}) %collective-permute-start.15) | collective-permute-done | bytes 884768 | tf_op jit(solution)/shard_map/ppermute | solution.py:668
  429.2 17.6 %convolution_convert_fusion.4 = bf16[3072,1152]{1,0:T(8,128)(2,1)} fusion(bf16[384,3072]{1,0:T(8,128)(2,1)} %copy-done.94, bf16[384,3072]{1,0:T(8,128)(2,1)} %fusion.74, bf16[384,3072]{1,0:T(8,128)(2,1)} %copy-done.95, bf16[384,3072]{1,0:T(8,128)(2,1)} %copy-done.93, bf16[384,1152]{1,0:T(8,128)(2,1)} %collective-permute-done.11, ...), kind=kOutput, calls=%fused_computation.4 | convolution fusion | flops 10927079424 | bytes 20054016 | tf_op jit(solution)/shard_map/dot_general | solution.py:488
  446.9 18.3 %convolution_convert_fusion.3 = bf16[3072,1152]{1,0:T(8,128)(2,1)} fusion(bf16[384,3072]{1,0:T(8,128)(2,1)} %copy-done.97, bf16[384,3072]{1,0:T(8,128)(2,1)} %copy-done.98, bf16[384,3072]{1,0:T(8,128)(2,1)} %copy-done.99, bf16[384,3072]{1,0:T(8,128)(2,1)} %get-tuple-element.95, bf16[384,1152]{1,0:T(8,128)(2,1)} %copy-done.87, ...), kind=kOutput, calls=%fused_computation.3 | convolution fusion | flops 10927079424 | bytes 20054016 | tf_op jit(solution)/shard_map/dot_general | solution.py:488
  466.3 7.7 pad_maximum_fusion.1
  485.1 17.6 %collective-permute-done.12 = bf16[384,1152]{1,0:T(8,128)(2,1)} collective-permute-done((bf16[384,1152]{1,0:T(8,128)(2,1)}, bf16[384,1152]{1,0:T(8,128)(2,1)}, u32[]{:S(2)}, u32[]{:S(2)}) %collective-permute-start.12) | collective-permute-done | bytes 884768 | tf_op jit(solution)/shard_map/ppermute | solution.py:668
  502.7 50.5 %collective-permute-done.10 = bf16[384,1152]{1,0:T(8,128)(2,1)} collective-permute-done((bf16[384,1152]{1,0:T(8,128)(2,1)S(1)}, bf16[384,1152]{1,0:T(8,128)(2,1)}, u32[]{:S(2)}, u32[]{:S(2)}) %collective-permute-start.10) | collective-permute-done | bytes 884768 | tf_op jit(solution)/shard_map/ppermute | solution.py:668
  595.5 10.6 %fusion.82 = f32[768,1152]{1,0:T(8,128)} fusion(bf16[768,2304]{1,0:T(8,128)(2,1)} %copy-done.20, bf16[1152,4608]{0,1:T(8,128)(2,1)} %all-gather.7.cloned.1.call-done), kind=kOutput, calls=%fused_computation.119 | convolution fusion | flops 4076863488 | bytes 12386304 | tf_op jit(solution)/shard_map/dot_general | solution.py:484
  606.0 17.1 %start_grads.2 = bf16[16,1152]{1,0:T(8,128)(2,1)} custom-call(bf16[768,72]{1,0:T(8,128)(2,1)} %copy.169.s_ref, bf16[72,2304]{1,0:T(8,128)(2,1)} %copy.170.w_ref, bf16[1,2304]{1,0:T(2,128)(2,1)} %copy.171.b_ref, f32[768,1]{1,0:T(8,128)} %broadcast_in_dim.155.st_ref, f32[768,2304]{1,0:T(8,128)} %get-tuple-element.105.dy_ref, ...), custom_call_target="tpu_custom_call" | custom-call | flops 84934656 | bytes 7077888 | tf_op jit(solution)/shard_map/start_grads/pallas_call | solution.py:421
  627.9 17.2 %start_grads.3 = bf16[16,1152]{1,0:T(8,128)(2,1)} custom-call(bf16[768,72]{1,0:T(8,128)(2,1)} %copy.169.s_ref, bf16[72,2304]{1,0:T(8,128)(2,1)} %copy.170.w_ref, bf16[1,2304]{1,0:T(2,128)(2,1)} %copy.171.b_ref, f32[768,1]{1,0:T(8,128)} %broadcast_in_dim.155.st_ref, f32[768,2304]{1,0:T(8,128)} %get-tuple-element.105.dy_ref, ...), custom_call_target="tpu_custom_call" | custom-call | flops 84934656 | bytes 7077888 | tf_op jit(solution)/shard_map/start_grads/pallas_call | solution.py:421
  666.2 97.0 %backward_scan.1 = (bf16[768,2304]{1,0:T(8,128)(2,1)}, f32[768,2304]{1,0:T(8,128)}, f32[16,2304]{1,0:T(8,128)}, f32[1,2304]{1,0:T(1,128)}, bf16[768,128]{1,0:T(8,128)(2,1)}, /*index=5*/f32[48,8,256]{2,1,0:T(8,128)}) custom-call(bf16[768,72]{1,0:T(8,128)(2,1)} %copy.169.s_ref, bf16[72,2304]{1,0:T(8,128)(2,1)} %copy.170.w_ref, bf16[1,2304]{1,0:T(2,128)(2,1)} %copy.171.b_ref, ...), custom_call_target="tpu_custom_call" | custom-call | flops 509607936 | bytes 77856768 | tf_op jit(solution)/shard_map/backward_scan/pallas_call | solution.py:438
  798.2 18.6 %conv_back.1 = (bf16[784,2304]{1,0:T(8,128)(2,1)}, f32[4,2304]{1,0:T(4,128)}, f32[1,2304]{1,0:T(1,128)}) custom-call(bf16[784,2304]{1,0:T(8,128)(2,1)} %copy-done.2, f32[768,2304]{1,0:T(8,128)} %get-tuple-element.122.du_ref, bf16[768,2304]{1,0:T(8,128)(2,1)} %get-tuple-element.241.slope_ref, bf16[768,104]{1,0:T(8,128)(2,1)} %copy-done.29, ...), custom_call_target="tpu_custom_call" | custom-call | flops 530841600 | bytes 14155776 | tf_op jit(solution)/shard_map/conv_back/pallas_call | solution.py:321
  818.3 9.7 convolution_convert_fusion
  828.0 7.4 fusion.85
  864.3 7.5 collective-permute-done.28
  871.8 19.9 %collective-permute-done.27 = bf16[144,1152]{1,0:T(8,128)(2,1)} collective-permute-done((bf16[144,1152]{1,0:T(8,128)(2,1)}, bf16[144,1152]{1,0:T(8,128)(2,1)}, u32[]{:S(2)}, u32[]{:S(2)}) %collective-permute-start.27) | collective-permute-done | bytes 331808 | tf_op jit(solution)/shard_map/ppermute | solution.py:528
  902.4 22.0 %collective-permute-done.30 = bf16[144,1152]{1,0:T(8,128)(2,1)S(1)} collective-permute-done((bf16[144,1152]{1,0:T(8,128)(2,1)S(1)}, bf16[144,1152]{1,0:T(8,128)(2,1)S(1)}, u32[]{:S(2)}, u32[]{:S(2)}) %collective-permute-start.30) | collective-permute-done | bytes 331808 | tf_op jit(solution)/shard_map/ppermute | solution.py:528
  933.3 12.2 %collective-permute-done.33 = bf16[88,1152]{1,0:T(8,128)(2,1)} collective-permute-done((bf16[88,1152]{1,0:T(8,128)(2,1)}, bf16[88,1152]{1,0:T(8,128)(2,1)}, u32[]{:S(2)}, u32[]{:S(2)}) %collective-permute-start.33) | collective-permute-done | bytes 202784 | tf_op jit(solution)/shard_map/ppermute | solution.py:528
  953.9 12.6 %collective-permute-done.36 = bf16[88,1152]{1,0:T(8,128)(2,1)S(1)} collective-permute-done((bf16[88,1152]{1,0:T(8,128)(2,1)S(1)}, bf16[88,1152]{1,0:T(8,128)(2,1)S(1)}, u32[]{:S(2)}, u32[]{:S(2)}) %collective-permute-start.36) | collective-permute-done | bytes 202784 | tf_op jit(solution)/shard_map/ppermute | solution.py:528
  974.8 8.7 collective-permute-done.38
  (515 shorter events, 366.0 us)
Async XLA Ops:
  7.2 71.5 %all-gather.7.cloned.1.call-start = ((), (), s32[]{:S(2)}) async-start(), calls=%async_computation.5 | async-start | bytes 11943936 | tf_op jit(solution)/shard_map/all_gather | solution.py:577
  7.9 208.0 %all-gather.9.cloned.1.call-start = ((), (), s32[]{:S(2)}) async-start(), calls=%async_computation.6 | async-start | bytes 5971968 | tf_op jit(solution)/shard_map/all_gather | solution.py:590
  8.7 239.4 %all-gather.11.cloned.1.call-start = ((), (), s32[]{:S(2)}) async-start(), calls=%async_computation.12 | async-start | bytes 7962624 | tf_op jit(solution)/shard_map/all_gather | solution.py:591
  9.4 248.8 %all-gather.13.cloned.1.call-start = ((), (), s32[]{:S(2)}) async-start(), calls=%async_computation.13 | async-start | bytes 7962624 | tf_op jit(solution)/shard_map/all_gather | solution.py:592
  42.0 23.9 %collective-permute-start = (bf16[3,1152]{1,0:T(4,128)(2,1)}, bf16[3,1152]{1,0:T(4,128)(2,1)}, u32[]{:S(2)}, u32[]{:S(2)}) collective-permute-start(bf16[3,1152]{1,0:T(4,128)(2,1)} %multiply_convert_fusion.6), channel_id=1, source_target_pairs={{0,1},{1,2},{2,3},{4,5},{5,6},{6,7},{8,9},{9,10},{10,11},{12,13},{... | collective-permute-start | bytes 20744 | tf_op jit(solution)/shard_map/ppermute | solution.py:472
  46.3 559.8 %reduce-scatter.6.cloned.1.call-start = ((), (), s32[]{:S(2)}) async-start(), calls=%async_computation.7 | async-start | bytes 7962624 | tf_op jit(solution)/shard_map/reduce_scatter | solution.py:704
  129.1 43.3 %collective-permute-start.3 = (bf16[32,1152]{1,0:T(8,128)(2,1)}, bf16[32,1152]{1,0:T(8,128)(2,1)S(1)}, u32[]{:S(2)}, u32[]{:S(2)}) collective-permute-start(bf16[32,1152]{1,0:T(8,128)(2,1)} %end_states.3), channel_id=1, source_target_pairs={{0,3},{4,7},{8,11},{12,15},{16,19},{20,23},{24,27},{28,31}} | collective-permute-start | bytes 221192 | tf_op jit(solution)/shard_map/ppermute | solution.py:472
  134.6 34.4 %collective-permute-start.2 = (bf16[32,1152]{1,0:T(8,128)(2,1)}, bf16[32,1152]{1,0:T(8,128)(2,1)S(1)}, u32[]{:S(2)}, u32[]{:S(2)}) collective-permute-start(bf16[32,1152]{1,0:T(8,128)(2,1)} %end_states.3), channel_id=1, source_target_pairs={{0,2},{1,3},{4,6},{5,7},{8,10},{9,11},{12,14},{13,15},{16,18},{17,... | collective-permute-start | bytes 221192 | tf_op jit(solution)/shard_map/ppermute | solution.py:472
  135.9 34.6 %collective-permute-start.1 = (bf16[32,1152]{1,0:T(8,128)(2,1)}, bf16[32,1152]{1,0:T(8,128)(2,1)S(1)}, u32[]{:S(2)}, u32[]{:S(2)}) collective-permute-start(bf16[32,1152]{1,0:T(8,128)(2,1)} %end_states.3), channel_id=1, source_target_pairs={{0,1},{1,2},{2,3},{4,5},{5,6},{6,7},{8,9},{9,10},{10,11},{12,13},{... | collective-permute-start | bytes 221192 | tf_op jit(solution)/shard_map/ppermute | solution.py:472
  228.5 48.6 %collective-permute-start.11 = (bf16[384,1152]{1,0:T(8,128)(2,1)}, bf16[384,1152]{1,0:T(8,128)(2,1)}, u32[]{:S(2)}, u32[]{:S(2)}) collective-permute-start(bf16[384,1152]{1,0:T(8,128)(2,1)} %convolution_convert_fusion.10), channel_id=1, source_target_pairs={{0,3},{1,2},{2,1},{3,0},{4,7},{5,6},{6,5},{7,4},{8,11},{9,10},{10,... | collective-permute-start | bytes 2654216 | tf_op jit(solution)/shard_map/ppermute | solution.py:668
  234.7 92.6 %collective-permute-start.9 = (bf16[384,1152]{1,0:T(8,128)(2,1)}, bf16[384,1152]{1,0:T(8,128)(2,1)}, u32[]{:S(2)}, u32[]{:S(2)}) collective-permute-start(bf16[384,1152]{1,0:T(8,128)(2,1)} %convolution_convert_fusion.12), channel_id=1, source_target_pairs={{0,2},{1,3},{2,0},{3,1},{4,6},{5,7},{6,4},{7,5},{8,10},{9,11},{10,... | collective-permute-start | bytes 2654216 | tf_op jit(solution)/shard_map/ppermute | solution.py:668
  236.6 90.6 %collective-permute-start.7 = (bf16[384,1152]{1,0:T(8,128)(2,1)}, bf16[384,1152]{1,0:T(8,128)(2,1)}, u32[]{:S(2)}, u32[]{:S(2)}) collective-permute-start(bf16[384,1152]{1,0:T(8,128)(2,1)} %convolution_convert_fusion.14), channel_id=1, source_target_pairs={{0,1},{1,0},{2,3},{3,2},{4,5},{5,4},{6,7},{7,6},{8,9},{9,8},{10,11... | collective-permute-start | bytes 2654216 | tf_op jit(solution)/shard_map/ppermute | solution.py:668
  277.1 85.7 %collective-permute-start.17 = (bf16[384,1152]{1,0:T(8,128)(2,1)S(1)}, bf16[384,1152]{1,0:T(8,128)(2,1)S(1)}, u32[]{:S(2)}, u32[]{:S(2)}) collective-permute-start(bf16[384,1152]{1,0:T(8,128)(2,1)S(1)} %copy-done.91), channel_id=1, source_target_pairs={{0,3},{1,2},{2,1},{3,0},{4,7},{5,6},{6,5},{7,4},{8,11},{9,10},{10,... | collective-permute-start | bytes 2654216 | tf_op jit(solution)/shard_map/ppermute | solution.py:668
  327.3 75.7 %collective-permute-start.15 = (bf16[384,1152]{1,0:T(8,128)(2,1)S(1)}, bf16[384,1152]{1,0:T(8,128)(2,1)S(1)}, u32[]{:S(2)}, u32[]{:S(2)}) collective-permute-start(bf16[384,1152]{1,0:T(8,128)(2,1)S(1)} %copy-done.90), channel_id=1, source_target_pairs={{0,2},{1,3},{2,0},{3,1},{4,6},{5,7},{6,4},{7,5},{8,10},{9,11},{10,... | collective-permute-start | bytes 2654216 | tf_op jit(solution)/shard_map/ppermute | solution.py:668
  327.3 88.3 %collective-permute-start.13 = (bf16[384,1152]{1,0:T(8,128)(2,1)S(1)}, bf16[384,1152]{1,0:T(8,128)(2,1)S(1)}, u32[]{:S(2)}, u32[]{:S(2)}) collective-permute-start(bf16[384,1152]{1,0:T(8,128)(2,1)S(1)} %convolution_convert_fusion.15), channel_id=1, source_target_pairs={{0,1},{1,0},{2,3},{3,2},{4,5},{5,4},{6,7},{7,6},{8,9},{9,8},{10,11... | collective-permute-start | bytes 2654216 | tf_op jit(solution)/shard_map/ppermute | solution.py:668
  376.6 88.6 %collective-permute-start.18 = (bf16[384,1152]{1,0:T(8,128)(2,1)}, bf16[384,1152]{1,0:T(8,128)(2,1)S(1)}, u32[]{:S(2)}, u32[]{:S(2)}) collective-permute-start(bf16[384,1152]{1,0:T(8,128)(2,1)} %fusion.140), channel_id=1, source_target_pairs={{0,3},{1,2},{2,1},{3,0},{4,7},{5,6},{6,5},{7,4},{8,11},{9,10},{10,... | collective-permute-start | bytes 2654216 | tf_op jit(solution)/shard_map/ppermute | solution.py:668
  415.5 49.7 %collective-permute-start.16 = (bf16[384,1152]{1,0:T(8,128)(2,1)}, bf16[384,1152]{1,0:T(8,128)(2,1)S(1)}, u32[]{:S(2)}, u32[]{:S(2)}) collective-permute-start(bf16[384,1152]{1,0:T(8,128)(2,1)} %fusion.137), channel_id=1, source_target_pairs={{0,2},{1,3},{2,0},{3,1},{4,6},{5,7},{6,4},{7,5},{8,10},{9,11},{10,... | collective-permute-start | bytes 2654216 | tf_op jit(solution)/shard_map/ppermute | solution.py:668
  425.8 40.5 %collective-permute-start.14 = (bf16[384,1152]{1,0:T(8,128)(2,1)}, bf16[384,1152]{1,0:T(8,128)(2,1)S(1)}, u32[]{:S(2)}, u32[]{:S(2)}) collective-permute-start(bf16[384,1152]{1,0:T(8,128)(2,1)} %fusion.134), channel_id=1, source_target_pairs={{0,1},{1,0},{2,3},{3,2},{4,5},{5,4},{6,7},{7,6},{8,9},{9,8},{10,11... | collective-permute-start | bytes 2654216 | tf_op jit(solution)/shard_map/ppermute | solution.py:668
  477.8 179.8 %reduce-scatter.8.cloned.1.call-start = ((), (), s32[]{:S(2)}) async-start(), calls=%async_computation.8 | async-start | bytes 7962624 | tf_op jit(solution)/shard_map/reduce_scatter | solution.py:705
  477.9 24.8 %collective-permute-start.12 = (bf16[384,1152]{1,0:T(8,128)(2,1)}, bf16[384,1152]{1,0:T(8,128)(2,1)}, u32[]{:S(2)}, u32[]{:S(2)}) collective-permute-start(bf16[384,1152]{1,0:T(8,128)(2,1)} %fusion.152), channel_id=1, source_target_pairs={{0,3},{1,2},{2,1},{3,0},{4,7},{5,6},{6,5},{7,4},{8,11},{9,10},{10,... | collective-permute-start | bytes 2654216 | tf_op jit(solution)/shard_map/ppermute | solution.py:668
  479.4 73.8 %collective-permute-start.10 = (bf16[384,1152]{1,0:T(8,128)(2,1)S(1)}, bf16[384,1152]{1,0:T(8,128)(2,1)}, u32[]{:S(2)}, u32[]{:S(2)}) collective-permute-start(bf16[384,1152]{1,0:T(8,128)(2,1)S(1)} %copy-done.86), channel_id=1, source_target_pairs={{0,2},{1,3},{2,0},{3,1},{4,6},{5,7},{6,4},{7,5},{8,10},{9,11},{10,... | collective-permute-start | bytes 2654216 | tf_op jit(solution)/shard_map/ppermute | solution.py:668
  479.4 73.8 %collective-permute-start.8 = (bf16[384,1152]{1,0:T(8,128)(2,1)S(1)}, bf16[384,1152]{1,0:T(8,128)(2,1)}, u32[]{:S(2)}, u32[]{:S(2)}) collective-permute-start(bf16[384,1152]{1,0:T(8,128)(2,1)S(1)} %copy-done.85), channel_id=1, source_target_pairs={{0,1},{1,0},{2,3},{3,2},{4,5},{5,4},{6,7},{7,6},{8,9},{9,8},{10,11... | collective-permute-start | bytes 2654216 | tf_op jit(solution)/shard_map/ppermute | solution.py:668
  485.0 282.4 %reduce-scatter.10.cloned.1.call-start = ((), (), s32[]{:S(2)}) async-start(), calls=%async_computation.9 | async-start | bytes 5971968 | tf_op jit(solution)/shard_map/reduce_scatter | solution.py:747
  623.9 32.2 %collective-permute-start.21 = (bf16[24,1152]{1,0:T(8,128)(2,1)S(1)}, bf16[24,1152]{1,0:T(8,128)(2,1)}, u32[]{:S(2)}, u32[]{:S(2)}) collective-permute-start(bf16[24,1152]{1,0:T(8,128)(2,1)S(1)} %pad_maximum_fusion.6), channel_id=1, source_target_pairs={{3,0},{7,4},{11,8},{15,12},{19,16},{23,20},{27,24},{31,28}} | collective-permute-start | bytes 165896 | tf_op jit(solution)/shard_map/ppermute | solution.py:472
  625.3 23.2 %collective-permute-start.20 = (bf16[24,1152]{1,0:T(8,128)(2,1)S(1)}, bf16[24,1152]{1,0:T(8,128)(2,1)S(1)}, u32[]{:S(2)}, u32[]{:S(2)}) collective-permute-start(bf16[24,1152]{1,0:T(8,128)(2,1)S(1)} %pad_maximum_fusion.6), channel_id=1, source_target_pairs={{2,0},{3,1},{6,4},{7,5},{10,8},{11,9},{14,12},{15,13},{18,16},{19,... | collective-permute-start | bytes 165896 | tf_op jit(solution)/shard_map/ppermute | solution.py:472
  626.6 23.2 %collective-permute-start.19 = (bf16[24,1152]{1,0:T(8,128)(2,1)S(1)}, bf16[24,1152]{1,0:T(8,128)(2,1)S(1)}, u32[]{:S(2)}, u32[]{:S(2)}) collective-permute-start(bf16[24,1152]{1,0:T(8,128)(2,1)S(1)} %pad_maximum_fusion.6), channel_id=1, source_target_pairs={{1,0},{2,1},{3,2},{5,4},{6,5},{7,6},{9,8},{10,9},{11,10},{13,12},{... | collective-permute-start | bytes 165896 | tf_op jit(solution)/shard_map/ppermute | solution.py:472
  657.7 117.0 %reduce-scatter.12.cloned.1.call-start = ((), (), s32[]{:S(2)}) async-start(), calls=%async_computation.10 | async-start | bytes 5971968 | tf_op jit(solution)/shard_map/reduce_scatter | solution.py:748
  658.5 266.4 %reduce-scatter.14.cloned.1.call-start = ((), (), s32[]{:S(2)}) async-start(), calls=%async_computation.11 | async-start | bytes 7299072 | tf_op jit(solution)/shard_map/reduce_scatter | solution.py:786
  863.2 28.5 %collective-permute-start.27 = (bf16[144,1152]{1,0:T(8,128)(2,1)}, bf16[144,1152]{1,0:T(8,128)(2,1)}, u32[]{:S(2)}, u32[]{:S(2)}) collective-permute-start(bf16[144,1152]{1,0:T(8,128)(2,1)} %get-tuple-element.256), channel_id=1, source_target_pairs={{0,2},{1,3},{2,0},{3,1},{4,6},{5,7},{6,4},{7,5},{8,10},{9,11},{10,... | collective-permute-start | bytes 995336 | tf_op jit(solution)/shard_map/ppermute | solution.py:528
  863.2 28.5 %collective-permute-start.26 = (bf16[144,1152]{1,0:T(8,128)(2,1)S(1)}, bf16[144,1152]{1,0:T(8,128)(2,1)}, u32[]{:S(2)}, u32[]{:S(2)}) collective-permute-start(bf16[144,1152]{1,0:T(8,128)(2,1)S(1)} %get-tuple-element.255), channel_id=1, source_target_pairs={{0,1},{1,2},{2,3},{3,0},{4,5},{5,6},{6,7},{7,4},{8,9},{9,10},{10,1... | collective-permute-start | bytes 995336 | tf_op jit(solution)/shard_map/ppermute | solution.py:528
  897.8 26.6 %collective-permute-start.30 = (bf16[144,1152]{1,0:T(8,128)(2,1)S(1)}, bf16[144,1152]{1,0:T(8,128)(2,1)S(1)}, u32[]{:S(2)}, u32[]{:S(2)}) collective-permute-start(bf16[144,1152]{1,0:T(8,128)(2,1)S(1)} %fusion.182), channel_id=1, source_target_pairs={{0,2},{1,3},{2,0},{3,1},{4,6},{5,7},{6,4},{7,5},{8,10},{9,11},{10,... | collective-permute-start | bytes 995336 | tf_op jit(solution)/shard_map/ppermute | solution.py:528
  900.5 24.0 %collective-permute-start.31 = (bf16[144,1152]{1,0:T(8,128)(2,1)S(1)}, bf16[144,1152]{1,0:T(8,128)(2,1)S(1)}, u32[]{:S(2)}, u32[]{:S(2)}) collective-permute-start(bf16[144,1152]{1,0:T(8,128)(2,1)S(1)} %fusion.182), channel_id=1, source_target_pairs={{0,1},{1,2},{2,3},{3,0},{4,5},{5,6},{6,7},{7,4},{8,9},{9,10},{10,1... | collective-permute-start | bytes 995336 | tf_op jit(solution)/shard_map/ppermute | solution.py:528
  (119 other events, 1998.7 us)
Sparse Core Ops, SparseCore 0:
  9.9 68.7 all-gather.6
  80.6 41.6 all-gather.8
  124.2 49.1 all-gather.10
  175.2 49.7 all-gather.12
  478.0 63.8 reduce-scatter.5
  545.6 65.4 reduce-scatter.7
  657.8 55.9 reduce-scatter.9
  717.6 57.0 reduce-scatter.11
  856.6 63.8 reduce-scatter.13

commit v6 on v5

--- a/solution.py
+++ b/solution.py
@@ -9,7 +9,7 @@
 
 TC = 16
 ROWS = 256
-CONV_ROWS = 128
+CONV_ROWS = 256
 PAD = 16
 UNROLL = 8
 FAR = 1e4
@@ -163,7 +163,7 @@
 
 def backward_kernel(
     s_ref, w_ref, b_ref, st_ref, u_ref, dy_ref, a_ref, skip_ref, cb_ref, bm_ref, om_ref, hs_ref, ck_ref, g0_ref,
-    ds_ref, du_ref, da_ref, dskip_ref, db_ref, dc_ref,
+    ds_ref, du_ref, da_ref, dskip_ref, dbias_ref, db_ref, dc_ref,
     pre_ref, dk_ref, dv_ref, q_ref, p_ref, lb0, lb1, wb0, wb1, grad_ref, accb_ref, accc_ref,
 ):
     step, seg = pl.program_id(0), pl.program_id(1)
@@ -185,6 +185,7 @@
         grad_ref[...] = g0_ref[...]
         da_ref[...] = jnp.zeros_like(da_ref)
         dskip_ref[...] = jnp.zeros_like(dskip_ref)
+        dbias_ref[...] = jnp.zeros_like(dbias_ref)
 
     a = a_ref[...]
     a_low = a.astype(BF16)
@@ -245,11 +246,19 @@
         pre = pre_ref[r, :]
         delta = jnp.maximum(pre, 0.0) + jnp.log1p(jnp.exp(-jnp.abs(pre)))
         dd = p_ref[r, :] * LN2 + u * q
-        ds_ref[r, :] = (dd / (1.0 + jnp.exp(-pre))).astype(BF16)
+        ds = (dd / (1.0 + jnp.exp(-pre))).astype(BF16)
+        ds_ref[r, :] = ds
         du_ref[r, :] = delta * q + dy * skip_ref[...].astype(F32)
-        return carry + jnp.sum(dy * u, axis=0, keepdims=True)
-
-    dskip_ref[...] += lax.fori_loop(0, rows // size, finish, jnp.zeros(dskip_ref.shape, F32))
+        skip, bias = carry
+        return (
+            skip + jnp.sum(dy * u, axis=0, keepdims=True),
+            bias + jnp.sum(ds.astype(F32), axis=0, keepdims=True),
+        )
+
+    zero = jnp.zeros(dskip_ref.shape, F32)
+    skip, bias = lax.fori_loop(0, rows // size, finish, (zero, zero))
+    dskip_ref[...] += skip
+    dbias_ref[...] += bias
 
     @pl.when((step == pl.num_programs(0) - 1) & (last == 0))
     def _():
@@ -440,8 +449,8 @@
         grid=k.grid,
         in_specs=[k.token(s.shape[1]), k.channel(w.shape[0]), k.channel(1), k.token(1), k.both(), k.both(), k.channel(states), k.channel(1),
                   k.lead(k.seg, states, 128), k.lead(k.seg // TC, *bm.shape[1:]), k.whole(om.shape), k.both(states), k.marks(states), k.channel(states)],
-        out_specs=[k.both(), k.both(), k.channel(states), k.channel(1), k.whole((rows, 128)), k.whole((chunks, 8, TC * states))],
-        out_shape=[sds((rows, width), BF16), sds((rows, width), F32), sds((states, width), F32), sds((1, width), F32),
+        out_specs=[k.both(), k.both(), k.channel(states), k.channel(1), k.channel(1), k.whole((rows, 128)), k.whole((chunks, 8, TC * states))],
+        out_shape=[sds((rows, width), BF16), sds((rows, width), F32), sds((states, width), F32), sds((1, width), F32), sds((1, width), F32),
                    sds((rows, 128), BF16), sds((chunks, 8, TC * states), F32)],
         scratch_shapes=[pltpu.VMEM((k.seg, k.cb), F32)] * 5
         + [pltpu.VMEM((TC * states, k.cb), BF16)] * 4
@@ -746,12 +755,11 @@
     )
     sum_output = lax.psum_scatter(grad_output_w, "dp", scatter_dimension=0, tiled=True)
     sum_input_z = lax.psum_scatter(grad_input_z, "dp", scatter_dimension=0, tiled=True)
-    grad_pre_step, grad_inner, grad_decay_t, grad_skip, grad_b, grad_c = backward_scan(
+    grad_pre_step, grad_inner, grad_decay_t, grad_skip, grad_step_bias, grad_b, grad_c = backward_scan(
         step_low, w_step, bias2, st, inner_low, grad_scanned, rate2, skip2,
         c_wide, b_block, one_block, history, marks, later_grad,
     )
     grad_pre_step, sum_output, sum_input_z = lax.optimization_barrier((grad_pre_step, sum_output, sum_input_z))
-    grad_step_bias = jnp.sum(grad_pre_step.astype(F32), axis=0, keepdims=True)
     grad_step_w = contract(step_low, grad_pre_step)
     grad_step_low = product_back(grad_pre_step, w_step).astype(BF16)
     grad_selected = jnp.concatenate(
@@ -775,13 +783,17 @@
     returned_edge = shifted(grad_norm_x[PAD - taps + 1 : PAD], "expert", -1) * edge_keep
     grad_norm_one = grad_norm_x[PAD:] + grad_norm_z + jnp.pad(returned_edge, ((rows - taps + 1, 0), (0, 0)))
     grad_norm_gain = jnp.sum(grad_norm_one * hidden_in * norm_r, axis=0, keepdims=True)
-    grad_input_x = halved(contract(grad_conv_in, norm_low).astype(BF16), devices)
+    grad_input_x = contract(grad_conv_in, norm_low).astype(BF16)
     tiny = jnp.concatenate([shares(jnp.concatenate([grad_kernel, grad_conv_b]), devices), shares(grad_norm_gain, devices)], 1)
     rest = jnp.concatenate([summed, tiny.astype(BF16)], 1)
     more = -(-rest.shape[1] // model)
     more += -(more + share) % (8 * groups)
     rest = jnp.pad(rest, ((0, 0), (0, more * model - rest.shape[1]))).reshape(devices, more, model)
-    packed = jnp.concatenate([grad_input_x, rest], axis=1).reshape(devices * (share + more), model)
+    pieces = []
+    for d in range(devices):
+        block = d % (devices // 2) * 2 + d // (devices // 2)
+        pieces += [grad_input_x[block * share : (block + 1) * share], rest[d]]
+    packed = jnp.concatenate(pieces)
     packed, sum_output, sum_input_z = lax.optimization_barrier((packed, sum_output, sum_input_z))
     packed = lax.psum_scatter(packed, "dp", scatter_dimension=0, tiled=True)
     sum_output, sum_input_z = expert_sum(sum_output, sum_input_z)

time: 1000 us -> 1020 us (1.020)
  local copies, waits for them, and re-layouts: 89.3 us -> 120 us
    unnamed x237 -> x254, local copies, waits for them, and re-layouts: 29.1 us -> 50.1 us
  transfers between devices with their start and end apart: 48 -> 48, of which waited for: 17 -> 18; matrix products, arithmetic and copies ran while one was open for 33% -> 32% of each run, Pallas kernels for 21% -> 21%
where the time goes in v6:
time: 1020 us; the launch traced here: 1010 us
  waiting for transfers between devices  255 us (25%)
  matrix products  240 us (24%)
  Pallas kernels  227 us (22%)
  local copies, waits for them, and re-layouts  120 us (12%)
  other arithmetic  72 us (7%)
  starting transfers between devices  63.3 us (6%)
  between operations  17.4 us (2%)
  blocking collectives  17.2 us (2%)
    ppermute x12, waiting for transfers between devices, swapped(): lax.ppermute(x, 'expert', [(i, i ^ k) for i in range(groups)])  141 us
    pallas_call x1, Pallas kernels, backward_scan(): pl.pallas_call(backward_kernel, grid=k.grid, in_specs=[k.token(s.shape[1]...  97.6 us
    dot_general x20, matrix products, dot(): return jnp.dot(a, b, preferred_element_type=F32)  86.9 us
    ppermute x12, waiting for transfers between devices, turned(): lax.ppermute(x, 'expert', [(i, (i + k) % n) for i in range(n)])  75.1 us
    dot_general x13, matrix products, product_back(): lax.dot_general(left, right, (((1,), (1,)), ((), ())), preferred_element_...  74.8 us
    dot_general x9, matrix products, contract(): lax.dot_general(left, right, (((0,), (0,)), ((), ())), preferred_element_...  70.1 us
    unnamed x254, local copies, waits for them, and re-layouts  50.1 us
    pallas_call x1, Pallas kernels, forward_scan(): pl.pallas_call(forward_kernel, grid=k.grid, in_specs=[k.token(s.shape[1])...  42.7 us
  transfers between devices with their start and end apart: 48, of which 18 were waited for; matrix products, arithmetic and copies ran while one was open for 32% of the time, Pallas kernels for 21%

profile of v6, /device:TPU:4, one launch (start us, length us, event | category | flops | bytes accessed | tf_op | source)
XLA Modules:
  0.0 1012.4 jit_solution(12102095315212512504)
XLA Ops:
  17.8 17.2 %all_gather.15 = bf16[208,2304]{0,1:T(8,128)(2,1)S(1)} all-gather(bf16[208,288]{0,1:T(8,128)(2,1)S(1)} %pad.21), channel_id=1, replica_groups=mesh['dp'=8,'expert'=4] {'dp'}, dimensions={1}, use_global_device_ids=true | all-gather | bytes 1078272 | tf_op jit(solution)/shard_map/all_gather | solution.py:595
  69.3 10.0 all-gather.7.cloned.1.call-done
  79.3 7.9 convolution_convert_fusion.5.xs_ref
  87.3 8.3 multiply_convert_fusion
  112.0 17.7 %end_states.3 = bf16[32,1152]{1,0:T(8,128)(2,1)} custom-call(bf16[768,72]{1,0:T(8,128)(2,1)} %copy.161.s_ref, bf16[72,2304]{1,0:T(8,128)(2,1)} %copy.162.w_ref, bf16[1,2304]{1,0:T(2,128)(2,1)} %copy.163.b_ref, f32[768,1]{1,0:T(8,128)} %broadcast_in_dim.154.st_ref, bf16[768,2304]{1,0:T(8,128)(2,1)} %copy-done.3, f32[16,2304]{1,0:T(8,128)} %negate_multiply_fusion.a_ref, ...), custom_call_target="tpu_custom_call" | custom-call | flops 84934656 | bytes 7077888 | tf_op jit(solution)/shard_map/end_states/pallas_call | solution.py:396
  138.9 17.7 %end_states.2 = bf16[32,1152]{1,0:T(8,128)(2,1)} custom-call(bf16[768,72]{1,0:T(8,128)(2,1)} %copy.161.s_ref, bf16[72,2304]{1,0:T(8,128)(2,1)} %copy.162.w_ref, bf16[1,2304]{1,0:T(2,128)(2,1)} %copy.163.b_ref, f32[768,1]{1,0:T(8,128)} %broadcast_in_dim.154.st_ref, bf16[768,2304]{1,0:T(8,128)(2,1)} %copy-done.3, f32[16,2304]{1,0:T(8,128)} %negate_multiply_fusion.a_ref, ...), custom_call_target="tpu_custom_call" | custom-call | flops 84934656 | bytes 7077888 | tf_op jit(solution)/shard_map/end_states/pallas_call | solution.py:396
  159.6 8.8 convolution_convert_fusion.6.z_ref
  173.8 42.7 %forward_scan.1 = (bf16[768,2304]{1,0:T(8,128)(2,1)}, bf16[768,2304]{1,0:T(8,128)(2,1)}, bf16[12288,2304]{1,0:T(8,128)(2,1)}, bf16[48,16,2304]{2,1,0:T(8,128)(2,1)}) custom-call(bf16[768,72]{1,0:T(8,128)(2,1)} %copy.161.s_ref, bf16[72,2304]{1,0:T(8,128)(2,1)} %copy.162.w_ref, bf16[1,2304]{1,0:T(2,128)(2,1)} %copy.163.b_ref, ...), custom_call_target="tpu_custom_call" | custom-call | flops 254803968 | bytes 77856768 | tf_op jit(solution)/shard_map/forward_scan/pallas_call | solution.py:412
  216.5 8.5 multiply_reduce_fusion.2
  248.5 10.2 %multiply_convert_fusion.5 = (bf16[384,3072]{1,0:T(8,128)(2,1)}, f32[384,3072]{1,0:T(8,128)}) fusion(bf16[384,1152]{1,0:T(8,128)(2,1)} %convolution_convert_fusion.16, bf16[1,1152,3072]{2,1,0:T(8,128)(2,1)} %all-gather.11.cloned.1.call-done), kind=kOutput, calls=%fused_computation.116 | convolution fusion | flops 2728525824 | bytes 15040512 | tf_op jit(solution)/shard_map/dot_general | solution.py:35
  258.7 8.6 fusion.60
  281.2 46.5 %collective-permute-done.9 = bf16[384,1152]{1,0:T(8,128)(2,1)} collective-permute-done((bf16[384,1152]{1,0:T(8,128)(2,1)}, bf16[384,1152]{1,0:T(8,128)(2,1)}, u32[]{:S(2)}, u32[]{:S(2)}) %collective-permute-start.9) | collective-permute-done | bytes 884768 | tf_op jit(solution)/shard_map/ppermute | solution.py:677
  331.3 7.3 multiply_convert_fusion.2
  378.1 25.4 %collective-permute-done.15 = bf16[384,1152]{1,0:T(8,128)(2,1)S(1)} collective-permute-done((bf16[384,1152]{1,0:T(8,128)(2,1)S(1)}, bf16[384,1152]{1,0:T(8,128)(2,1)S(1)}, u32[]{:S(2)}, u32[]{:S(2)}) %collective-permute-start.15) | collective-permute-done | bytes 884768 | tf_op jit(solution)/shard_map/ppermute | solution.py:677
  429.8 17.6 %convolution_convert_fusion.4 = bf16[3072,1152]{1,0:T(8,128)(2,1)} fusion(bf16[384,3072]{1,0:T(8,128)(2,1)} %copy-done.95, bf16[384,3072]{1,0:T(8,128)(2,1)} %fusion.74, bf16[384,3072]{1,0:T(8,128)(2,1)} %copy-done.96, bf16[384,3072]{1,0:T(8,128)(2,1)} %copy-done.94, bf16[384,1152]{1,0:T(8,128)(2,1)} %collective-permute-done.11, ...), kind=kOutput, calls=%fused_computation.4 | convolution fusion | flops 10927079424 | bytes 20054016 | tf_op jit(solution)/shard_map/dot_general | solution.py:497
  447.4 18.4 %convolution_convert_fusion.3 = bf16[3072,1152]{1,0:T(8,128)(2,1)} fusion(bf16[384,3072]{1,0:T(8,128)(2,1)} %copy-done.98, bf16[384,3072]{1,0:T(8,128)(2,1)} %copy-done.99, bf16[384,3072]{1,0:T(8,128)(2,1)} %copy-done.100, bf16[384,3072]{1,0:T(8,128)(2,1)} %get-tuple-element.96, bf16[384,1152]{1,0:T(8,128)(2,1)} %copy-done.88, ...), kind=kOutput, calls=%fused_computation.3 | convolution fusion | flops 10927079424 | bytes 20054016 | tf_op jit(solution)/shard_map/dot_general | solution.py:497
  466.8 8.0 pad_maximum_fusion
  485.9 17.6 %collective-permute-done.12 = bf16[384,1152]{1,0:T(8,128)(2,1)} collective-permute-done((bf16[384,1152]{1,0:T(8,128)(2,1)}, bf16[384,1152]{1,0:T(8,128)(2,1)}, u32[]{:S(2)}, u32[]{:S(2)}) %collective-permute-start.12) | collective-permute-done | bytes 884768 | tf_op jit(solution)/shard_map/ppermute | solution.py:677
  503.5 50.5 %collective-permute-done.10 = bf16[384,1152]{1,0:T(8,128)(2,1)} collective-permute-done((bf16[384,1152]{1,0:T(8,128)(2,1)S(1)}, bf16[384,1152]{1,0:T(8,128)(2,1)}, u32[]{:S(2)}, u32[]{:S(2)}) %collective-permute-start.10) | collective-permute-done | bytes 884768 | tf_op jit(solution)/shard_map/ppermute | solution.py:677
  596.3 10.2 %fusion.82 = f32[768,1152]{1,0:T(8,128)} fusion(bf16[768,2304]{1,0:T(8,128)(2,1)} %copy-done.21, bf16[1152,4608]{0,1:T(8,128)(2,1)} %all-gather.7.cloned.1.call-done), kind=kOutput, calls=%fused_computation.118 | convolution fusion | flops 4076863488 | bytes 12386304 | tf_op jit(solution)/shard_map/dot_general | solution.py:493
  606.5 17.1 %start_grads.2 = bf16[16,1152]{1,0:T(8,128)(2,1)} custom-call(bf16[768,72]{1,0:T(8,128)(2,1)} %copy.161.s_ref, bf16[72,2304]{1,0:T(8,128)(2,1)} %copy.162.w_ref, bf16[1,2304]{1,0:T(2,128)(2,1)} %copy.163.b_ref, f32[768,1]{1,0:T(8,128)} %broadcast_in_dim.154.st_ref, f32[768,2304]{1,0:T(8,128)} %get-tuple-element.106.dy_ref, ...), custom_call_target="tpu_custom_call" | custom-call | flops 84934656 | bytes 7077888 | tf_op jit(solution)/shard_map/start_grads/pallas_call | solution.py:430
  628.5 17.2 %start_grads.3 = bf16[16,1152]{1,0:T(8,128)(2,1)} custom-call(bf16[768,72]{1,0:T(8,128)(2,1)} %copy.161.s_ref, bf16[72,2304]{1,0:T(8,128)(2,1)} %copy.162.w_ref, bf16[1,2304]{1,0:T(2,128)(2,1)} %copy.163.b_ref, f32[768,1]{1,0:T(8,128)} %broadcast_in_dim.154.st_ref, f32[768,2304]{1,0:T(8,128)} %get-tuple-element.106.dy_ref, ...), custom_call_target="tpu_custom_call" | custom-call | flops 84934656 | bytes 7077888 | tf_op jit(solution)/shard_map/start_grads/pallas_call | solution.py:430
  667.4 97.6 %backward_scan.1 = (bf16[768,2304]{1,0:T(8,128)(2,1)}, f32[768,2304]{1,0:T(8,128)}, f32[16,2304]{1,0:T(8,128)}, f32[1,2304]{1,0:T(1,128)}, f32[1,2304]{1,0:T(1,1...) custom-call(bf16[768,72]{1,0:T(8,128)(2,1)} %copy.161.s_ref, bf16[72,2304]{1,0:T(8,128)(2,1)} %copy.162.w_ref, ...), custom_call_target="tpu_custom_call" | custom-call | flops 509607936 | bytes 77856768 | tf_op jit(solution)/shard_map/backward_scan/pallas_call | solution.py:447
  796.4 17.4 %conv_back.1 = (bf16[784,2304]{1,0:T(8,128)(2,1)}, f32[4,2304]{1,0:T(4,128)}, f32[1,2304]{1,0:T(1,128)}) custom-call(bf16[784,2304]{1,0:T(8,128)(2,1)} %copy-done.2, f32[768,2304]{1,0:T(8,128)} %get-tuple-element.124.du_ref, bf16[768,2304]{1,0:T(8,128)(2,1)} %get-tuple-element.251.slope_ref, bf16[768,104]{1,0:T(8,128)(2,1)} %copy-done.30, ...), custom_call_target="tpu_custom_call" | custom-call | flops 530841600 | bytes 14155776 | tf_op jit(solution)/shard_map/conv_back/pallas_call | solution.py:330
  813.8 8.1 convolution_convert_fusion
  824.6 7.5 fusion.85
  845.5 9.7 fusion.201
  889.7 20.6 %collective-permute-done.27 = bf16[144,1152]{1,0:T(8,128)(2,1)} collective-permute-done((bf16[144,1152]{1,0:T(8,128)(2,1)}, bf16[144,1152]{1,0:T(8,128)(2,1)}, u32[]{:S(2)}, u32[]{:S(2)}) %collective-permute-start.27) | collective-permute-done | bytes 331808 | tf_op jit(solution)/shard_map/ppermute | solution.py:537
  920.4 22.6 %collective-permute-done.30 = bf16[144,1152]{1,0:T(8,128)(2,1)S(1)} collective-permute-done((bf16[144,1152]{1,0:T(8,128)(2,1)S(1)}, bf16[144,1152]{1,0:T(8,128)(2,1)S(1)}, u32[]{:S(2)}, u32[]{:S(2)}) %collective-permute-start.30) | collective-permute-done | bytes 331808 | tf_op jit(solution)/shard_map/ppermute | solution.py:537
  953.2 10.9 %collective-permute-done.33 = bf16[88,1152]{1,0:T(8,128)(2,1)} collective-permute-done((bf16[88,1152]{1,0:T(8,128)(2,1)}, bf16[88,1152]{1,0:T(8,128)(2,1)}, u32[]{:S(2)}, u32[]{:S(2)}) %collective-permute-start.33) | collective-permute-done | bytes 202784 | tf_op jit(solution)/shard_map/ppermute | solution.py:537
  973.3 12.6 %collective-permute-done.36 = bf16[88,1152]{1,0:T(8,128)(2,1)S(1)} collective-permute-done((bf16[88,1152]{1,0:T(8,128)(2,1)S(1)}, bf16[88,1152]{1,0:T(8,128)(2,1)S(1)}, u32[]{:S(2)}, u32[]{:S(2)}) %collective-permute-start.36) | collective-permute-done | bytes 202784 | tf_op jit(solution)/shard_map/ppermute | solution.py:537
  994.2 9.4 collective-permute-done.38
  (537 shorter events, 385.0 us)
Async XLA Ops:
  7.2 72.0 %all-gather.7.cloned.1.call-start = ((), (), s32[]{:S(2)}) async-start(), calls=%async_computation.5 | async-start | bytes 11943936 | tf_op jit(solution)/shard_map/all_gather | solution.py:586
  7.9 208.5 %all-gather.9.cloned.1.call-start = ((), (), s32[]{:S(2)}) async-start(), calls=%async_computation.6 | async-start | bytes 5971968 | tf_op jit(solution)/shard_map/all_gather | solution.py:599
  8.7 239.8 %all-gather.11.cloned.1.call-start = ((), (), s32[]{:S(2)}) async-start(), calls=%async_computation.12 | async-start | bytes 7962624 | tf_op jit(solution)/shard_map/all_gather | solution.py:600
  9.4 249.3 %all-gather.13.cloned.1.call-start = ((), (), s32[]{:S(2)}) async-start(), calls=%async_computation.13 | async-start | bytes 7962624 | tf_op jit(solution)/shard_map/all_gather | solution.py:601
  43.2 23.7 %collective-permute-start = (bf16[3,1152]{1,0:T(4,128)(2,1)}, bf16[3,1152]{1,0:T(4,128)(2,1)}, u32[]{:S(2)}, u32[]{:S(2)}) collective-permute-start(bf16[3,1152]{1,0:T(4,128)(2,1)} %multiply_convert_fusion.6), channel_id=1, source_target_pairs={{0,1},{1,2},{2,3},{4,5},{5,6},{6,7},{8,9},{9,10},{10,11},{12,13},{... | collective-permute-start | bytes 20744 | tf_op jit(solution)/shard_map/ppermute | solution.py:481
  47.3 559.3 %reduce-scatter.6.cloned.1.call-start = ((), (), s32[]{:S(2)}) async-start(), calls=%async_computation.7 | async-start | bytes 7962624 | tf_op jit(solution)/shard_map/reduce_scatter | solution.py:713
  129.7 43.2 %collective-permute-start.3 = (bf16[32,1152]{1,0:T(8,128)(2,1)}, bf16[32,1152]{1,0:T(8,128)(2,1)S(1)}, u32[]{:S(2)}, u32[]{:S(2)}) collective-permute-start(bf16[32,1152]{1,0:T(8,128)(2,1)} %end_states.3), channel_id=1, source_target_pairs={{0,3},{4,7},{8,11},{12,15},{16,19},{20,23},{24,27},{28,31}} | collective-permute-start | bytes 221192 | tf_op jit(solution)/shard_map/ppermute | solution.py:481
  135.1 34.4 %collective-permute-start.2 = (bf16[32,1152]{1,0:T(8,128)(2,1)}, bf16[32,1152]{1,0:T(8,128)(2,1)S(1)}, u32[]{:S(2)}, u32[]{:S(2)}) collective-permute-start(bf16[32,1152]{1,0:T(8,128)(2,1)} %end_states.3), channel_id=1, source_target_pairs={{0,2},{1,3},{4,6},{5,7},{8,10},{9,11},{12,14},{13,15},{16,18},{17,... | collective-permute-start | bytes 221192 | tf_op jit(solution)/shard_map/ppermute | solution.py:481
  136.4 34.6 %collective-permute-start.1 = (bf16[32,1152]{1,0:T(8,128)(2,1)}, bf16[32,1152]{1,0:T(8,128)(2,1)S(1)}, u32[]{:S(2)}, u32[]{:S(2)}) collective-permute-start(bf16[32,1152]{1,0:T(8,128)(2,1)} %end_states.3), channel_id=1, source_target_pairs={{0,1},{1,2},{2,3},{4,5},{5,6},{6,7},{8,9},{9,10},{10,11},{12,13},{... | collective-permute-start | bytes 221192 | tf_op jit(solution)/shard_map/ppermute | solution.py:481
  229.0 48.4 %collective-permute-start.11 = (bf16[384,1152]{1,0:T(8,128)(2,1)}, bf16[384,1152]{1,0:T(8,128)(2,1)}, u32[]{:S(2)}, u32[]{:S(2)}) collective-permute-start(bf16[384,1152]{1,0:T(8,128)(2,1)} %convolution_convert_fusion.10), channel_id=1, source_target_pairs={{0,3},{1,2},{2,1},{3,0},{4,7},{5,6},{6,5},{7,4},{8,11},{9,10},{10,... | collective-permute-start | bytes 2654216 | tf_op jit(solution)/shard_map/ppermute | solution.py:677
  235.2 92.6 %collective-permute-start.9 = (bf16[384,1152]{1,0:T(8,128)(2,1)}, bf16[384,1152]{1,0:T(8,128)(2,1)}, u32[]{:S(2)}, u32[]{:S(2)}) collective-permute-start(bf16[384,1152]{1,0:T(8,128)(2,1)} %convolution_convert_fusion.12), channel_id=1, source_target_pairs={{0,2},{1,3},{2,0},{3,1},{4,6},{5,7},{6,4},{7,5},{8,10},{9,11},{10,... | collective-permute-start | bytes 2654216 | tf_op jit(solution)/shard_map/ppermute | solution.py:677
  237.1 90.6 %collective-permute-start.7 = (bf16[384,1152]{1,0:T(8,128)(2,1)}, bf16[384,1152]{1,0:T(8,128)(2,1)}, u32[]{:S(2)}, u32[]{:S(2)}) collective-permute-start(bf16[384,1152]{1,0:T(8,128)(2,1)} %convolution_convert_fusion.14), channel_id=1, source_target_pairs={{0,1},{1,0},{2,3},{3,2},{4,5},{5,4},{6,7},{7,6},{8,9},{9,8},{10,11... | collective-permute-start | bytes 2654216 | tf_op jit(solution)/shard_map/ppermute | solution.py:677
  277.4 85.9 %collective-permute-start.17 = (bf16[384,1152]{1,0:T(8,128)(2,1)S(1)}, bf16[384,1152]{1,0:T(8,128)(2,1)S(1)}, u32[]{:S(2)}, u32[]{:S(2)}) collective-permute-start(bf16[384,1152]{1,0:T(8,128)(2,1)S(1)} %copy-done.92), channel_id=1, source_target_pairs={{0,3},{1,2},{2,1},{3,0},{4,7},{5,6},{6,5},{7,4},{8,11},{9,10},{10,... | collective-permute-start | bytes 2654216 | tf_op jit(solution)/shard_map/ppermute | solution.py:677
  327.7 75.7 %collective-permute-start.15 = (bf16[384,1152]{1,0:T(8,128)(2,1)S(1)}, bf16[384,1152]{1,0:T(8,128)(2,1)S(1)}, u32[]{:S(2)}, u32[]{:S(2)}) collective-permute-start(bf16[384,1152]{1,0:T(8,128)(2,1)S(1)} %copy-done.91), channel_id=1, source_target_pairs={{0,2},{1,3},{2,0},{3,1},{4,6},{5,7},{6,4},{7,5},{8,10},{9,11},{10,... | collective-permute-start | bytes 2654216 | tf_op jit(solution)/shard_map/ppermute | solution.py:677
  327.8 88.3 %collective-permute-start.13 = (bf16[384,1152]{1,0:T(8,128)(2,1)S(1)}, bf16[384,1152]{1,0:T(8,128)(2,1)S(1)}, u32[]{:S(2)}, u32[]{:S(2)}) collective-permute-start(bf16[384,1152]{1,0:T(8,128)(2,1)S(1)} %convolution_convert_fusion.15), channel_id=1, source_target_pairs={{0,1},{1,0},{2,3},{3,2},{4,5},{5,4},{6,7},{7,6},{8,9},{9,8},{10,11... | collective-permute-start | bytes 2654216 | tf_op jit(solution)/shard_map/ppermute | solution.py:677
  377.2 88.7 %collective-permute-start.18 = (bf16[384,1152]{1,0:T(8,128)(2,1)}, bf16[384,1152]{1,0:T(8,128)(2,1)S(1)}, u32[]{:S(2)}, u32[]{:S(2)}) collective-permute-start(bf16[384,1152]{1,0:T(8,128)(2,1)} %fusion.140), channel_id=1, source_target_pairs={{0,3},{1,2},{2,1},{3,0},{4,7},{5,6},{6,5},{7,4},{8,11},{9,10},{10,... | collective-permute-start | bytes 2654216 | tf_op jit(solution)/shard_map/ppermute | solution.py:677
  416.0 49.8 %collective-permute-start.16 = (bf16[384,1152]{1,0:T(8,128)(2,1)}, bf16[384,1152]{1,0:T(8,128)(2,1)S(1)}, u32[]{:S(2)}, u32[]{:S(2)}) collective-permute-start(bf16[384,1152]{1,0:T(8,128)(2,1)} %fusion.137), channel_id=1, source_target_pairs={{0,2},{1,3},{2,0},{3,1},{4,6},{5,7},{6,4},{7,5},{8,10},{9,11},{10,... | collective-permute-start | bytes 2654216 | tf_op jit(solution)/shard_map/ppermute | solution.py:677
  426.3 40.6 %collective-permute-start.14 = (bf16[384,1152]{1,0:T(8,128)(2,1)}, bf16[384,1152]{1,0:T(8,128)(2,1)}, u32[]{:S(2)}, u32[]{:S(2)}) collective-permute-start(bf16[384,1152]{1,0:T(8,128)(2,1)} %fusion.134), channel_id=1, source_target_pairs={{0,1},{1,0},{2,3},{3,2},{4,5},{5,4},{6,7},{7,6},{8,9},{9,8},{10,11... | collective-permute-start | bytes 2654216 | tf_op jit(solution)/shard_map/ppermute | solution.py:677
  478.7 179.6 %reduce-scatter.8.cloned.1.call-start = ((), (), s32[]{:S(2)}) async-start(), calls=%async_computation.8 | async-start | bytes 7962624 | tf_op jit(solution)/shard_map/reduce_scatter | solution.py:714
  478.7 24.8 %collective-permute-start.12 = (bf16[384,1152]{1,0:T(8,128)(2,1)}, bf16[384,1152]{1,0:T(8,128)(2,1)}, u32[]{:S(2)}, u32[]{:S(2)}) collective-permute-start(bf16[384,1152]{1,0:T(8,128)(2,1)} %fusion.152), channel_id=1, source_target_pairs={{0,3},{1,2},{2,1},{3,0},{4,7},{5,6},{6,5},{7,4},{8,11},{9,10},{10,... | collective-permute-start | bytes 2654216 | tf_op jit(solution)/shard_map/ppermute | solution.py:677
  480.3 73.8 %collective-permute-start.10 = (bf16[384,1152]{1,0:T(8,128)(2,1)S(1)}, bf16[384,1152]{1,0:T(8,128)(2,1)}, u32[]{:S(2)}, u32[]{:S(2)}) collective-permute-start(bf16[384,1152]{1,0:T(8,128)(2,1)S(1)} %copy-done.87), channel_id=1, source_target_pairs={{0,2},{1,3},{2,0},{3,1},{4,6},{5,7},{6,4},{7,5},{8,10},{9,11},{10,... | collective-permute-start | bytes 2654216 | tf_op jit(solution)/shard_map/ppermute | solution.py:677
  480.3 73.7 %collective-permute-start.8 = (bf16[384,1152]{1,0:T(8,128)(2,1)S(1)}, bf16[384,1152]{1,0:T(8,128)(2,1)}, u32[]{:S(2)}, u32[]{:S(2)}) collective-permute-start(bf16[384,1152]{1,0:T(8,128)(2,1)S(1)} %copy-done.86), channel_id=1, source_target_pairs={{0,1},{1,0},{2,3},{3,2},{4,5},{5,4},{6,7},{7,6},{8,9},{9,8},{10,11... | collective-permute-start | bytes 2654216 | tf_op jit(solution)/shard_map/ppermute | solution.py:677
  485.9 284.8 %reduce-scatter.10.cloned.1.call-start = ((), (), s32[]{:S(2)}) async-start(), calls=%async_computation.9 | async-start | bytes 5971968 | tf_op jit(solution)/shard_map/reduce_scatter | solution.py:756
  624.4 32.2 %collective-permute-start.21 = (bf16[24,1152]{1,0:T(8,128)(2,1)S(1)}, bf16[24,1152]{1,0:T(8,128)(2,1)}, u32[]{:S(2)}, u32[]{:S(2)}) collective-permute-start(bf16[24,1152]{1,0:T(8,128)(2,1)S(1)} %pad_maximum_fusion.5), channel_id=1, source_target_pairs={{3,0},{7,4},{11,8},{15,12},{19,16},{23,20},{27,24},{31,28}} | collective-permute-start | bytes 165896 | tf_op jit(solution)/shard_map/ppermute | solution.py:481
  625.9 23.2 %collective-permute-start.20 = (bf16[24,1152]{1,0:T(8,128)(2,1)S(1)}, bf16[24,1152]{1,0:T(8,128)(2,1)S(1)}, u32[]{:S(2)}, u32[]{:S(2)}) collective-permute-start(bf16[24,1152]{1,0:T(8,128)(2,1)S(1)} %pad_maximum_fusion.5), channel_id=1, source_target_pairs={{2,0},{3,1},{6,4},{7,5},{10,8},{11,9},{14,12},{15,13},{18,16},{19,... | collective-permute-start | bytes 165896 | tf_op jit(solution)/shard_map/ppermute | solution.py:481
  627.2 23.2 %collective-permute-start.19 = (bf16[24,1152]{1,0:T(8,128)(2,1)S(1)}, bf16[24,1152]{1,0:T(8,128)(2,1)S(1)}, u32[]{:S(2)}, u32[]{:S(2)}) collective-permute-start(bf16[24,1152]{1,0:T(8,128)(2,1)S(1)} %pad_maximum_fusion.5), channel_id=1, source_target_pairs={{1,0},{2,1},{3,2},{5,4},{6,5},{7,6},{9,8},{10,9},{11,10},{13,12},{... | collective-permute-start | bytes 165896 | tf_op jit(solution)/shard_map/ppermute | solution.py:481
  658.3 117.2 %reduce-scatter.12.cloned.1.call-start = ((), (), s32[]{:S(2)}) async-start(), calls=%async_computation.10 | async-start | bytes 5971968 | tf_op jit(solution)/shard_map/reduce_scatter | solution.py:757
  659.0 284.4 %reduce-scatter.14.cloned.1.call-start = ((), (), s32[]{:S(2)}) async-start(), calls=%async_computation.11 | async-start | bytes 7299072 | tf_op jit(solution)/shard_map/reduce_scatter | solution.py:798
  881.0 29.3 %collective-permute-start.27 = (bf16[144,1152]{1,0:T(8,128)(2,1)}, bf16[144,1152]{1,0:T(8,128)(2,1)}, u32[]{:S(2)}, u32[]{:S(2)}) collective-permute-start(bf16[144,1152]{1,0:T(8,128)(2,1)} %get-tuple-element.266), channel_id=1, source_target_pairs={{0,2},{1,3},{2,0},{3,1},{4,6},{5,7},{6,4},{7,5},{8,10},{9,11},{10,... | collective-permute-start | bytes 995336 | tf_op jit(solution)/shard_map/ppermute | solution.py:537
  882.3 28.0 %collective-permute-start.26 = (bf16[144,1152]{1,0:T(8,128)(2,1)S(1)}, bf16[144,1152]{1,0:T(8,128)(2,1)}, u32[]{:S(2)}, u32[]{:S(2)}) collective-permute-start(bf16[144,1152]{1,0:T(8,128)(2,1)S(1)} %get-tuple-element.265), channel_id=1, source_target_pairs={{0,1},{1,2},{2,3},{3,0},{4,5},{5,6},{6,7},{7,4},{8,9},{9,10},{10,1... | collective-permute-start | bytes 995336 | tf_op jit(solution)/shard_map/ppermute | solution.py:537
  916.4 26.6 %collective-permute-start.30 = (bf16[144,1152]{1,0:T(8,128)(2,1)S(1)}, bf16[144,1152]{1,0:T(8,128)(2,1)S(1)}, u32[]{:S(2)}, u32[]{:S(2)}) collective-permute-start(bf16[144,1152]{1,0:T(8,128)(2,1)S(1)} %fusion.182), channel_id=1, source_target_pairs={{0,2},{1,3},{2,0},{3,1},{4,6},{5,7},{6,4},{7,5},{8,10},{9,11},{10,... | collective-permute-start | bytes 995336 | tf_op jit(solution)/shard_map/ppermute | solution.py:537
  918.4 24.7 %collective-permute-start.31 = (bf16[144,1152]{1,0:T(8,128)(2,1)S(1)}, bf16[144,1152]{1,0:T(8,128)(2,1)S(1)}, u32[]{:S(2)}, u32[]{:S(2)}) collective-permute-start(bf16[144,1152]{1,0:T(8,128)(2,1)S(1)} %fusion.182), channel_id=1, source_target_pairs={{0,1},{1,2},{2,3},{3,0},{4,5},{5,6},{6,7},{7,4},{8,9},{9,10},{10,1... | collective-permute-start | bytes 995336 | tf_op jit(solution)/shard_map/ppermute | solution.py:537
  (120 other events, 2054.2 us)
Sparse Core Ops, SparseCore 0:
  9.9 69.2 all-gather.6
  81.1 41.6 all-gather.8
  124.7 49.1 all-gather.10
  175.7 49.7 all-gather.12
  478.8 64.0 reduce-scatter.5
  546.6 65.4 reduce-scatter.7
  658.4 56.2 reduce-scatter.9
  718.5 56.9 reduce-scatter.11
  878.1 61.8 reduce-scatter.13
